TPU v7x, 512 devices: a whole 4x4x16 slice. The times are simulated.
512 devices in a mesh: coil: 16 (over z_lo, core), slab: 32 (over x, z_hi, y).
Axes of the slice: x: 4, y: 4, z: 16 (z_hi: 2, z_lo: 8; z = z_hi * 8 + z_lo), core: 2. Of those that a mesh axis runs over, the one named last changes fastest.
Arguments:
- kspace_data: bfloat16 [32, 2, 128, 128, 128], P('coil', None, None, 'slab'), may hold values from -4 to 4
- coil_maps: bfloat16 [32, 2, 128, 128, 128], P('coil', None, 'slab'), may hold values from -1.796875 to 1.796875
- sample_mask: int32 [32, 128, 128], P('coil', None, 'slab'), may hold values 0 or 1
- initial_image: float32 [2, 128, 128, 128], P(None, 'slab', 'coil'), may hold values from -6 to 6
Outputs:
- image: float32 [2, 128, 128, 128], P(None, 'slab', 'coil')
All inputs are finite; a program needn't handle non-finite values. No bound on the sum of `sample_mask` on one device may be relied on, other than what follows from the above.
Results may differ from a plain program's by a relative error of at most 0.0045.
Values may be sent and summed in bfloat16 or wider, within the bound.
No kernel may reach another device: no remote copies, remote signals or barrier semaphores. Data moves between devices by JAX's collectives and lax.ppermute only.
A program may use at most 64 MiB of HBM per device.

v0:
```python
import math

import jax
import jax.numpy as jnp
from jax import lax
from jax.sharding import PartitionSpec as P

NX = 128
NY = 128
NZ = 128
ITERS = 2


dual_step = 0.25
primal_step = 0.25
tv_weight = 0.5


def from_behind(block, axis, distance):
    devices = range(lax.axis_size(axis))
    route = [(i - distance, i) for i in devices if i - distance in devices]
    return lax.ppermute(block, axis, route)


def in_blocks(shard, dim, size):
    before, after = (shard.shape[:dim], shard.shape[dim + 1 :])
    return jnp.moveaxis(shard.reshape(*before, size, -1, *after), dim, 0)


def sum_at_owner(shard, axis, dim):
    tiles = in_blocks(shard, dim, lax.axis_size(axis))
    arrived = lax.all_to_all(tiles, axis, split_axis=0, concat_axis=0, tiled=True)
    return arrived.sum(axis=0)


def dft_table(length, inverse):
    counter = jnp.arange(length, dtype=jnp.int32)
    product = counter[:, None] * counter[None, :] % length
    phase = 2.0 * math.pi / length * product.astype(jnp.float32)
    scale = 1.0 / math.sqrt(length)
    real_part = jnp.cos(phase) * scale
    imag_part = jnp.sin(phase) * scale
    if not inverse:
        imag_part = -imag_part
    table = jnp.stack([jnp.stack([real_part, imag_part]), jnp.stack([-imag_part, real_part])])
    return table.astype(jnp.bfloat16)


def data_term(guess, coil_maps, kspace_data, sample_mask, dual_data, tables):
    forward_x, forward_y, forward_z, inverse_x, inverse_y, inverse_z = tables
    maps_real = coil_maps[:, 0].astype(jnp.float32)
    maps_imag = coil_maps[:, 1].astype(jnp.float32)
    pieces = jnp.stack(
        [maps_real * guess[0] - maps_imag * guess[1], maps_real * guess[1] + maps_imag * guess[0]],
        1,
    ).astype(jnp.bfloat16)
    pieces = jnp.einsum(
        "ckzyx,kjxw->cjzyw", pieces, forward_x, preferred_element_type=jnp.float32
    ).astype(jnp.bfloat16)
    pieces = jnp.einsum(
        "ckzyx,kjyv->cjzvx", pieces, forward_y, preferred_element_type=jnp.float32
    ).astype(jnp.bfloat16)
    spectrum = jnp.einsum(
        "ckzyx,kjzw->cjwyx",
        lax.all_to_all(pieces, "slab", split_axis=3, concat_axis=2, tiled=True),
        forward_z,
        preferred_element_type=jnp.float32,
    )
    sampled = sample_mask[:, None, :, :, None].astype(jnp.float32)
    dual_new = (
        dual_data + dual_step * (sampled * (spectrum - kspace_data.astype(jnp.float32)))
    ) / (1.0 + dual_step)
    back_field = jnp.einsum(
        "ckzyx,kjzw->cjwyx",
        dual_new.astype(jnp.bfloat16),
        inverse_z,
        preferred_element_type=jnp.float32,
    ).astype(jnp.bfloat16)
    back_field = jnp.einsum(
        "ckzyx,kjyv->cjzvx",
        lax.all_to_all(back_field, "slab", split_axis=2, concat_axis=3, tiled=True),
        inverse_y,
        preferred_element_type=jnp.float32,
    ).astype(jnp.bfloat16)
    back_field = jnp.einsum(
        "ckzyx,kjxw->cjzyw", back_field, inverse_x, preferred_element_type=jnp.float32
    )
    real_sum = jnp.sum(maps_real * back_field[:, 0] + maps_imag * back_field[:, 1], 0)
    imag_sum = jnp.sum(maps_real * back_field[:, 1] - maps_imag * back_field[:, 0], 0)
    return (jnp.stack([real_sum, imag_sum]), dual_new)


def tv_update(guess, duals):
    planes = guess.shape[1]
    plane_pos = lax.axis_index("slab") * planes + lax.broadcasted_iota(
        jnp.int32, (1, planes, 1, 1), 1
    )
    next_plane = from_behind(guess[:, :1], "slab", -1)
    ahead_z = jnp.concatenate([guess[:, 1:], next_plane], 1)
    grad_z = jnp.where(plane_pos < NZ - 1, ahead_z - guess, 0.0)
    grad_y = jnp.concatenate(
        [guess[:, :, 1:] - guess[:, :, :-1], jnp.zeros_like(guess[:, :, :1])], 2
    )
    grad_x = jnp.concatenate([guess[..., 1:] - guess[..., :-1], jnp.zeros_like(guess[..., :1])], 3)
    moved_z = duals[0] + dual_step * grad_z
    moved_y = duals[1] + dual_step * grad_y
    moved_x = duals[2] + dual_step * grad_x
    magnitude = jnp.sqrt(
        jnp.sum(moved_z * moved_z, 0)
        + jnp.sum(moved_y * moved_y, 0)
        + jnp.sum(moved_x * moved_x, 0)
    )
    factor = 1.0 / jnp.maximum(1.0, magnitude / tv_weight)
    dual_z = moved_z * factor
    dual_y = moved_y * factor
    dual_x = moved_x * factor
    prior_plane = from_behind(dual_z[:, -1:], "slab", 1)
    spread_z = jnp.concatenate([prior_plane, dual_z[:, :-1]], 1) - dual_z
    spread_y = jnp.concatenate([jnp.zeros_like(dual_y[:, :, :1]), dual_y[:, :, :-1]], 2) - dual_y
    spread_x = jnp.concatenate([jnp.zeros_like(dual_x[..., :1]), dual_x[..., :-1]], 3) - dual_x
    return ((dual_z, dual_y, dual_x), spread_z + spread_y + spread_x)


def on_device(kspace_data, coil_maps, sample_mask, initial_image):
    tables = (
        dft_table(NX, False),
        dft_table(NY, False),
        dft_table(NZ, False),
        dft_table(NX, True),
        dft_table(NY, True),
        dft_table(NZ, True),
    )
    dual_data = jnp.zeros(kspace_data.shape, jnp.float32)
    share_rows = initial_image.shape[2]
    current = initial_image
    guess = current
    duals = None
    for turn_index in range(ITERS):
        whole_guess = lax.all_gather(guess, "coil", axis=2, tiled=True)
        if duals is None:
            duals = (
                jnp.zeros_like(whole_guess),
                jnp.zeros_like(whole_guess),
                jnp.zeros_like(whole_guess),
            )
        data_grad, dual_data = data_term(
            whole_guess, coil_maps, kspace_data, sample_mask, dual_data, tables
        )
        data_grad = sum_at_owner(data_grad, "coil", 2)
        duals, spread = tv_update(whole_guess, duals)
        spread_share = lax.dynamic_slice_in_dim(
            spread, lax.axis_index("coil") * share_rows, share_rows, 2
        )
        updated = current - primal_step * (data_grad + spread_share)
        guess = 2.0 * updated - current
        current = updated
    return current


def solution(mesh):
    placed = (
        P("coil", None, None, "slab", None),
        P("coil", None, "slab", None, None),
        P("coil", None, "slab"),
        P(None, "slab", "coil", None),
    )
    return jax.shard_map(
        on_device,
        mesh=mesh,
        in_specs=placed,
        out_specs=P(None, "slab", "coil", None),
        check_vma=False,
    )
```

profile of v0, /device:TPU:130, one launch (start us, length us, event | category | flops | bytes accessed | tf_op | source)
XLA Modules:
  0.0 341.5 jit_solution(4469572003324194506)
XLA Ops:
  0.0 0.3 negate_convert_fusion
  0.3 0.0 copy-start.6
  0.3 0.3 fusion.85
  0.6 0.5 copy-done.6
  1.0 20.8 %all_gather.6 = f32[2,4,128,128]{3,2,1,0:T(8,128)S(1)} all-gather(f32[2,4,8,128]{3,2,1,0:T(8,128)S(1)} %copy-done.6), channel_id=1, replica_groups=mesh['coil'=16,'slab'=32] {'coil'}, dimensions={2}, use_global_device_ids=true | all-gather | bytes 557056 | tf_op jit(solution)/shard_map/all_gather | solution.py:139
  21.8 1.0 copy-done.2
  22.8 0.2 fusion.24
  23.1 0.6 fusion.21
  23.6 1.2 copy.77
  24.8 13.6 %all-to-all-start = ((bf16[2,2,4,128,128]{4,2,0,1,3:T(4,128)(2,1)}), bf16[2,2,4,128,128]{4,2,0,1,3:T(4,128)(2,1)S(1)}, u32[]{:S(2)}, u32[]{:S(2)}) async-start(bf16[2,2,4,128,128]{4,2,0,1,3:T(4,128)(2,1)} %copy.77), calls=%async_computation | async-start | bytes 1048576 | tf_op jit(solution)/shard_map/all_to_all | solution.py:65
  38.5 19.4 %all-to-all-done = bf16[2,2,4,128,128]{4,2,0,1,3:T(4,128)(2,1)S(1)} async-done(((bf16[2,2,4,128,128]{4,2,0,1,3:T(4,128)(2,1)}), bf16[2,2,4,128,128]{4,2,0,1,3:T(4,128)(2,1)S(1)}, u32[]{:S(2)}, u32[]{:S(2)}) %all-to-all-start) | async-done | bytes 524320 | tf_op jit(solution)/shard_map/all_to_all | solution.py:65
  57.9 0.2 copy.78
  58.2 0.8 copy-done.4
  58.9 1.3 fusion.105
  60.3 0.3 fusion.20
  60.6 0.4 copy.82
  61.0 33.9 %all_to_all.82 = bf16[2,2,128,4,128]{4,3,0,1,2:T(4,128)(2,1)S(1)} all-to-all(bf16[2,2,128,4,128]{4,3,0,1,2:T(4,128)(2,1)S(1)} %copy.82), channel_id=1, replica_groups=mesh['coil'=16,'slab'=32] {'slab'}, dimensions={2} | all-to-all | bytes 1048576 | tf_op jit(solution)/shard_map/all_to_all | solution.py:81
  94.9 0.2 copy.83
  95.2 0.5 convolution_bitcast_fusion.2
  95.7 0.2 fusion.28
  95.9 0.9 copy.92
  96.8 26.0 %all-to-all-start.2 = ((f32[16,2,4,8,128]{4,3,2,1,0:T(8,128)}), f32[16,2,4,8,128]{4,3,2,1,0:T(8,128)}, u32[]{:S(2)}, u32[]{:S(2)}) async-start(f32[16,2,4,8,128]{4,3,2,1,0:T(8,128)} %copy.92), calls=%async_computation.2 | async-start | bytes 1048576 | tf_op jit(solution)/shard_map/all_to_all | solution.py:32
  122.8 9.0 %collective-permute-start = (f32[2,1,128,128]{3,2,1,0:T(8,128)S(1)}, f32[2,1,128,128]{3,2,1,0:T(8,128)S(1)}, u32[]{:S(2)}, u32[]{:S(2)}) collective-permute-start(f32[2,1,128,128]{3,2,1,0:T(8,128)S(1)} %slice.135), channel_id=1, source_target_pairs={{1,0},{2,1},{3,2},{4,3},{5,4},{6,5},{7,6},{8,7},{9,8},{10,9},{11,1... | collective-permute-start | bytes 393224 | tf_op jit(solution)/shard_map/ppermute | solution.py:22
  131.9 0.2 slice_subtract_fusion.2
  132.1 0.1 slice_subtract_fusion.3
  132.2 0.1 multiply_reduce_fusion.3
  132.3 23.6 %collective-permute-done = f32[2,1,128,128]{3,2,1,0:T(8,128)S(1)} collective-permute-done((f32[2,1,128,128]{3,2,1,0:T(8,128)S(1)}, f32[2,1,128,128]{3,2,1,0:T(8,128)S(1)}, u32[]{:S(2)}, u32[]{:S(2)}) %collective-permute-start) | collective-permute-done | bytes 131104 | tf_op jit(solution)/shard_map/ppermute | solution.py:22
  155.9 0.2 multiply_reduce_fusion.5
  156.1 0.1 divide_multiply_fusion
  156.2 0.3 broadcast_multiply_fusion.3
  156.5 1.9 collective-permute-start.1
  158.5 1.1 reduce_sum.110
  159.6 18.0 %collective-permute-done.1 = f32[2,1,128,128]{3,2,1,0:T(8,128)S(1)} collective-permute-done((f32[2,1,128,128]{3,2,1,0:T(8,128)S(1)}, f32[2,1,128,128]{3,2,1,0:T(8,128)S(1)}, u32[]{:S(2)}, u32[]{:S(2)}) %collective-permute-start.1) | collective-permute-done | bytes 131104 | tf_op jit(solution)/shard_map/ppermute | solution.py:22
  177.6 0.1 multiply_subtract_fusion.1
  177.6 15.8 %all_gather.7 = f32[2,4,128,128]{3,2,1,0:T(8,128)S(1)} all-gather(f32[2,4,8,128]{3,2,1,0:T(8,128)S(1)} %get-tuple-element.11), channel_id=1, replica_groups=mesh['coil'=16,'slab'=32] {'coil'}, dimensions={2}, use_global_device_ids=true | all-gather | bytes 557056 | tf_op jit(solution)/shard_map/all_gather | solution.py:139
  193.4 1.0 fusion.32
  194.4 2.4 fusion.18
  196.8 1.4 copy.94
  198.3 35.9 %all_to_all.83 = bf16[2,2,4,128,128]{4,2,0,1,3:T(4,128)(2,1)S(1)} all-to-all(bf16[2,2,4,128,128]{4,2,0,1,3:T(4,128)(2,1)S(1)} %copy.94), channel_id=1, replica_groups=mesh['coil'=16,'slab'=32] {'slab'}, dimensions={3} | all-to-all | bytes 1048576 | tf_op jit(solution)/shard_map/all_to_all | solution.py:65
  234.3 0.2 copy.95
  234.5 0.8 copy-done.5
  235.3 0.4 fusion.6
  235.7 0.3 fusion.17
  236.0 0.4 copy.99
  236.4 26.2 %all_to_all.84 = bf16[2,2,128,4,128]{4,3,0,1,2:T(4,128)(2,1)S(1)} all-to-all(bf16[2,2,128,4,128]{4,3,0,1,2:T(4,128)(2,1)S(1)} %copy.99), channel_id=1, replica_groups=mesh['coil'=16,'slab'=32] {'slab'}, dimensions={2} | all-to-all | bytes 1048576 | tf_op jit(solution)/shard_map/all_to_all | solution.py:81
  262.7 1.1 copy.100
  263.8 2.5 convolution_bitcast_fusion
  266.3 1.4 fusion.36
  267.8 0.9 copy.109
  268.7 18.8 %all-to-all-start.5 = ((f32[16,2,4,8,128]{4,3,2,1,0:T(8,128)}), f32[16,2,4,8,128]{4,3,2,1,0:T(8,128)}, u32[]{:S(2)}, u32[]{:S(2)}) async-start(f32[16,2,4,8,128]{4,3,2,1,0:T(8,128)} %copy.109), calls=%async_computation.5 | async-start | bytes 1048576 | tf_op jit(solution)/shard_map/all_to_all | solution.py:32
  287.5 10.7 %collective-permute-start.2 = (f32[2,1,128,128]{3,2,1,0:T(8,128)S(1)}, f32[2,1,128,128]{3,2,1,0:T(8,128)S(1)}, u32[]{:S(2)}, u32[]{:S(2)}) collective-permute-start(f32[2,1,128,128]{3,2,1,0:T(8,128)S(1)} %slice.149), channel_id=1, source_target_pairs={{1,0},{2,1},{3,2},{4,3},{5,4},{6,5},{7,6},{8,7},{9,8},{10,9},{11,1... | collective-permute-start | bytes 393224 | tf_op jit(solution)/shard_map/ppermute | solution.py:22
  298.1 0.2 slice_subtract_fusion
  298.3 0.1 multiply_reduce_fusion
  298.4 0.1 slice_subtract_fusion.1
  298.5 0.0 slice-start
  298.5 0.1 multiply_reduce_fusion.1
  298.6 21.9 %collective-permute-done.2 = f32[2,1,128,128]{3,2,1,0:T(8,128)S(1)} collective-permute-done((f32[2,1,128,128]{3,2,1,0:T(8,128)S(1)}, f32[2,1,128,128]{3,2,1,0:T(8,128)S(1)}, u32[]{:S(2)}, u32[]{:S(2)}) %collective-permute-start.2) | collective-permute-done | bytes 131104 | tf_op jit(solution)/shard_map/ppermute | solution.py:22
  320.5 0.2 multiply_reduce_fusion.2
  320.7 0.1 maximum_divide_fusion
  320.8 0.3 broadcast_multiply_fusion.2
  321.1 1.9 collective-permute-start.3
  323.1 1.1 reduce_sum.116
  324.2 16.7 %collective-permute-done.3 = f32[2,1,128,128]{3,2,1,0:T(8,128)S(1)} collective-permute-done((f32[2,1,128,128]{3,2,1,0:T(8,128)S(1)}, f32[2,1,128,128]{3,2,1,0:T(8,128)S(1)}, u32[]{:S(2)}, u32[]{:S(2)}) %collective-permute-start.3) | collective-permute-done | bytes 131104 | tf_op jit(solution)/shard_map/ppermute | solution.py:22
  340.8 0.7 multiply_subtract_fusion
  (28 shorter events, 0.3 us)
Async XLA Ops:
  0.3 0.8 copy-start.6
  21.8 1.0 copy-start.2
  24.8 13.6 %copy-start.7 = (s32[2,128,4]{1,2,0:T(4,128)S(1)}, s32[2,128,4]{1,2,0:T(4,128)}, u32[]{:S(2)}) copy-start(s32[2,128,4]{1,2,0:T(4,128)} %param.6) | copy-start | bytes 12292
  24.8 33.1 %all-to-all-start = ((bf16[2,2,4,128,128]{4,2,0,1,3:T(4,128)(2,1)}), bf16[2,2,4,128,128]{4,2,0,1,3:T(4,128)(2,1)S(1)}, u32[]{:S(2)}, u32[]{:S(2)}) async-start(bf16[2,2,4,128,128]{4,2,0,1,3:T(4,128)(2,1)} %copy.77), calls=%async_computation | async-start | bytes 1048576 | tf_op jit(solution)/shard_map/all_to_all | solution.py:65
  57.9 1.0 copy-start.4
  96.8 61.7 %all-to-all-start.2 = ((f32[16,2,4,8,128]{4,3,2,1,0:T(8,128)}), f32[16,2,4,8,128]{4,3,2,1,0:T(8,128)}, u32[]{:S(2)}, u32[]{:S(2)}) async-start(f32[16,2,4,8,128]{4,3,2,1,0:T(8,128)} %copy.92), calls=%async_computation.2 | async-start | bytes 1048576 | tf_op jit(solution)/shard_map/all_to_all | solution.py:32
  122.8 33.0 %collective-permute-start = (f32[2,1,128,128]{3,2,1,0:T(8,128)S(1)}, f32[2,1,128,128]{3,2,1,0:T(8,128)S(1)}, u32[]{:S(2)}, u32[]{:S(2)}) collective-permute-start(f32[2,1,128,128]{3,2,1,0:T(8,128)S(1)} %slice.135), channel_id=1, source_target_pairs={{1,0},{2,1},{3,2},{4,3},{5,4},{6,5},{7,6},{8,7},{9,8},{10,9},{11,1... | collective-permute-start | bytes 393224 | tf_op jit(solution)/shard_map/ppermute | solution.py:22
  156.5 21.0 %collective-permute-start.1 = (f32[2,1,128,128]{3,2,1,0:T(8,128)S(1)}, f32[2,1,128,128]{3,2,1,0:T(8,128)S(1)}, u32[]{:S(2)}, u32[]{:S(2)}) collective-permute-start(f32[2,1,128,128]{3,2,1,0:T(8,128)S(1)} %slice.140), channel_id=1, source_target_pairs={{0,1},{1,2},{2,3},{3,4},{4,5},{5,6},{6,7},{7,8},{8,9},{9,10},{10,1... | collective-permute-start | bytes 393224 | tf_op jit(solution)/shard_map/ppermute | solution.py:22
  193.4 105.0 %copy-start = (f32[2,4,128,128]{3,2,1,0:T(8,128)}, f32[2,4,128,128]{3,2,1,0:T(8,128)S(1)}, u32[]{:S(2)}) copy-start(f32[2,4,128,128]{3,2,1,0:T(8,128)S(1)} %all_gather.7) | copy-start | bytes 1572868
  198.3 36.2 %copy-start.3 = (f32[2,2,128,4,128]{4,2,3,0,1:T(8,128)S(1)}, f32[2,2,128,4,128]{4,2,3,0,1:T(8,128)}, u32[]{:S(2)}) copy-start(f32[2,2,128,4,128]{4,2,3,0,1:T(8,128)} %get-tuple-element.34) | copy-start | bytes 3145732
  234.3 1.0 copy-start.5
  268.7 54.4 %all-to-all-start.5 = ((f32[16,2,4,8,128]{4,3,2,1,0:T(8,128)}), f32[16,2,4,8,128]{4,3,2,1,0:T(8,128)}, u32[]{:S(2)}, u32[]{:S(2)}) async-start(f32[16,2,4,8,128]{4,3,2,1,0:T(8,128)} %copy.109), calls=%async_computation.5 | async-start | bytes 1048576 | tf_op jit(solution)/shard_map/all_to_all | solution.py:32
  287.5 33.0 %collective-permute-start.2 = (f32[2,1,128,128]{3,2,1,0:T(8,128)S(1)}, f32[2,1,128,128]{3,2,1,0:T(8,128)S(1)}, u32[]{:S(2)}, u32[]{:S(2)}) collective-permute-start(f32[2,1,128,128]{3,2,1,0:T(8,128)S(1)} %slice.149), channel_id=1, source_target_pairs={{1,0},{2,1},{3,2},{4,3},{5,4},{6,5},{7,6},{8,7},{9,8},{10,9},{11,1... | collective-permute-start | bytes 393224 | tf_op jit(solution)/shard_map/ppermute | solution.py:22
  298.5 22.0 %copy-start.1 = (f32[2,4,128,128]{3,2,1,0:T(8,128)S(1)}, f32[2,4,128,128]{3,2,1,0:T(8,128)}, u32[]{:S(2)}) copy-start(f32[2,4,128,128]{3,2,1,0:T(8,128)} %copy-done) | copy-start | bytes 1572868
  298.5 22.0 %slice-start = ((f32[2,4,128,128]{3,2,1,0:T(8,128)}), f32[2,3,128,128]{3,2,1,0:T(8,128)S(1)}, s32[]{:S(2)}) async-start(f32[2,4,128,128]{3,2,1,0:T(8,128)} %copy-done), calls=%async_computation.6 | async-start | bytes 786432 | tf_op jit(solution)/shard_map/slice | solution.py:99
  321.1 19.7 %collective-permute-start.3 = (f32[2,1,128,128]{3,2,1,0:T(8,128)S(1)}, f32[2,1,128,128]{3,2,1,0:T(8,128)S(1)}, u32[]{:S(2)}, u32[]{:S(2)}) collective-permute-start(f32[2,1,128,128]{3,2,1,0:T(8,128)S(1)} %slice.154), channel_id=1, source_target_pairs={{0,1},{1,2},{2,3},{3,4},{4,5},{5,6},{6,7},{7,8},{8,9},{9,10},{10,1... | collective-permute-start | bytes 393224 | tf_op jit(solution)/shard_map/ppermute | solution.py:22
where the time goes:
time: 343 us; the launch traced here: 342 us
  blocking collectives  133 us (39%)
  waiting for transfers between devices  99.5 us (29%)
  starting transfers between devices  81.9 us (24%)
  local copies, waits for them, and re-layouts  10.3 us (3%)
  other arithmetic  8.42 us (2%)
  matrix products  8.42 us (2%)
    ppermute x4, waiting for transfers between devices, from_behind(): return lax.ppermute(block, axis, route)  80.1 us
    all_to_all x2, blocking collectives, data_term(): lax.all_to_all(back_field, 'slab', split_axis=2, concat_axis=3, tiled=True)  60.1 us
    all_to_all x2, starting transfers between devices, sum_at_owner(): lax.all_to_all(tiles, axis, split_axis=0, concat_axis=0, tiled=True)  44.8 us
    all_gather x2, blocking collectives, on_device(): whole_guess = lax.all_gather(guess, 'coil', axis=2, tiled=True)  36.5 us
    all_to_all x1, blocking collectives, data_term(): lax.all_to_all(pieces, 'slab', split_axis=3, concat_axis=2, tiled=True)  35.9 us
    ppermute x4, starting transfers between devices, from_behind(): return lax.ppermute(block, axis, route)  23.5 us
    all_to_all x1, waiting for transfers between devices, data_term(): lax.all_to_all(pieces, 'slab', split_axis=3, concat_axis=2, tiled=True)  19.4 us
    all_to_all x1, starting transfers between devices, data_term(): lax.all_to_all(pieces, 'slab', split_axis=3, concat_axis=2, tiled=True)  13.6 us
  transfers between devices with their start and end apart: 7, of which 5 were waited for; matrix products, arithmetic and copies ran while one was open for 1% of the time, Pallas kernels for 0%

commit v1 on v0

v1 whole, which is shorter than its diff:
```python
import math

import jax
import jax.numpy as jnp
from jax import lax
from jax.sharding import Mesh
from jax.sharding import PartitionSpec as P

ITERS = 2
dual_step = 0.25
primal_step = 0.25
tv_weight = 0.5

COLUMN = ("zq", "x", "zhi", "y")
GROUP = ("zp", "core")
bf16 = jnp.bfloat16
f32 = jnp.float32


def dft_table(length, inverse):
    counter = jnp.arange(length, dtype=jnp.int32)
    product = counter[:, None] * counter[None, :] % length
    phase = 2.0 * math.pi / length * product.astype(jnp.float32)
    scale = 1.0 / math.sqrt(length)
    real_part = jnp.cos(phase) * scale
    imag_part = jnp.sin(phase) * scale
    if not inverse:
        imag_part = -imag_part
    table = jnp.stack([jnp.stack([real_part, imag_part]), jnp.stack([-imag_part, real_part])])
    return table.astype(bf16)


def matmul(spec, a, b):
    return jnp.einsum(spec, a, b, preferred_element_type=f32)


def data_term(guess, maps, data, mask, dual, fwd, inv):
    pieces = jnp.stack(
        [maps[:, 0] * guess[0] - maps[:, 1] * guess[1], maps[:, 0] * guess[1] + maps[:, 1] * guess[0]],
        1,
    ).astype(bf16)
    pieces = matmul("ckzy,kjzw->cjwy", pieces, fwd).astype(bf16)
    spectrum = matmul("ckwy,kjyv->cjvw", pieces, fwd)
    dual = (dual + dual_step * (mask * (spectrum - data))) / (1.0 + dual_step)
    back = matmul("ckvw,kjwz->cjzv", dual.astype(bf16), inv).astype(bf16)
    back = matmul("ckzv,kjvy->cjzy", back, inv)
    real_sum = jnp.sum(maps[:, 0] * back[:, 0] + maps[:, 1] * back[:, 1], 0)
    imag_sum = jnp.sum(maps[:, 0] * back[:, 1] - maps[:, 1] * back[:, 0], 0)
    return jnp.stack([real_sum, imag_sum]), dual


def diff_up(a, axis):
    n = a.shape[axis]
    up = lax.slice_in_dim(a, 1, n, axis=axis) - lax.slice_in_dim(a, 0, n - 1, axis=axis)
    return jnp.concatenate([up, jnp.zeros_like(lax.slice_in_dim(a, 0, 1, axis=axis))], axis)


def diff_back(a, axis):
    n = a.shape[axis]
    low = lax.slice_in_dim(a, 0, n - 1, axis=axis)
    return jnp.concatenate([jnp.zeros_like(lax.slice_in_dim(a, 0, 1, axis=axis)), low], axis) - a


def shrink(here, ahead, duals):
    moved = (
        duals[0] + dual_step * diff_up(here, 1),
        duals[1] + dual_step * diff_up(here, 2),
        duals[2] + dual_step * (ahead - here),
    )
    size = jnp.sqrt(sum(jnp.sum(m * m, 0) for m in moved))
    factor = 1.0 / jnp.maximum(1.0, size / tv_weight)
    return tuple(m * factor for m in moved)


def on_device(kspace_data, coil_maps, sample_mask, initial_image):
    coils, _, planes, ny, nx = coil_maps.shape
    nz, lines = kspace_data.shape[2:4]
    rows = initial_image.shape[2]
    zq, x, zhi, y = (lax.axis_size(a) for a in COLUMN)
    group = lax.axis_size(GROUP)
    count = zhi * zq * x * y
    fwd, inv = dft_table(nz, False), dft_table(nz, True)
    inv_x = dft_table(nx, True)
    me = lax.axis_index(COLUMN)

    def spread(blocks):
        return lax.all_to_all(blocks, COLUMN, 0, 0, tiled=True)

    high = initial_image.astype(bf16)
    low = (initial_image - high.astype(f32)).astype(bf16)
    image_row = jnp.stack([high, low]).transpose(4, 0, 1, 2, 3).reshape(nx, 1, 1, ny)
    image_row = jnp.pad(image_row, ((0, 0), (0, 0), (0, planes - 1), (0, 0)))
    map_rows = coil_maps.transpose(4, 0, 1, 2, 3).reshape(nx, coils * 2, planes, ny)
    first = spread(jnp.concatenate([map_rows, image_row], 1))

    turned = matmul("ckzyw,kjwx->xcjyz", kspace_data, inv_x).astype(bf16)
    turned = turned.reshape(nx, coils * 2, lines, nz)
    mask_rows = jnp.broadcast_to(sample_mask.transpose(0, 2, 1).astype(bf16), (nx, coils, lines, nz))
    second = spread(jnp.concatenate([turned, mask_rows], 1))

    def to_planes(blocks, per):
        blocks = blocks.reshape(zq, -1, coils, per, blocks.shape[-2], blocks.shape[-1])
        return blocks.transpose(0, 2, 3, 1, 4, 5).reshape(zq * coils, per, -1, blocks.shape[-1])

    maps = to_planes(first[:, : 2 * coils], 2).astype(f32)
    data = to_planes(second[:, : 2 * coils], 2).astype(f32)
    mask = to_planes(second[:, 2 * coils :], 1).astype(f32)

    part = first[:, 2 * coils, 0].astype(f32).reshape(zq, -1, 2, 2, planes, rows).sum(2)
    part = part.transpose(2, 1, 3, 0, 4).reshape(2, nz, zq, rows)
    current = lax.all_gather(part, GROUP, axis=3, tiled=False).reshape(2, nz, ny)

    def neighbours(a):
        before = lax.ppermute(a, COLUMN, [(i, i + 1) for i in range(count - 1)])
        after = lax.ppermute(a, COLUMN, [(i + 1, i) for i in range(count - 1)])
        return before, jnp.where(me < count - 1, after, a)

    guess = current
    dual = jnp.zeros_like(data)
    zero = jnp.zeros_like(current)
    duals, duals_before = (zero,) * 3, (zero,) * 3
    for turn in range(ITERS):
        before, after = neighbours(guess)
        grad, dual = data_term(guess, maps, data, mask, dual, fwd, inv)
        duals = shrink(guess, after, duals)
        duals_before = shrink(before, guess, duals_before)
        spread_sum = (
            diff_back(duals[0], 1)
            + diff_back(duals[1], 2)
            + jnp.where(me > 0, duals_before[2], 0.0)
            - duals[2]
        )
        if turn < ITERS - 1:
            grad = lax.all_gather(grad.astype(bf16), GROUP, axis=0).astype(f32).sum(0)
            updated = current - primal_step * (grad + spread_sum)
            guess = 2.0 * updated - current
            current = updated
    grad = grad.reshape(2, nz, zq, group, rows).transpose(3, 0, 1, 2, 4).astype(bf16)
    grad = lax.all_to_all(grad, GROUP, 0, 0, tiled=True).astype(f32).sum(0)
    rest = (current - primal_step * spread_sum).reshape(2, nz, zq, group, rows)
    rest = lax.dynamic_index_in_dim(rest, lax.axis_index(GROUP), 3, keepdims=False)
    result = rest - primal_step * grad
    result = result.reshape(2, -1, planes, zq, rows).transpose(3, 1, 0, 2, 4)
    result = spread(result.reshape(count, 2 * planes * rows))
    return result.T.reshape(2, planes, rows, nx)


def solution(mesh):
    devices = mesh.devices.reshape(4, 2, 2, 4, 2, 4)
    split = Mesh(devices, ("zq", "zp", "core", "x", "zhi", "y"))
    coil, slab = ("zq", "zp", "core"), ("x", "zhi", "y")
    return jax.shard_map(
        on_device,
        mesh=split,
        in_specs=(
            P(coil, None, None, slab, None),
            P(coil, None, slab, None, None),
            P(coil, None, slab),
            P(None, slab, coil, None),
        ),
        out_specs=P(None, slab, coil, None),
        check_vma=False,
    )
```

time: 343 us -> 227 us (0.66)
  the two profiles are of different devices: /device:TPU:130 before, /device:TPU:1 now
where the time goes in v1:
time: 227 us; the launch traced here: 223 us
  blocking collectives  107 us (47%)
  starting transfers between devices  47.7 us (21%)
  waiting for transfers between devices  34 us (15%)
  other arithmetic  14.7 us (6%)
  local copies, waits for them, and re-layouts  11.9 us (5%)
  matrix products  7.09 us (3%)
    all_to_all x1, blocking collectives, spread(): return lax.all_to_all(blocks, COLUMN, 0, 0, tiled=True)  62.9 us
    all_to_all x2, starting transfers between devices, spread(): return lax.all_to_all(blocks, COLUMN, 0, 0, tiled=True)  35.5 us
    all_gather x1, blocking collectives, on_device(): lax.all_gather(part, GROUP, axis=3, tiled=False).reshape(2, nz, ny)  34.7 us
    all_to_all x2, waiting for transfers between devices, spread(): return lax.all_to_all(blocks, COLUMN, 0, 0, tiled=True)  31.6 us
    all_gather x1, blocking collectives, on_device(): grad = lax.all_gather(grad.astype(bf16), GROUP, axis=0).astype(f32).sum(0)  9.33 us
    dot_general x6, matrix products, matmul(): return jnp.einsum(spec, a, b, preferred_element_type=f32)  7.09 us
    all_to_all x1, starting transfers between devices, on_device(): grad = lax.all_to_all(grad, GROUP, 0, 0, tiled=True).astype(f32).sum(0)  5.15 us
  transfers between devices with their start and end apart: 7, of which 2 were waited for; matrix products, arithmetic and copies ran while one was open for 8% of the time, Pallas kernels for 0%

profile of v1, /device:TPU:1, one launch (start us, length us, event | category | flops | bytes accessed | tf_op | source)
XLA Modules:
  0.0 223.2 jit_solution(16283611078892797923)
XLA Ops:
  0.0 0.8 convert_bitcast_fusion.6
  0.8 0.1 copy.261
  1.0 1.5 copy.175
  2.5 1.2 fusion.21
  3.6 23.1 %all-to-all-start = ((bf16[128,5,4,128]{3,2,1,0:T(4,128)(2,1)}), bf16[128,5,4,128]{3,2,1,0:T(4,128)(2,1)S(1)}, u32[]{:S(2)}, u32[]{:S(2)}) async-start(bf16[128,5,4,128]{3,2,1,0:T(4,128)(2,1)} %fusion.21), calls=%async_computation | async-start | bytes 1310720 | tf_op jit(solution)/shard_map/all_to_all | solution.py:87
  26.7 0.3 fusion.60
  27.0 0.3 negate_convert_fusion
  27.3 0.3 fusion.20
  27.7 0.3 copy-done.28
  28.2 1.5 copy.187
  29.7 31.6 %all-to-all-done = bf16[128,5,4,128]{3,2,1,0:T(4,128)(2,1)S(1)} async-done(((bf16[128,5,4,128]{3,2,1,0:T(4,128)(2,1)}), bf16[128,5,4,128]{3,2,1,0:T(4,128)(2,1)S(1)}, u32[]{:S(2)}, u32[]{:S(2)}) %all-to-all-start) | async-done | bytes 655392 | tf_op jit(solution)/shard_map/all_to_all | solution.py:87
  61.3 12.4 %all-to-all-start.1 = ((bf16[128,6,4,128]{3,2,1,0:T(4,128)(2,1)}), bf16[128,6,4,128]{3,2,1,0:T(4,128)(2,1)S(1)}, u32[]{:S(2)}, u32[]{:S(2)}) async-start(bf16[128,6,4,128]{3,2,1,0:T(4,128)(2,1)} %copy.187), calls=%async_computation.1 | async-start | bytes 1572864 | tf_op jit(solution)/shard_map/all_to_all | solution.py:87
  73.8 0.7 fusion.70
  74.7 0.2 reshape.257
  74.9 0.3 copy.179
  75.2 0.2 copy.180
  75.4 34.7 %all_gather.7 = f32[2,128,4,4,8]{1,4,2,0,3:T(8,128)S(1)} all-gather(f32[2,128,4,1,8]{1,4,2,0,3:T(8,128)S(1)} %copy.180), channel_id=1, replica_groups=mesh['zq'=4,'zp'=2,'core'=2,'x'=4,'zhi'=2,'y'=4] {'zp','core'}, dimensions={3}, use_global_device_ids=true | all-gather | bytes 163840 | tf_op jit(solution)/shard_map/all_gather | solution.py:111
  110.2 2.3 %collective-permute-start.1 = (f32[2,128,128]{2,1,0:T(8,128)S(1)}, f32[2,128,128]{2,1,0:T(8,128)S(1)}, u32[]{:S(2)}, u32[]{:S(2)}) collective-permute-start(f32[2,128,128]{2,1,0:T(8,128)S(1)} %copy.209), channel_id=1, source_target_pairs={{0,1},{1,2},{2,3},{3,4},{4,5},{5,6},{6,7},{7,8},{8,9},{9,10},{10,1... | collective-permute-start | bytes 393224 | tf_op jit(solution)/shard_map/ppermute | solution.py:114
  112.5 1.5 collective-permute-start
  114.0 0.2 slice.161
  114.2 0.1 copy.257
  114.3 0.1 convert_bitcast_fusion.1
  114.5 0.7 copy.183
  115.6 1.0 subtract_convert_fusion.1
  116.7 2.4 %collective-permute-done = f32[2,128,128]{2,1,0:T(8,128)S(1)} collective-permute-done((f32[2,128,128]{2,1,0:T(8,128)S(1)}, f32[2,128,128]{2,1,0:T(8,128)S(1)}, u32[]{:S(2)}, u32[]{:S(2)}) %collective-permute-start) | collective-permute-done | bytes 131104 | tf_op jit(solution)/shard_map/ppermute | solution.py:115
  119.1 0.7 multiply_reduce_fusion.6
  119.8 0.7 divide_multiply_fusion
  120.5 0.7 pad_multiply_fusion.1
  121.2 0.2 slice.167
  121.4 0.1 copy.260
  121.5 0.1 convert_bitcast_fusion
  121.7 0.7 copy.197
  122.6 1.2 copy.189
  123.7 1.9 fusion.3
  125.7 1.5 convolution_bitcast_fusion.4
  127.2 1.4 add_reduce_fusion.1
  128.7 9.3 %all_gather.8 = bf16[4,2,128,128]{3,2,1,0:T(8,128)(2,1)S(1)} all-gather(bf16[1,2,128,128]{3,2,1,0:T(8,128)(2,1)S(1)} %pad_maximum_fusion.7), channel_id=1, replica_groups=mesh['zq'=4,'zp'=2,'core'=2,'x'=4,'zhi'=2,'y'=4] {'zp','core'}, dimensions={0}, use_global_device_ids=true | all-gather | bytes 327680 | tf_op jit(solution)/shard_map/all_gather | solution.py:134
  138.1 0.8 multiply_subtract_fusion.1
  138.9 1.9 collective-permute-start.3
  140.8 1.3 collective-permute-start.2
  142.1 0.8 slice_subtract_fusion.2
  142.9 0.6 multiply_reduce_fusion.5
  143.6 0.1 subtract_convert_fusion
  143.7 0.1 copy-done.19
  143.8 0.3 fusion.17
  144.1 0.6 copy-done
  144.8 1.3 fusion.15
  146.0 1.7 convolution_bitcast_fusion
  147.8 0.2 add_reduce_fusion
  148.1 0.1 copy.218
  148.3 0.6 copy.220
  148.9 5.2 %all-to-all-start.2 = ((bf16[4,2,128,4,8]{2,4,3,1,0:T(8,128)(2,1)}), bf16[4,2,128,4,8]{2,4,3,1,0:T(8,128)(2,1)S(1)}, u32[]{:S(2)}, u32[]{:S(2)}) async-start(bf16[4,2,128,4,8]{2,4,3,1,0:T(8,128)(2,1)} %copy.220), calls=%async_computation.2 | async-start | bytes 131072 | tf_op jit(solution)/shard_map/all_to_all | solution.py:139
  154.1 1.1 slice_subtract_fusion
  155.2 1.0 slice_subtract_fusion.1
  156.3 1.1 multiply_reduce_fusion.1
  157.6 0.7 copy-done.25
  158.3 0.1 multiply_subtract_fusion
  158.6 0.2 copy.212
  158.8 0.2 copy.222
  159.0 0.1 subtract_bitcast_fusion
  159.2 0.2 copy.223
  159.4 0.1 all_to_all.20
  159.6 62.9 %all_to_all.27 = f32[128,1,64]{2,1,0:T(1,128)S(1)} all-to-all(f32[128,1,64]{2,1,0:T(1,128)S(1)} %copy.224), channel_id=1, replica_groups=mesh['zq'=4,'zp'=2,'core'=2,'x'=4,'zhi'=2,'y'=4] {'zq','x','zhi','y'}, dimensions={0} | all-to-all | bytes 65536 | tf_op jit(solution)/shard_map/all_to_all | solution.py:87
  222.5 0.7 copy.225
  (99 shorter events, 1.9 us)
Async XLA Ops:
  3.6 23.7 %copy-start.26 = (bf16[2,2,128,4,128]{4,3,2,1,0:T(4,128)(2,1)S(1)}, bf16[2,2,128,4,128]{4,3,2,1,0:T(4,128)(2,1)}, u32[]{:S(2)}) copy-start(bf16[2,2,128,4,128]{4,3,2,1,0:T(4,128)(2,1)} %param.4) | copy-start | bytes 1572868
  3.6 57.7 %all-to-all-start = ((bf16[128,5,4,128]{3,2,1,0:T(4,128)(2,1)}), bf16[128,5,4,128]{3,2,1,0:T(4,128)(2,1)S(1)}, u32[]{:S(2)}, u32[]{:S(2)}) async-start(bf16[128,5,4,128]{3,2,1,0:T(4,128)(2,1)} %fusion.21), calls=%async_computation | async-start | bytes 1310720 | tf_op jit(solution)/shard_map/all_to_all | solution.py:87
  27.3 0.8 copy-start.3
  27.3 0.8 copy-start.5
  27.3 0.7 copy-start.28
  61.3 59.9 %all-to-all-start.1 = ((bf16[128,6,4,128]{3,2,1,0:T(4,128)(2,1)}), bf16[128,6,4,128]{3,2,1,0:T(4,128)(2,1)S(1)}, u32[]{:S(2)}, u32[]{:S(2)}) async-start(bf16[128,6,4,128]{3,2,1,0:T(4,128)(2,1)} %copy.187), calls=%async_computation.1 | async-start | bytes 1572864 | tf_op jit(solution)/shard_map/all_to_all | solution.py:87
  110.2 6.3 %collective-permute-start.1 = (f32[2,128,128]{2,1,0:T(8,128)S(1)}, f32[2,128,128]{2,1,0:T(8,128)S(1)}, u32[]{:S(2)}, u32[]{:S(2)}) collective-permute-start(f32[2,128,128]{2,1,0:T(8,128)S(1)} %copy.209), channel_id=1, source_target_pairs={{0,1},{1,2},{2,3},{3,4},{4,5},{5,6},{6,7},{7,8},{8,9},{9,10},{10,1... | collective-permute-start | bytes 393224 | tf_op jit(solution)/shard_map/ppermute | solution.py:114
  112.5 6.6 %collective-permute-start = (f32[2,128,128]{2,1,0:T(8,128)S(1)}, f32[2,128,128]{2,1,0:T(8,128)S(1)}, u32[]{:S(2)}, u32[]{:S(2)}) collective-permute-start(f32[2,128,128]{2,1,0:T(8,128)S(1)} %copy.209), channel_id=1, source_target_pairs={{1,0},{2,1},{3,2},{4,3},{5,4},{6,5},{7,6},{8,7},{9,8},{10,9},{11,1... | collective-permute-start | bytes 393224 | tf_op jit(solution)/shard_map/ppermute | solution.py:115
  116.6 4.5 %copy-start.7 = (f32[2,128,127]{2,1,0:T(8,128)}, f32[2,128,127]{2,1,0:T(8,128)S(1)}, u32[]{:S(2)}) copy-start(f32[2,128,127]{2,1,0:T(8,128)S(1)} %slice_subtract_fusion.4) | copy-start | bytes 390148
  116.7 4.5 %copy-start.9 = (f32[2,127,128]{2,1,0:T(8,128)}, f32[2,127,128]{2,1,0:T(8,128)S(1)}, u32[]{:S(2)}) copy-start(f32[2,127,128]{2,1,0:T(8,128)S(1)} %slice_subtract_fusion.5) | copy-start | bytes 390148
  119.1 2.1 copy-start.11
  119.8 1.4 copy-start.20
  123.7 1.9 copy-start.4
  123.7 1.9 copy-start.6
  127.2 10.8 %copy-start.1 = (f32[2,128,128]{2,1,0:T(8,128)S(1)}, f32[2,128,128]{2,1,0:T(8,128)}, u32[]{:S(2)}) copy-start(f32[2,128,128]{2,1,0:T(8,128)} %get-tuple-element.39) | copy-start | bytes 393220
  127.2 10.8 %copy-start.12 = (f32[2,128,128]{2,1,0:T(8,128)S(1)}, f32[2,128,128]{2,1,0:T(8,128)}, u32[]{:S(2)}) copy-start(f32[2,128,128]{2,1,0:T(8,128)} %copy-done.11) | copy-start | bytes 393220
  127.2 10.8 %copy-start.14 = (f32[2,128,128]{2,1,0:T(8,128)S(1)}, f32[2,128,128]{2,1,0:T(8,128)}, u32[]{:S(2)}) copy-start(f32[2,128,128]{2,1,0:T(8,128)} %get-tuple-element.18) | copy-start | bytes 393220
  127.2 10.9 %copy-start.21 = (f32[128,128]{1,0:T(8,128)S(1)}, f32[128,128]{1,0:T(8,128)}, u32[]{:S(2)}) copy-start(f32[128,128]{1,0:T(8,128)} %copy-done.20) | copy-start | bytes 196612
  127.2 10.9 %copy-start.23 = (f32[128,128]{1,0:T(8,128)S(1)}, f32[128,128]{1,0:T(8,128)}, u32[]{:S(2)}) copy-start(f32[128,128]{1,0:T(8,128)} %divide_multiply_fusion) | copy-start | bytes 196612
  138.9 15.2 %collective-permute-start.3 = (f32[2,128,128]{2,1,0:T(8,128)S(1)}, f32[2,128,128]{2,1,0:T(8,128)}, u32[]{:S(2)}, u32[]{:S(2)}) collective-permute-start(f32[2,128,128]{2,1,0:T(8,128)S(1)} %get-tuple-element.15), channel_id=1, source_target_pairs={{0,1},{1,2},{2,3},{3,4},{4,5},{5,6},{6,7},{7,8},{8,9},{9,10},{10,1... | collective-permute-start | bytes 393224 | tf_op jit(solution)/shard_map/ppermute | solution.py:114
  140.8 15.4 %collective-permute-start.2 = (f32[2,128,128]{2,1,0:T(8,128)S(1)}, f32[2,128,128]{2,1,0:T(8,128)}, u32[]{:S(2)}, u32[]{:S(2)}) collective-permute-start(f32[2,128,128]{2,1,0:T(8,128)S(1)} %get-tuple-element.15), channel_id=1, source_target_pairs={{1,0},{2,1},{3,2},{4,3},{5,4},{6,5},{7,6},{8,7},{9,8},{10,9},{11,1... | collective-permute-start | bytes 393224 | tf_op jit(solution)/shard_map/ppermute | solution.py:115
  142.1 0.8 copy-start.16
  142.9 0.9 copy-start.19
  143.7 1.1 copy-start
  147.8 6.3 %copy-start.2 = (f32[2,128,128]{2,1,0:T(8,128)S(1)}, f32[2,128,128]{2,1,0:T(8,128)}, u32[]{:S(2)}) copy-start(f32[2,128,128]{2,1,0:T(8,128)} %get-tuple-element.39) | copy-start | bytes 393220
  147.8 6.3 %copy-start.18 = (f32[2,128,127]{2,1,0:T(8,128)S(1)}, f32[2,128,127]{2,1,0:T(8,128)}, u32[]{:S(2)}) copy-start(f32[2,128,127]{2,1,0:T(8,128)} %slice_subtract_fusion.2) | copy-start | bytes 390148
  148.0 8.3 %copy-start.8 = (f32[2,128,127]{2,1,0:T(8,128)S(1)}, f32[2,128,127]{2,1,0:T(8,128)}, u32[]{:S(2)}) copy-start(f32[2,128,127]{2,1,0:T(8,128)} %copy-done.7) | copy-start | bytes 390148
  148.0 8.3 %copy-start.10 = (f32[2,127,128]{2,1,0:T(8,128)S(1)}, f32[2,127,128]{2,1,0:T(8,128)}, u32[]{:S(2)}) copy-start(f32[2,127,128]{2,1,0:T(8,128)} %copy-done.9) | copy-start | bytes 390148
  148.0 8.3 %copy-start.13 = (f32[2,128,128]{2,1,0:T(8,128)S(1)}, f32[2,128,128]{2,1,0:T(8,128)}, u32[]{:S(2)}) copy-start(f32[2,128,128]{2,1,0:T(8,128)} %copy-done.11) | copy-start | bytes 393220
  148.0 8.3 %copy-start.15 = (f32[2,128,128]{2,1,0:T(8,128)S(1)}, f32[2,128,128]{2,1,0:T(8,128)}, u32[]{:S(2)}) copy-start(f32[2,128,128]{2,1,0:T(8,128)} %get-tuple-element.18) | copy-start | bytes 393220
  148.0 8.3 %copy-start.22 = (f32[128,128]{1,0:T(8,128)S(1)}, f32[128,128]{1,0:T(8,128)}, u32[]{:S(2)}) copy-start(f32[128,128]{1,0:T(8,128)} %copy-done.20) | copy-start | bytes 196612
  148.0 8.3 %copy-start.24 = (f32[128,128]{1,0:T(8,128)S(1)}, f32[128,128]{1,0:T(8,128)}, u32[]{:S(2)}) copy-start(f32[128,128]{1,0:T(8,128)} %divide_multiply_fusion) | copy-start | bytes 196612
  148.9 9.9 %all-to-all-start.2 = ((bf16[4,2,128,4,8]{2,4,3,1,0:T(8,128)(2,1)}), bf16[4,2,128,4,8]{2,4,3,1,0:T(8,128)(2,1)S(1)}, u32[]{:S(2)}, u32[]{:S(2)}) async-start(bf16[4,2,128,4,8]{2,4,3,1,0:T(8,128)(2,1)} %copy.220), calls=%async_computation.2 | async-start | bytes 131072 | tf_op jit(solution)/shard_map/all_to_all | solution.py:139
  156.2 1.2 copy-start.27
  156.2 1.3 copy-start.17
  157.4 0.9 copy-start.25

commit v2 on v1

v2 whole, which is shorter than its diff:
```python
import functools
import math

import jax
import jax.numpy as jnp
import ml_dtypes
import numpy as np
from jax import lax
from jax.experimental import pallas as pl
from jax.experimental.pallas import tpu as pltpu
from jax.sharding import Mesh
from jax.sharding import PartitionSpec as P

dual_step = 0.25
primal_step = 0.25
tv_weight = 0.5

COLUMN = ("zq", "x", "zhi", "y")
GROUP = ("zp", "core")
bf16 = jnp.bfloat16
f32 = jnp.float32


def table(length, inverse):
    product = np.outer(np.arange(length), np.arange(length)) % length
    phase = (2.0 * math.pi / length) * product
    real = np.cos(phase) / math.sqrt(length)
    imag = np.sin(phase) / math.sqrt(length) * (1.0 if inverse else -1.0)
    whole = np.stack([np.stack([real, -imag], 1), np.stack([imag, real], 1)])
    return whole.astype(np.float32).astype(ml_dtypes.bfloat16)


def snake(zq, x, zhi, y):
    column = np.zeros((zq, x, zhi, y), np.int32)
    for a in range(zq):
        for h in range(zhi):
            turn = h * zq + a
            for i in range(x):
                for j in range(y):
                    step = i * y + (j if i % 2 == 0 else y - 1 - j)
                    column[a, i, h, j] = turn * x * y + (step if turn % 2 == 0 else x * y - 1 - step)
    return column.reshape(-1)


def dot(a, b):
    return lax.dot_general(a, b, (((1,), (0,)), ((), ())), preferred_element_type=f32)


def dot_t(a, b):
    return lax.dot_general(a, b, (((1,), (1,)), ((), ())), preferred_element_type=f32)


def lanes_to_rows(value, coils):
    n = value.shape[0] // 2
    m = value.shape[1] // coils
    return jnp.concatenate(
        [
            jnp.concatenate([value[p * n : (p + 1) * n, c * m : (c + 1) * m] for p in range(2)], 1)
            for c in range(coils)
        ],
        0,
    )


def to_kspace(maps, image, fz, fy):
    columns = []
    for c in range(maps.shape[0]):
        real, imag = maps[c, 0].astype(f32), maps[c, 1].astype(f32)
        columns.append(
            jnp.concatenate(
                [real * image[0] - imag * image[1], real * image[1] + imag * image[0]], 0
            ).astype(bf16)
        )
    half = dot(fz, jnp.concatenate(columns, 1)).astype(bf16)
    return dot_t(fy, lanes_to_rows(half, maps.shape[0]))


def to_image(dual, maps, gy, gz):
    coils, n = maps.shape[0], maps.shape[2]
    half = dot(gy, dual).astype(bf16)
    field = dot_t(gz, lanes_to_rows(half, coils))
    real_sum, imag_sum = 0.0, 0.0
    for c in range(coils):
        real, imag = maps[c, 0].astype(f32), maps[c, 1].astype(f32)
        m = field.shape[1] // coils
        h_real, h_imag = field[:n, c * m : (c + 1) * m], field[n:, c * m : (c + 1) * m]
        real_sum += real * h_real + imag * h_imag
        imag_sum += real * h_imag - imag * h_real
    return real_sum, imag_sum


def as_lines(data, coils):
    data = data.astype(f32)
    per = data.shape[1] // coils
    return jnp.concatenate(
        [data[:, c * per : (c + 1) * per].reshape(-1, data.shape[2]) for c in range(coils)], 1
    )


def accumulate(sums_ref, out_ref, parts):
    step = pl.program_id(0)

    @pl.when(step == 0)
    def _():
        sums_ref[...] = jnp.zeros_like(sums_ref)

    sums_ref[0] += parts[0]
    sums_ref[1] += parts[1]

    @pl.when(step == pl.num_programs(0) - 1)
    def _():
        out_ref[...] = sums_ref[...].astype(out_ref.dtype)


def spectrum_kernel(maps_ref, image_ref, fz_ref, fy_ref, out_ref):
    out_ref[0] = to_kspace(maps_ref[0], image_ref, fz_ref[...], fy_ref[...])


def first_kernel(spectrum_ref, data_ref, mask_ref, maps_ref, gy_ref, gz_ref, dual_ref, out_ref, sums_ref):
    maps = maps_ref[0]
    data = as_lines(data_ref[0], maps.shape[0])
    mask = mask_ref[0].astype(f32)
    dual = (dual_step * (mask * (spectrum_ref[0] - data))) * (1.0 / (1.0 + dual_step))
    dual_ref[0] = dual
    accumulate(sums_ref, out_ref, to_image(dual.astype(bf16), maps, gy_ref[...], gz_ref[...]))


def second_kernel(
    guess_ref, dual_ref, data_ref, mask_ref, maps_ref, fz_ref, fy_ref, gy_ref, gz_ref, out_ref, sums_ref
):
    maps = maps_ref[0]
    spectrum = to_kspace(maps, guess_ref, fz_ref[...], fy_ref[...])
    data = as_lines(data_ref[0], maps.shape[0])
    mask = mask_ref[0].astype(f32)
    dual = (dual_ref[0] + dual_step * (mask * (spectrum - data))) * (1.0 / (1.0 + dual_step))
    accumulate(sums_ref, out_ref, to_image(dual.astype(bf16), maps, gy_ref[...], gz_ref[...]))


def step_block(a):
    rest = (0,) * (a.ndim - 1)
    return pl.BlockSpec((1, *a.shape[1:]), lambda i: (i, *rest))


def whole_block(a):
    zeros = (0,) * a.ndim
    return pl.BlockSpec(a.shape, lambda i: zeros)


def call(kernel, out, stepped, *operands, sums=None):
    like = jax.tree.leaves(out)
    specs = [step_block(a) if s else whole_block(a) for a, s in zip((*operands, *like), stepped)]
    return pl.pallas_call(
        kernel,
        grid=(next(a.shape[0] for a, s in zip(operands, stepped) if s),),
        in_specs=specs[: len(operands)],
        out_specs=specs[len(operands) :],
        out_shape=like,
        scratch_shapes=[] if sums is None else [pltpu.VMEM(sums, f32)],
        compiler_params=pltpu.CompilerParams(vmem_limit_bytes=40 * 1024 * 1024),
    )(*operands)


def diff_up(a, axis):
    n = a.shape[axis]
    up = lax.slice_in_dim(a, 1, n, axis=axis) - lax.slice_in_dim(a, 0, n - 1, axis=axis)
    return jnp.concatenate([up, jnp.zeros_like(lax.slice_in_dim(a, 0, 1, axis=axis))], axis)


def diff_back(a, axis):
    n = a.shape[axis]
    low = lax.slice_in_dim(a, 0, n - 1, axis=axis)
    return jnp.concatenate([jnp.zeros_like(lax.slice_in_dim(a, 0, 1, axis=axis)), low], axis) - a


def shrink(here, ahead, duals):
    moved = (
        duals[0] + dual_step * diff_up(here, 1),
        duals[1] + dual_step * diff_up(here, 2),
        duals[2] + dual_step * (ahead - here),
    )
    size = jnp.sqrt(sum(jnp.sum(m * m, 0) for m in moved))
    factor = 1.0 / jnp.maximum(1.0, size / tv_weight)
    return tuple(m * factor for m in moved)


def on_device(kspace_data, coil_maps, sample_mask, initial_image):
    coils, _, planes, ny, nx = coil_maps.shape
    nz, lines = kspace_data.shape[2:4]
    rows = initial_image.shape[2]
    sizes = [lax.axis_size(a) for a in COLUMN]
    zq, group = sizes[0], lax.axis_size(GROUP)
    count = math.prod(sizes)
    slabs = count // zq
    column_of = snake(*sizes)
    place_of = np.argsort(column_of)
    me = lax.axis_index(COLUMN)
    is_first, is_last = me == int(place_of[0]), me == int(place_of[-1])
    quarters = sizes[3]

    def spread(blocks):
        return lax.all_to_all(blocks, COLUMN, 0, 0, tiled=True)

    pick = np.eye(nx, dtype=np.float32)[column_of]
    near = [pick, np.roll(pick, -1, 1), np.roll(pick, 1, 1)]
    map_rows = jnp.einsum(
        "wx,iryx->wiry", pick.astype(ml_dtypes.bfloat16), coil_maps.reshape(coils * 2, planes, ny, nx),
        preferred_element_type=f32,
    ).astype(bf16)
    high = initial_image.astype(bf16)
    low = (initial_image - high.astype(f32)).astype(bf16)
    image_rows = jnp.einsum(
        "wx,kx->wk",
        np.concatenate(near).astype(ml_dtypes.bfloat16),
        jnp.concatenate([high.reshape(-1, nx), low.reshape(-1, nx)]),
        preferred_element_type=f32,
    ).astype(bf16)
    half = image_rows.shape[1] // 2
    image_rows = jnp.concatenate(
        [image_rows[:nx], image_rows[nx : 2 * nx, :half], image_rows[2 * nx :, :half]], 1
    ).reshape(nx, 2, 4 * half // 2)
    mask_rows = sample_mask.transpose(0, 2, 1).astype(bf16).reshape(quarters, -1, nz)
    mask_rows = jnp.broadcast_to(mask_rows[None], (count // quarters, *mask_rows.shape))
    extra = jnp.concatenate([image_rows, mask_rows.reshape(nx, -1, nz)], 1)
    first = spread(jnp.concatenate([map_rows, extra[:, None]], 1))

    inv_x = table(nx, True)[:, column_of]
    turned = jnp.einsum(
        "ckzyw,jxkw->xcjyz", kspace_data, inv_x, preferred_element_type=f32
    ).astype(bf16)
    second = spread(turned.reshape(nx, coils * 2 * lines, nz))

    maps = first[:, : 2 * coils].reshape(zq, slabs, coils, 2, planes, ny)
    maps = maps.transpose(0, 2, 3, 1, 4, 5).reshape(zq, coils, 2, nz, ny)

    mask = lax.all_gather(first[:, 2 * coils, 2:], COLUMN[3], axis=0)
    mask = mask.reshape(coils, quarters // coils, zq, slabs, 1, -1, nz)
    mask = jnp.broadcast_to(
        mask.transpose(2, 3, 4, 1, 5, 0, 6), (zq, slabs, 2, quarters // coils, mask.shape[5], coils, nz)
    ).reshape(zq, slabs * 2 * lines, coils * nz)

    image = first[:, 2 * coils, :2].reshape(zq, slabs, 4, 2, planes, rows)
    image = lax.all_gather(image.transpose(2, 3, 1, 4, 0, 5), GROUP, axis=5)
    image = image.reshape(4, 2, nz, ny).astype(f32)
    current = image[0] + image[1]
    before = image[2]
    after = jnp.where(is_last, current, image[3])

    ny_order = np.arange(ny).reshape(slabs, lines)
    fz = table(nz, False).reshape(2 * nz, 2 * nz)
    fy = table(ny, False)[:, ny_order].transpose(1, 0, 2, 3, 4).reshape(2 * ny, 2 * ny)
    gy = table(ny, True)[..., ny_order].transpose(0, 1, 3, 2, 4).reshape(2 * ny, 2 * ny)
    gz = table(nz, True).reshape(2 * nz, 2 * nz)
    dual_like = jax.ShapeDtypeStruct((zq, 2 * ny, coils * nz), f32)
    image_like = jax.ShapeDtypeStruct((2, nz, ny), bf16)

    spectrum = call(spectrum_kernel, dual_like, (1, 0, 0, 0, 1), maps, current, fz, fy)[0]
    zero = jnp.zeros_like(current)
    duals = shrink(current, after, (zero,) * 3)
    duals_before = shrink(before, current, (zero,) * 3)

    def tv_gradient():
        return (
            diff_back(duals[0], 1)
            + diff_back(duals[1], 2)
            + jnp.where(is_first, 0.0, duals_before[2])
            - duals[2]
        )

    settled = current - primal_step * tv_gradient()
    data = second.reshape(zq, slabs, coils * 2 * lines, nz)
    dual, grad = call(
        first_kernel, (dual_like, image_like), (1, 1, 1, 1, 0, 0, 1, 0),
        spectrum, data, mask, maps, gy, gz, sums=image_like.shape,
    )
    grad = lax.all_gather(grad, GROUP, axis=0).astype(f32).sum(0)
    updated = settled - primal_step * grad
    guess = 2.0 * updated - current

    forth = [(int(place_of[i]), int(place_of[i + 1])) for i in range(count - 1)]
    before = lax.ppermute(guess, COLUMN, forth)
    after = jnp.where(is_last, guess, lax.ppermute(guess, COLUMN, [(b, a) for a, b in forth]))
    (grad,) = call(
        second_kernel, image_like, (0, 1, 1, 1, 1, 0, 0, 0, 0, 0),
        guess, dual, data, mask, maps, fz, fy, gy, gz, sums=image_like.shape,
    )
    grad = grad.reshape(2, nz, zq, group, rows).transpose(3, 0, 1, 2, 4)
    grad = lax.all_to_all(grad, GROUP, 0, 0, tiled=True).astype(f32).sum(0)

    duals = shrink(guess, after, duals)
    duals_before = shrink(before, guess, duals_before)
    rest = (updated - primal_step * tv_gradient()).reshape(2, nz, zq, group, rows)
    rest = lax.dynamic_index_in_dim(rest, lax.axis_index(GROUP), 3, keepdims=False)
    result = rest - primal_step * grad
    result = result.reshape(2, slabs, planes, zq, rows).transpose(3, 1, 0, 2, 4)
    result = spread(result.reshape(count, 2 * planes * rows))
    return result[place_of].T.reshape(2, planes, rows, nx)


def solution(mesh):
    devices = mesh.devices.reshape(4, 2, 2, 4, 2, 4)
    split = Mesh(devices, ("zq", "zp", "core", "x", "zhi", "y"))
    coil, slab = ("zq", "zp", "core"), ("x", "zhi", "y")
    return jax.shard_map(
        on_device,
        mesh=split,
        in_specs=(
            P(coil, None, None, slab, None),
            P(coil, None, slab, None, None),
            P(coil, None, slab),
            P(None, slab, coil, None),
        ),
        out_specs=P(None, slab, coil, None),
        check_vma=False,
    )
```

time: 227 us -> 197 us (0.87); the launches traced: 223 us -> 196 us
  blocking collectives: 107 us -> 48.3 us
  starting transfers between devices: 47.7 us -> 61.8 us
  waiting for transfers between devices: 34 us -> 48 us
  Pallas kernels: 0 us -> 7.25 us
  matrix products: 7.09 us -> 2.47 us
  local copies, waits for them, and re-layouts: 11.9 us -> 16.3 us
  other arithmetic: 14.7 us -> 11.4 us
    all_to_all x1 -> x0, blocking collectives: 62.9 us -> none  [spread(): return lax.all_to_all(blocks, COLUMN, 0, 0, tiled=True)]
    all_to_all x2 -> x3, starting transfers between devices: 35.5 us -> 54.1 us  [spread(): return lax.all_to_all(blocks, COLUMN, 0, 0, tiled=True)]
    all_to_all x2 -> x3, waiting for transfers between devices: 31.6 us -> 48 us  [spread(): return lax.all_to_all(blocks, COLUMN, 0, 0, tiled=True)]
    pallas_call x0 -> x3, Pallas kernels: none -> 7.25 us  [call(): pl.pallas_call(kernel, grid=(next((a.shape[0] for a, s in zip(operands, s...]
    dot_general x6 -> x3, matrix products: 7.09 us -> 2.47 us  [the longest x1 1.08 us: on_device(): jnp.einsum('wx,kx->wk', np.concatenate(near).astype(ml_dtypes.bfloat16),...]
    all_gather x2 -> x3, blocking collectives: 44 us -> 48.3 us  [the longest x1 29.9 us: on_device(): image = lax.all_gather(image.transpose(2, 3, 1, 4, 0, 5), GROUP, axis=5)]
    convert_element_type x7 -> x1, local copies, waits for them, and re-layouts: 3.5 us -> 0.04 us  [on_device(): turned = jnp.einsum('ckzyw,jxkw->xcjyz', kspace_data, inv_x, preferred_el...]
    another operation x9 -> x0, other arithmetic: 3.24 us -> none
  transfers between devices with their start and end apart: 7 -> 6, of which waited for: 2 -> 2; matrix products, arithmetic and copies ran while one was open for 8% -> 10% of each run, Pallas kernels for 0% -> 3%
where the time goes in v2:
time: 197 us; the launch traced here: 196 us
  starting transfers between devices  61.8 us (31%)
  blocking collectives  48.3 us (25%)
  waiting for transfers between devices  48 us (24%)
  local copies, waits for them, and re-layouts  16.3 us (8%)
  other arithmetic  11.4 us (6%)
  Pallas kernels  7.25 us (4%)
  matrix products  2.47 us (1%)
    all_to_all x3, starting transfers between devices, spread(): return lax.all_to_all(blocks, COLUMN, 0, 0, tiled=True)  54.1 us
    all_to_all x3, waiting for transfers between devices, spread(): return lax.all_to_all(blocks, COLUMN, 0, 0, tiled=True)  48 us
    all_gather x1, blocking collectives, on_device(): image = lax.all_gather(image.transpose(2, 3, 1, 4, 0, 5), GROUP, axis=5)  29.9 us
    all_gather x1, blocking collectives, on_device(): mask = lax.all_gather(first[:, 2 * coils, 2:], COLUMN[3], axis=0)  9.58 us
    all_gather x1, blocking collectives, on_device(): grad = lax.all_gather(grad, GROUP, axis=0).astype(f32).sum(0)  8.8 us
    pallas_call x3, Pallas kernels, call(): pl.pallas_call(kernel, grid=(next((a.shape[0] for a, s in zip(operands, s...  7.25 us
    reduce_sum x6, other arithmetic, shrink(): size = jnp.sqrt(sum((jnp.sum(m * m, 0) for m in moved)))  4.34 us
  transfers between devices with their start and end apart: 6, of which 2 were waited for; matrix products, arithmetic and copies ran while one was open for 10% of the time, Pallas kernels for 3%

profile of v2, /device:TPU:1, one launch (start us, length us, event | category | flops | bytes accessed | tf_op | source)
XLA Modules:
  0.0 196.3 jit_solution(9513468291858419401)
XLA Ops:
  0.0 0.8 subtract_convert_fusion
  0.8 1.1 fusion.2
  2.0 0.1 copy.58
  2.1 0.7 convert_element_type.46
  2.9 1.1 convolution_convert_fusion
  4.0 1.4 copy.59
  5.4 23.0 %all-to-all-start = ((bf16[128,5,4,128]{3,2,1,0:T(4,128)(2,1)}), bf16[128,5,4,128]{3,2,1,0:T(4,128)(2,1)S(1)}, u32[]{:S(2)}, u32[]{:S(2)}) async-start(bf16[128,5,4,128]{3,2,1,0:T(4,128)(2,1)} %copy.59), calls=%async_computation | async-start | bytes 1310720 | tf_op jit(solution)/shard_map/all_to_all | solution.py:201
  28.4 0.3 fusion.1
  28.8 1.1 copy.67
  29.9 33.1 %all-to-all-done = bf16[128,5,4,128]{3,2,1,0:T(4,128)(2,1)S(1)} async-done(((bf16[128,5,4,128]{3,2,1,0:T(4,128)(2,1)}), bf16[128,5,4,128]{3,2,1,0:T(4,128)(2,1)S(1)}, u32[]{:S(2)}, u32[]{:S(2)}) %all-to-all-start) | async-done | bytes 655392 | tf_op jit(solution)/shard_map/all_to_all | solution.py:201
  63.0 12.4 %all-to-all-start.1 = ((bf16[128,16,128]{2,1,0:T(8,128)(2,1)}), bf16[128,16,128]{2,1,0:T(8,128)(2,1)S(1)}, u32[]{:S(2)}, u32[]{:S(2)}) async-start(bf16[128,16,128]{2,1,0:T(8,128)(2,1)} %copy.67), calls=%async_computation.1 | async-start | bytes 1048576 | tf_op jit(solution)/shard_map/all_to_all | solution.py:201
  75.4 0.7 fusion.13
  76.1 0.1 copy.60
  76.2 0.2 reshape_squeeze.3
  76.4 29.9 %all-gather = bf16[4,2,32,4,4,32]{2,4,5,3,1,0:T(4,128)(2,1)S(1)} all-gather(bf16[4,2,32,4,4,8]{2,4,5,3,1,0:T(4,128)(2,1)S(1)} %bitcast.84), channel_id=2, replica_groups=mesh['zq'=4,'zp'=2,'core'=2,'x'=4,'zhi'=2,'y'=4] {'zp','core'}, dimensions={5}, use_global_device_ids=true | all-gather | bytes 327680 | tf_op jit(solution)/shard_map/all_gather | solution.py:242
  106.3 0.2 convert_element_type.53
  106.5 0.1 slice_add_fusion
  106.6 1.0 copy.61
  107.7 1.3 add.138.image_ref
  109.0 0.9 fusion.12
  109.9 1.4 copy.62
  111.3 0.9 squeeze.12
  112.2 0.3 copy.63
  112.5 0.9 squeeze.13
  113.4 0.2 slice.148
  113.6 0.2 copy.64
  113.9 9.6 %all-gather.1 = bf16[512,1,2,128]{3,2,1,0:T(2,128)(2,1)S(1)} all-gather(bf16[128,1,2,128]{3,2,1,0:T(2,128)(2,1)} %get-tuple-element.23), channel_id=3, replica_groups=mesh['zq'=4,'zp'=2,'core'=2,'x'=4,'zhi'=2,'y'=4] {'y'}, dimensions={0}, use_global_device_ids=true | all-gather | bytes 327680 | tf_op jit(solution)/shard_map/all_gather | solution.py:235
  123.5 0.4 copy.68
  123.9 0.3 broadcast_in_dim.40
  124.2 0.3 reshape.121.mask_ref
  124.5 1.8 shard_map.127.spectrum_ref
  126.4 0.1 slice_subtract_fusion.6
  126.6 0.7 slice_subtract_fusion.4
  127.3 0.7 slice_subtract_fusion.5
  128.0 1.3 multiply_reduce_fusion.6
  129.3 0.6 copy-done.24
  129.9 0.7 pad_multiply_fusion.1
  130.7 2.0 shard_map.128
  132.7 8.8 %all-gather.2 = bf16[8,128,128]{2,1,0:T(8,128)(2,1)S(1)} all-gather(bf16[2,128,128]{2,1,0:T(8,128)(2,1)S(1)} %get-tuple-element.7), channel_id=4, replica_groups=mesh['zq'=4,'zp'=2,'core'=2,'x'=4,'zhi'=2,'y'=4] {'zp','core'}, dimensions={0}, use_global_device_ids=true | all-gather | bytes 327680 | tf_op jit(solution)/shard_map/all_gather | solution.py:275
  141.8 0.8 multiply_subtract_fusion.1
  142.5 2.6 %collective-permute-start.1 = (f32[2,128,128]{2,1,0:T(8,128)S(1)}, f32[2,128,128]{2,1,0:T(8,128)S(1)}, u32[]{:S(2)}, u32[]{:S(2)}) collective-permute-start(f32[2,128,128]{2,1,0:T(8,128)S(1)} %get-tuple-element.15.guess_ref), channel_id=1, source_target_pairs={{0,1},{1,2},{2,3},{3,11},{11,10},{10,9},{9,8},{8,16},{16,17},{17,1... | collective-permute-start | bytes 393224 | tf_op jit(solution)/shard_map/ppermute | solution.py:280
  145.1 1.5 collective-permute-start
  146.6 0.7 slice_subtract_fusion.2
  147.3 0.7 slice_subtract_fusion.3
  148.1 3.5 %shard_map.129 = bf16[2,128,128]{2,1,0:T(8,128)(2,1)S(1)} custom-call(f32[2,128,128]{2,1,0:T(8,128)S(1)} %get-tuple-element.15.guess_ref, f32[4,256,256]{2,1,0:T(8,128)S(1)} %get-tuple-element.8.dual_ref, bf16[4,32,16,128]{3,2,1,0:T(8,128)(2,1)S(1)} %bitcast.74, bf16[4,256,256]{2,1,0:T(8,128)(2,1)S(1)} %reshape.121.mask_ref, ...), custom_call_target="tpu_custom_call" | custom-call | tf_op jit(solution)/shard_map/pallas_call | solution.py:152
  151.6 0.1 copy.71
  151.7 0.6 copy.72
  152.3 3.7 %all-to-all-start.2 = ((bf16[4,2,128,4,8]{2,4,3,1,0:T(8,128)(2,1)}), bf16[4,2,128,4,8]{2,4,3,1,0:T(8,128)(2,1)S(1)}, u32[]{:S(2)}, u32[]{:S(2)}) async-start(bf16[4,2,128,4,8]{2,4,3,1,0:T(8,128)(2,1)} %copy.72), calls=%async_computation.2 | async-start | bytes 131072 | tf_op jit(solution)/shard_map/all_to_all | solution.py:287
  156.0 0.9 multiply_reduce_fusion.4
  157.0 0.9 multiply_reduce_fusion.5
  158.0 0.1 slice_subtract_fusion
  158.1 1.1 multiply_reduce_fusion.1
  159.4 0.1 multiply_subtract_fusion
  159.6 0.1 copy.69
  159.7 0.2 copy.70
  159.9 0.2 copy.74
  160.1 0.1 subtract_bitcast_fusion
  160.3 0.2 copy.75
  160.5 0.1 all_to_all.20
  160.6 0.7 copy.76
  161.3 18.7 %all-to-all-start.3 = ((f32[128,1,64]{2,1,0:T(1,128)}), f32[128,1,64]{2,1,0:T(1,128)S(1)}, u32[]{:S(2)}, u32[]{:S(2)}) async-start(f32[128,1,64]{2,1,0:T(1,128)} %copy.76), calls=%async_computation.3 | async-start | bytes 131072 | tf_op jit(solution)/shard_map/all_to_all | solution.py:201
  180.1 14.9 %all-to-all-done.3 = f32[128,1,64]{2,1,0:T(1,128)S(1)} async-done(((f32[128,1,64]{2,1,0:T(1,128)}), f32[128,1,64]{2,1,0:T(1,128)S(1)}, u32[]{:S(2)}, u32[]{:S(2)}) %all-to-all-start.3) | async-done | bytes 32800 | tf_op jit(solution)/shard_map/all_to_all | solution.py:201
  195.0 0.6 gather_fusion
  195.6 0.7 copy.77
  (91 shorter events, 0.7 us)
Async XLA Ops:
  0.0 2.8 %copy-start = (bf16[2,2,4,128,128]{4,3,2,1,0:T(8,128)(2,1)S(1)}, bf16[2,2,4,128,128]{4,3,2,1,0:T(8,128)(2,1)}, u32[]{:S(2)}) copy-start(bf16[2,2,4,128,128]{4,3,2,1,0:T(8,128)(2,1)} %param.14) | copy-start | bytes 1572868
  3.9 24.4 %copy-start.29 = (bf16[2,2,128,4,128]{4,3,2,1,0:T(4,128)(2,1)S(1)}, bf16[2,2,128,4,128]{4,3,2,1,0:T(4,128)(2,1)}, u32[]{:S(2)}) copy-start(bf16[2,2,128,4,128]{4,3,2,1,0:T(4,128)(2,1)} %param.13) | copy-start | bytes 1572868
  3.9 24.4 %copy-start.31 = (bf16[2,128,2,128,1,1]{3,1,2,5,4,0:T(8,128)(2,1)S(1)}, bf16[2,128,2,128,1,1]{3,1,2,5,4,0:T(8,128)(2,1)}, u32[]{:S(2)}) copy-start(bf16[2,128,2,128,1,1]{3,1,2,5,4,0:T(8,128)(2,1)} %constant.116) | copy-start | bytes 393220
  5.4 57.6 %all-to-all-start = ((bf16[128,5,4,128]{3,2,1,0:T(4,128)(2,1)}), bf16[128,5,4,128]{3,2,1,0:T(4,128)(2,1)S(1)}, u32[]{:S(2)}, u32[]{:S(2)}) async-start(bf16[128,5,4,128]{3,2,1,0:T(4,128)(2,1)} %copy.59), calls=%async_computation | async-start | bytes 1310720 | tf_op jit(solution)/shard_map/all_to_all | solution.py:201
  63.0 67.7 %all-to-all-start.1 = ((bf16[128,16,128]{2,1,0:T(8,128)(2,1)}), bf16[128,16,128]{2,1,0:T(8,128)(2,1)S(1)}, u32[]{:S(2)}, u32[]{:S(2)}) async-start(bf16[128,16,128]{2,1,0:T(8,128)(2,1)} %copy.67), calls=%async_computation.1 | async-start | bytes 1048576 | tf_op jit(solution)/shard_map/all_to_all | solution.py:201
  113.6 10.9 %copy-start.4 = (bf16[256,256]{1,0:T(8,128)(2,1)S(1)}, bf16[256,256]{1,0:T(8,128)(2,1)}, u32[]{:S(2)}) copy-start(bf16[256,256]{1,0:T(8,128)(2,1)} %constant.79.clone.fz_ref) | copy-start | bytes 393220
  113.6 10.9 %copy-start.6 = (bf16[256,256]{1,0:T(8,128)(2,1)S(1)}, bf16[256,256]{1,0:T(8,128)(2,1)}, u32[]{:S(2)}) copy-start(bf16[256,256]{1,0:T(8,128)(2,1)} %constant.80.clone.fy_ref) | copy-start | bytes 393220
  124.5 2.0 %copy-start.8 = (f32[2,128,128]{2,1,0:T(8,128)S(1)}, f32[2,128,128]{2,1,0:T(8,128)}, u32[]{:S(2)}) copy-start(f32[2,128,128]{2,1,0:T(8,128)} %squeeze.13) | copy-start | bytes 393220
  124.5 3.5 %copy-start.13 = (f32[2,128,128]{2,1,0:T(8,128)S(1)}, f32[2,128,128]{2,1,0:T(8,128)}, u32[]{:S(2)}) copy-start(f32[2,128,128]{2,1,0:T(8,128)} %squeeze.12) | copy-start | bytes 393220
  126.3 4.3 %copy-start.1 = (bf16[256,256]{1,0:T(8,128)(2,1)S(1)}, bf16[256,256]{1,0:T(8,128)(2,1)}, u32[]{:S(2)}) copy-start(bf16[256,256]{1,0:T(8,128)(2,1)} %constant.81.clone.gy_ref) | copy-start | bytes 393220
  126.4 4.3 %copy-start.2 = (bf16[256,256]{1,0:T(8,128)(2,1)S(1)}, bf16[256,256]{1,0:T(8,128)(2,1)}, u32[]{:S(2)}) copy-start(bf16[256,256]{1,0:T(8,128)(2,1)} %constant.82.clone.gz_ref) | copy-start | bytes 393220
  129.3 0.6 copy-start.24
  130.7 10.9 %copy-start.16 = (f32[2,128,127]{2,1,0:T(8,128)S(1)}, f32[2,128,127]{2,1,0:T(8,128)}, u32[]{:S(2)}) copy-start(f32[2,128,127]{2,1,0:T(8,128)} %slice_subtract_fusion.4) | copy-start | bytes 390148
  130.7 10.9 %copy-start.18 = (f32[2,127,128]{2,1,0:T(8,128)S(1)}, f32[2,127,128]{2,1,0:T(8,128)}, u32[]{:S(2)}) copy-start(f32[2,127,128]{2,1,0:T(8,128)} %slice_subtract_fusion.5) | copy-start | bytes 390148
  130.7 11.0 %copy-start.30 = (f32[128,128]{1,0:T(8,128)S(1)}, f32[128,128]{1,0:T(8,128)}, u32[]{:S(2)}) copy-start(f32[128,128]{1,0:T(8,128)} %get-tuple-element.17) | copy-start | bytes 196612
  130.7 11.0 %copy-start.9 = (f32[2,128,128]{2,1,0:T(8,128)S(1)}, f32[2,128,128]{2,1,0:T(8,128)}, u32[]{:S(2)}) copy-start(f32[2,128,128]{2,1,0:T(8,128)} %get-tuple-element.36) | copy-start | bytes 393220
  130.7 11.0 %copy-start.11 = (f32[2,128,128]{2,1,0:T(8,128)S(1)}, f32[2,128,128]{2,1,0:T(8,128)}, u32[]{:S(2)}) copy-start(f32[2,128,128]{2,1,0:T(8,128)} %get-tuple-element.37) | copy-start | bytes 393220
  130.7 11.0 %copy-start.14 = (f32[2,128,128]{2,1,0:T(8,128)S(1)}, f32[2,128,128]{2,1,0:T(8,128)}, u32[]{:S(2)}) copy-start(f32[2,128,128]{2,1,0:T(8,128)} %squeeze.12) | copy-start | bytes 393220
  130.7 11.0 %copy-start.20 = (f32[2,128,128]{2,1,0:T(8,128)S(1)}, f32[2,128,128]{2,1,0:T(8,128)}, u32[]{:S(2)}) copy-start(f32[2,128,128]{2,1,0:T(8,128)} %get-tuple-element.18) | copy-start | bytes 393220
  130.7 11.0 %copy-start.25 = (f32[128,128]{1,0:T(8,128)S(1)}, f32[128,128]{1,0:T(8,128)}, u32[]{:S(2)}) copy-start(f32[128,128]{1,0:T(8,128)} %copy-done.24) | copy-start | bytes 196612
  132.7 15.3 %copy-start.3 = (bf16[256,256]{1,0:T(8,128)(2,1)S(1)}, bf16[256,256]{1,0:T(8,128)(2,1)}, u32[]{:S(2)}) copy-start(bf16[256,256]{1,0:T(8,128)(2,1)} %constant.82.clone.gz_ref) | copy-start | bytes 393220
  132.7 15.3 %copy-start.5 = (bf16[256,256]{1,0:T(8,128)(2,1)S(1)}, bf16[256,256]{1,0:T(8,128)(2,1)}, u32[]{:S(2)}) copy-start(bf16[256,256]{1,0:T(8,128)(2,1)} %constant.79.clone.fz_ref) | copy-start | bytes 393220
  132.7 15.3 %copy-start.7 = (bf16[256,256]{1,0:T(8,128)(2,1)S(1)}, bf16[256,256]{1,0:T(8,128)(2,1)}, u32[]{:S(2)}) copy-start(bf16[256,256]{1,0:T(8,128)(2,1)} %constant.80.clone.fy_ref) | copy-start | bytes 393220
  141.7 6.3 %copy-start.27 = (f32[128,128]{1,0:T(8,128)}, f32[128,128]{1,0:T(8,128)S(1)}, u32[]{:S(2)}) copy-start(f32[128,128]{1,0:T(8,128)S(1)} %divide_multiply_fusion) | copy-start | bytes 196612
  142.5 15.4 %collective-permute-start.1 = (f32[2,128,128]{2,1,0:T(8,128)S(1)}, f32[2,128,128]{2,1,0:T(8,128)S(1)}, u32[]{:S(2)}, u32[]{:S(2)}) collective-permute-start(f32[2,128,128]{2,1,0:T(8,128)S(1)} %get-tuple-element.15.guess_ref), channel_id=1, source_target_pairs={{0,1},{1,2},{2,3},{3,11},{11,10},{10,9},{9,8},{8,16},{16,17},{17,1... | collective-permute-start | bytes 393224 | tf_op jit(solution)/shard_map/ppermute | solution.py:280
  145.1 13.0 %collective-permute-start = (f32[2,128,128]{2,1,0:T(8,128)S(1)}, f32[2,128,128]{2,1,0:T(8,128)}, u32[]{:S(2)}, u32[]{:S(2)}) collective-permute-start(f32[2,128,128]{2,1,0:T(8,128)S(1)} %get-tuple-element.15.guess_ref), channel_id=1, source_target_pairs={{1,0},{2,1},{3,2},{11,3},{10,11},{9,10},{8,9},{16,8},{17,16},{18,1... | collective-permute-start | bytes 393224 | tf_op jit(solution)/shard_map/ppermute | solution.py:281
  147.3 8.7 %copy-start.12 = (f32[2,128,128]{2,1,0:T(8,128)S(1)}, f32[2,128,128]{2,1,0:T(8,128)}, u32[]{:S(2)}) copy-start(f32[2,128,128]{2,1,0:T(8,128)} %get-tuple-element.37) | copy-start | bytes 393220
  148.0 9.0 %copy-start.10 = (f32[2,128,128]{2,1,0:T(8,128)S(1)}, f32[2,128,128]{2,1,0:T(8,128)}, u32[]{:S(2)}) copy-start(f32[2,128,128]{2,1,0:T(8,128)} %get-tuple-element.36) | copy-start | bytes 393220
  148.0 10.1 %copy-start.15 = (f32[2,128,128]{2,1,0:T(8,128)S(1)}, f32[2,128,128]{2,1,0:T(8,128)}, u32[]{:S(2)}) copy-start(f32[2,128,128]{2,1,0:T(8,128)} %squeeze.12) | copy-start | bytes 393220
  148.0 10.1 %copy-start.17 = (f32[2,128,127]{2,1,0:T(8,128)S(1)}, f32[2,128,127]{2,1,0:T(8,128)}, u32[]{:S(2)}) copy-start(f32[2,128,127]{2,1,0:T(8,128)} %slice_subtract_fusion.4) | copy-start | bytes 390148
  148.0 10.1 %copy-start.19 = (f32[2,127,128]{2,1,0:T(8,128)S(1)}, f32[2,127,128]{2,1,0:T(8,128)}, u32[]{:S(2)}) copy-start(f32[2,127,128]{2,1,0:T(8,128)} %slice_subtract_fusion.5) | copy-start | bytes 390148
  148.0 10.1 %copy-start.21 = (f32[2,128,128]{2,1,0:T(8,128)S(1)}, f32[2,128,128]{2,1,0:T(8,128)}, u32[]{:S(2)}) copy-start(f32[2,128,128]{2,1,0:T(8,128)} %get-tuple-element.18) | copy-start | bytes 393220
  148.1 10.1 %copy-start.26 = (f32[128,128]{1,0:T(8,128)S(1)}, f32[128,128]{1,0:T(8,128)}, u32[]{:S(2)}) copy-start(f32[128,128]{1,0:T(8,128)} %copy-done.24) | copy-start | bytes 196612
  151.6 7.7 %copy-start.22 = (f32[2,128,127]{2,1,0:T(8,128)S(1)}, f32[2,128,127]{2,1,0:T(8,128)}, u32[]{:S(2)}) copy-start(f32[2,128,127]{2,1,0:T(8,128)} %slice_subtract_fusion.2) | copy-start | bytes 390148
  151.6 7.7 %copy-start.23 = (f32[2,127,128]{2,1,0:T(8,128)S(1)}, f32[2,127,128]{2,1,0:T(8,128)}, u32[]{:S(2)}) copy-start(f32[2,127,128]{2,1,0:T(8,128)} %slice_subtract_fusion.3) | copy-start | bytes 390148
  152.3 7.5 %all-to-all-start.2 = ((bf16[4,2,128,4,8]{2,4,3,1,0:T(8,128)(2,1)}), bf16[4,2,128,4,8]{2,4,3,1,0:T(8,128)(2,1)S(1)}, u32[]{:S(2)}, u32[]{:S(2)}) async-start(bf16[4,2,128,4,8]{2,4,3,1,0:T(8,128)(2,1)} %copy.72), calls=%async_computation.2 | async-start | bytes 131072 | tf_op jit(solution)/shard_map/all_to_all | solution.py:287
  157.9 1.5 copy-start.28
  159.5 20.5 %copy-start.32 = (s32[128]{0:T(128)S(1)}, s32[128]{0:T(128)}, u32[]{:S(2)}) copy-start(s32[128]{0:T(128)} %constant.114) | copy-start | bytes 1540
  161.3 33.6 %all-to-all-start.3 = ((f32[128,1,64]{2,1,0:T(1,128)}), f32[128,1,64]{2,1,0:T(1,128)S(1)}, u32[]{:S(2)}, u32[]{:S(2)}) async-start(f32[128,1,64]{2,1,0:T(1,128)} %copy.76), calls=%async_computation.3 | async-start | bytes 131072 | tf_op jit(solution)/shard_map/all_to_all | solution.py:201

commit v3 on v2

v3 whole, which is shorter than its diff:
```python
import math

import jax
import jax.numpy as jnp
import ml_dtypes
import numpy as np
from jax import lax
from jax.experimental import pallas as pl
from jax.experimental.pallas import tpu as pltpu
from jax.sharding import Mesh
from jax.sharding import PartitionSpec as P

dual_step = 0.25
primal_step = 0.25
tv_weight = 0.5

COLUMN = ("zq", "x", "zhi", "y")
GROUP = ("zp", "core")
bf16 = jnp.bfloat16
f32 = jnp.float32


def table(length, inverse):
    product = np.outer(np.arange(length), np.arange(length)) % length
    phase = (2.0 * math.pi / length) * product
    real = np.cos(phase) / math.sqrt(length)
    imag = np.sin(phase) / math.sqrt(length) * (1.0 if inverse else -1.0)
    whole = np.stack([np.stack([real, -imag], 1), np.stack([imag, real], 1)])
    return whole.astype(np.float32).astype(ml_dtypes.bfloat16)


def snake(zq, x, zhi, y):
    column = np.zeros((zq, x, zhi, y), np.int32)
    for a in range(zq):
        for h in range(zhi):
            turn = h * zq + a
            for i in range(x):
                for j in range(y):
                    step = i * y + (j if i % 2 == 0 else y - 1 - j)
                    column[a, i, h, j] = turn * x * y + (step if turn % 2 == 0 else x * y - 1 - step)
    return column.reshape(-1)


def dot(a, b):
    return lax.dot_general(a, b, (((1,), (0,)), ((), ())), preferred_element_type=f32)


def dot_t(a, b):
    return lax.dot_general(a, b, (((1,), (1,)), ((), ())), preferred_element_type=f32)


def lanes_to_rows(value, coils):
    n = value.shape[0] // 2
    m = value.shape[1] // coils
    return jnp.concatenate(
        [
            jnp.concatenate([value[p * n : (p + 1) * n, c * m : (c + 1) * m] for p in range(2)], 1)
            for c in range(coils)
        ],
        0,
    )


def to_kspace(maps, image, fz, fy):
    columns = []
    for real, imag in maps:
        columns.append(
            jnp.concatenate(
                [real * image[0] - imag * image[1], real * image[1] + imag * image[0]], 0
            ).astype(bf16)
        )
    half = dot(fz, jnp.concatenate(columns, 1)).astype(bf16)
    return dot_t(fy, lanes_to_rows(half, len(maps)))


def to_image(dual, maps, gy, gz):
    coils, n = len(maps), maps[0][0].shape[0]
    half = dot(gy, dual).astype(bf16)
    field = dot_t(gz, lanes_to_rows(half, coils))
    real_sum, imag_sum = 0.0, 0.0
    for c, (real, imag) in enumerate(maps):
        m = field.shape[1] // coils
        h_real, h_imag = field[:n, c * m : (c + 1) * m], field[n:, c * m : (c + 1) * m]
        real_sum += real * h_real + imag * h_imag
        imag_sum += real * h_imag - imag * h_real
    return real_sum, imag_sum


def accumulate(sums_ref, out_ref, parts):
    step = pl.program_id(0)

    @pl.when(step == 0)
    def _():
        sums_ref[...] = jnp.zeros_like(sums_ref)

    sums_ref[0] += parts[0]
    sums_ref[1] += parts[1]

    @pl.when(step == pl.num_programs(0) - 1)
    def _():
        out_ref[...] = sums_ref[...].astype(out_ref.dtype)


def split_blocks(block_ref, coils):
    n = block_ref.shape[1]

    def lane(i):
        return block_ref[0, :, i * n : (i + 1) * n].astype(f32)

    maps = [[lane(2 * c + p) for p in range(2)] for c in range(coils)]
    data = jnp.concatenate(
        [
            jnp.concatenate([lane(2 * coils + 2 * c + p) for c in range(coils)], 1)
            for p in range(2)
        ],
        0,
    )
    return maps, data


def masked(mask_ref, value):
    mask = mask_ref[0].astype(f32)
    return jnp.concatenate([mask, mask], 0) * value


def shifted(a, axis, step):
    n = a.shape[axis]
    if step > 0:
        pieces = (lax.slice_in_dim(a, 1, n, axis=axis), lax.slice_in_dim(a, 0, 1, axis=axis))
    else:
        pieces = (lax.slice_in_dim(a, n - 1, n, axis=axis), lax.slice_in_dim(a, 0, n - 1, axis=axis))
    return jnp.concatenate(pieces, axis)


def position(shape, axis):
    return lax.broadcasted_iota(jnp.int32, shape, axis)


def shrink(here, ahead, duals):
    moved = []
    for p in range(2):
        a = here[p]
        up_z = jnp.where(position(a.shape, 0) < a.shape[0] - 1, shifted(a, 0, 1) - a, 0.0)
        up_y = jnp.where(position(a.shape, 1) < a.shape[1] - 1, shifted(a, 1, 1) - a, 0.0)
        steps = [dual_step * up_z, dual_step * up_y, dual_step * (ahead[p] - a)]
        moved.append(steps if duals is None else [d + s for d, s in zip(duals[p], steps)])
    size = jnp.sqrt(sum(m * m for part in moved for m in part))
    factor = 1.0 / jnp.maximum(1.0, size / tv_weight)
    return [[m * factor for m in part] for part in moved]


def divergence(duals, duals_before, has_before):
    sums = []
    for p in range(2):
        d_z, d_y, d_x = duals[p]
        back_z = jnp.where(position(d_z.shape, 0) > 0, shifted(d_z, 0, -1), 0.0)
        back_y = jnp.where(position(d_y.shape, 1) > 0, shifted(d_y, 1, -1), 0.0)
        sums.append((back_z - d_z) + (back_y - d_y) + (has_before * duals_before[p][2] - d_x))
    return sums


def read_start(edge_ref, start_ref):
    here = [start_ref[0, p].astype(f32) + start_ref[1, p].astype(f32) for p in range(2)]
    before = [start_ref[2, p].astype(f32) for p in range(2)]
    has_after = edge_ref[1]
    after = [jnp.where(has_after > 0.0, start_ref[3, p].astype(f32), here[p]) for p in range(2)]
    return before, here, after


def first_kernel(
    edge_ref, start_ref, block_ref, mask_ref, fz_ref, fy_ref, gy_ref, gz_ref,
    dual_ref, out_ref, settled_ref, image_ref, sums_ref,
):
    @pl.when(pl.program_id(0) == 0)
    def _():
        before, here, after = read_start(edge_ref, start_ref)
        spread = divergence(shrink(here, after, None), shrink(before, here, None), edge_ref[0])
        for p in range(2):
            image_ref[p] = here[p]
            settled_ref[p] = here[p] - primal_step * spread[p]

    maps, data = split_blocks(block_ref, mask_ref.shape[2] // mask_ref.shape[1])
    spectrum = to_kspace(maps, image_ref, fz_ref[...], fy_ref[...])
    dual = (dual_step * masked(mask_ref, spectrum - data)) * (1.0 / (1.0 + dual_step))
    dual_ref[0] = dual
    accumulate(sums_ref, out_ref, to_image(dual.astype(bf16), maps, gy_ref[...], gz_ref[...]))


def second_kernel(
    guess_ref, dual_ref, block_ref, mask_ref, fz_ref, fy_ref, gy_ref, gz_ref, out_ref, sums_ref
):
    maps, data = split_blocks(block_ref, mask_ref.shape[2] // mask_ref.shape[1])
    spectrum = to_kspace(maps, guess_ref, fz_ref[...], fy_ref[...])
    dual = (dual_ref[0] + dual_step * masked(mask_ref, spectrum - data)) * (1.0 / (1.0 + dual_step))
    accumulate(sums_ref, out_ref, to_image(dual.astype(bf16), maps, gy_ref[...], gz_ref[...]))


def last_kernel(edge_ref, start_ref, updated_ref, guess_ref, before_ref, after_ref, out_ref):
    old_before, old_here, old_after = read_start(edge_ref, start_ref)
    has_after = edge_ref[1]
    here = [guess_ref[p] for p in range(2)]
    before = [before_ref[p] for p in range(2)]
    after = [jnp.where(has_after > 0.0, after_ref[p], here[p]) for p in range(2)]
    duals = shrink(here, after, shrink(old_here, old_after, None))
    duals_before = shrink(before, here, shrink(old_before, old_here, None))
    spread = divergence(duals, duals_before, edge_ref[0])
    for p in range(2):
        out_ref[p] = updated_ref[p] - primal_step * spread[p]


def step_block(a):
    rest = (0,) * (a.ndim - 1)
    return pl.BlockSpec((1, *a.shape[1:]), lambda i: (i, *rest))


def whole_block(a):
    if a.ndim == 1:
        return pl.BlockSpec(memory_space=pltpu.SMEM)
    zeros = (0,) * a.ndim
    return pl.BlockSpec(a.shape, lambda i: zeros)


def call(kernel, outs, stepped, *operands, steps, scratch=()):
    specs = [step_block(a) if s else whole_block(a) for a, s in zip((*operands, *outs), stepped)]
    return pl.pallas_call(
        kernel,
        grid=(steps,),
        in_specs=specs[: len(operands)],
        out_specs=specs[len(operands) :],
        out_shape=outs,
        scratch_shapes=[pltpu.VMEM(shape, f32) for shape in scratch],
        compiler_params=pltpu.CompilerParams(vmem_limit_bytes=40 * 1024 * 1024),
    )(*operands)


def on_device(kspace_data, coil_maps, sample_mask, initial_image):
    coils, _, planes, ny, nx = coil_maps.shape
    nz, lines = kspace_data.shape[2:4]
    rows = initial_image.shape[2]
    sizes = [lax.axis_size(a) for a in COLUMN]
    zq, group = sizes[0], lax.axis_size(GROUP)
    count = math.prod(sizes)
    slabs = count // zq
    column_of = snake(*sizes)
    place_of = np.argsort(column_of)
    me = lax.axis_index(COLUMN)
    is_first, is_last = me == int(place_of[0]), me == int(place_of[-1])
    quarters = sizes[3]

    def spread(blocks):
        return lax.all_to_all(blocks, COLUMN, 0, 0, tiled=True)

    pick = np.eye(nx, dtype=np.float32)[column_of]
    near = [pick, np.roll(pick, -1, 1), np.roll(pick, 1, 1)]
    map_rows = jnp.einsum(
        "wx,iryx->wriy", pick.astype(ml_dtypes.bfloat16), coil_maps.reshape(coils * 2, planes, ny, nx),
        preferred_element_type=f32,
    ).astype(bf16)
    inv_x = table(nx, True)[:, column_of]
    turned = jnp.einsum(
        "ckzyw,jxkw->xycjz", kspace_data, inv_x, preferred_element_type=f32
    ).astype(bf16)
    high = initial_image.astype(bf16)
    low = (initial_image - high.astype(f32)).astype(bf16)
    image_rows = jnp.einsum(
        "wx,kx->wk",
        np.concatenate(near).astype(ml_dtypes.bfloat16),
        jnp.concatenate([high.reshape(-1, nx), low.reshape(-1, nx)]),
        preferred_element_type=f32,
    ).astype(bf16)
    half = image_rows.shape[1] // 2
    image_rows = jnp.concatenate(
        [image_rows[:nx], image_rows[nx : 2 * nx, :half], image_rows[2 * nx :, :half]], 1
    ).reshape(nx, 2, 2 * half)
    mask_rows = sample_mask.transpose(0, 2, 1).astype(bf16).reshape(quarters, -1, nz)
    mask_rows = jnp.broadcast_to(mask_rows[None], (count // quarters, *mask_rows.shape))
    extra = jnp.concatenate([image_rows, mask_rows.reshape(nx, -1, nz)], 1)
    lanes = coils * 2 * ny
    blocks = spread(
        jnp.concatenate([map_rows.reshape(nx, planes, lanes), turned.reshape(nx, lines, lanes), extra], 2)
    )
    extra = blocks[:, :, 2 * lanes :]
    blocks = blocks.reshape(zq, nz, -1)

    mask = lax.all_gather(extra[:, 2:], COLUMN[3], axis=0)
    mask = mask.reshape(coils, quarters // coils, zq, slabs, -1, nz)
    mask = mask.transpose(2, 3, 1, 4, 0, 5).reshape(zq, slabs * lines, coils * nz)

    start = extra[:, :2].reshape(zq, slabs, 4, 2, planes, rows)
    start = lax.all_gather(start.transpose(2, 3, 1, 4, 0, 5), GROUP, axis=5)
    start = start.reshape(4, 2, nz, ny)
    edge = jnp.stack([1.0 - is_first.astype(f32), 1.0 - is_last.astype(f32)])

    fz, fy = (table(n, False).reshape(2 * n, 2 * n) for n in (nz, ny))
    gy, gz = (table(n, True).reshape(2 * n, 2 * n) for n in (ny, nz))
    dual_like = jax.ShapeDtypeStruct((zq, 2 * ny, coils * nz), f32)
    grad_like = jax.ShapeDtypeStruct((2, nz, ny), bf16)
    image_like = jax.ShapeDtypeStruct((2, nz, ny), f32)

    dual, grad, settled, current = call(
        first_kernel, (dual_like, grad_like, image_like, image_like), (0, 0, 1, 1, 0, 0, 0, 0, 1, 0, 0, 0),
        edge, start, blocks, mask, fz, fy, gy, gz, steps=zq, scratch=[image_like.shape],
    )
    grad = lax.all_gather(grad, GROUP, axis=0).astype(f32).sum(0)
    updated = settled - primal_step * grad
    guess = 2.0 * updated - current

    forth = [(int(place_of[i]), int(place_of[i + 1])) for i in range(count - 1)]
    before = lax.ppermute(guess, COLUMN, forth)
    after = lax.ppermute(guess, COLUMN, [(b, a) for a, b in forth])
    (grad,) = call(
        second_kernel, (grad_like,), (0, 1, 1, 1, 0, 0, 0, 0, 0),
        guess, dual, blocks, mask, fz, fy, gy, gz, steps=zq, scratch=[image_like.shape],
    )
    grad = grad.reshape(2, nz, zq, group, rows).transpose(3, 0, 1, 2, 4)
    grad = lax.all_to_all(grad, GROUP, 0, 0, tiled=True).astype(f32).sum(0)

    (rest,) = call(
        last_kernel, (image_like,), (0,) * 7, edge, start, updated, guess, before, after, steps=1
    )
    rest = rest.reshape(2, nz, zq, group, rows)
    rest = lax.dynamic_index_in_dim(rest, lax.axis_index(GROUP), 3, keepdims=False)
    result = rest - primal_step * grad
    result = result.reshape(2, slabs, planes, zq, rows).transpose(3, 1, 0, 2, 4)
    result = spread(result.reshape(count, 2 * planes * rows))
    return result[place_of].T.reshape(2, planes, rows, nx)


def solution(mesh):
    devices = mesh.devices.reshape(4, 2, 2, 4, 2, 4)
    split = Mesh(devices, ("zq", "zp", "core", "x", "zhi", "y"))
    coil, slab = ("zq", "zp", "core"), ("x", "zhi", "y")
    return jax.shard_map(
        on_device,
        mesh=split,
        in_specs=(
            P(coil, None, None, slab, None),
            P(coil, None, slab, None, None),
            P(coil, None, slab),
            P(None, slab, coil, None),
        ),
        out_specs=P(None, slab, coil, None),
        check_vma=False,
    )
```

time: 197 us -> 176 us (0.89)
  waiting for transfers between devices: 48 us -> 72.5 us
  starting transfers between devices: 61.8 us -> 42.6 us
  blocking collectives: 48.3 us -> 32.9 us
  other arithmetic: 11.4 us -> 1.23 us
  local copies, waits for them, and re-layouts: 16.3 us -> 13.9 us
    all_to_all x3 -> x2, waiting for transfers between devices: 48 us -> 70.6 us  [spread(): return lax.all_to_all(blocks, COLUMN, 0, 0, tiled=True)]
    all_to_all x3 -> x2, starting transfers between devices: 54.1 us -> 35.8 us  [spread(): return lax.all_to_all(blocks, COLUMN, 0, 0, tiled=True)]
    all_gather x2, blocking collectives: 39.4 us -> 24.2 us  [the longest x1 14.9 us: on_device(): start = lax.all_gather(start.transpose(2, 3, 1, 4, 0, 5), GROUP, axis=5)]
    reduce_sum x6 -> x0, other arithmetic: 4.34 us -> none  [shrink(): size = jnp.sqrt(sum((jnp.sum(m * m, 0) for m in moved)))]
    slice x6 -> x2, local copies, waits for them, and re-layouts: 3.63 us -> 0.22 us  [the longest x1 0.12 us: on_device(): start = extra[:, :2].reshape(zq, slabs, 4, 2, planes, rows)]
    sub x9 -> x0, other arithmetic: 3.18 us -> none  [the longest x8 3.06 us: diff_up(): lax.slice_in_dim(a, 1, n, axis=axis)]
    reshape x4 -> x5, local copies, waits for them, and re-layouts: 1.83 us -> 4.82 us  [the longest x1 2.42 us: on_device(): blocks = blocks.reshape(zq, nz, -1)]
    add x2 -> x0, local copies, waits for them, and re-layouts: 2.33 us -> none  [on_device(): current = image[0] + image[1]]
  transfers between devices with their start and end apart: 6 -> 5, of which waited for: 2 -> 3; matrix products, arithmetic and copies ran while one was open for 10% -> 1% of each run, Pallas kernels for 3% -> 3%
where the time goes in v3:
time: 176 us; the launch traced here: 175 us
  waiting for transfers between devices  72.5 us (41%)
  starting transfers between devices  42.6 us (24%)
  blocking collectives  32.9 us (19%)
  local copies, waits for them, and re-layouts  13.9 us (8%)
  Pallas kernels  8.94 us (5%)
  matrix products  2.86 us (2%)
    all_to_all x2, waiting for transfers between devices, spread(): return lax.all_to_all(blocks, COLUMN, 0, 0, tiled=True)  70.6 us
    all_to_all x2, starting transfers between devices, spread(): return lax.all_to_all(blocks, COLUMN, 0, 0, tiled=True)  35.8 us
    all_gather x1, blocking collectives, on_device(): start = lax.all_gather(start.transpose(2, 3, 1, 4, 0, 5), GROUP, axis=5)  14.9 us
    all_gather x1, blocking collectives, on_device(): mask = lax.all_gather(extra[:, 2:], COLUMN[3], axis=0)  9.37 us
    pallas_call x3, Pallas kernels, call(): pl.pallas_call(kernel, grid=(steps,), in_specs=specs[:len(operands)], out...  8.94 us
    all_gather x1, blocking collectives, on_device(): grad = lax.all_gather(grad, GROUP, axis=0).astype(f32).sum(0)  8.66 us
    all_to_all x1, starting transfers between devices, on_device(): grad = lax.all_to_all(grad, GROUP, 0, 0, tiled=True).astype(f32).sum(0)  3.7 us
  transfers between devices with their start and end apart: 5, of which 3 were waited for; matrix products, arithmetic and copies ran while one was open for 1% of the time, Pallas kernels for 3%

profile of v3, /device:TPU:1, one launch (start us, length us, event | category | flops | bytes accessed | tf_op | source)
XLA Modules:
  0.0 175.3 jit_solution(137150820080203951)
XLA Ops:
  0.0 0.0 copy-start
  0.0 0.8 subtract_convert_fusion
  0.8 1.1 fusion.3
  1.9 0.0 copy-start.4
  1.9 0.0 copy-start.5
  2.0 1.5 fusion.1
  3.5 0.0 copy-done
  3.5 0.0 copy-start.6
  3.5 0.0 copy-done.4
  3.5 0.0 copy-done.5
  3.5 0.3 fusion.2
  3.8 0.0 slice-start
  3.9 0.3 copy-done.6
  4.2 0.1 copy.51
  4.4 0.2 slice-done
  4.6 0.1 maximum_maximum_fusion
  4.7 2.1 %copy.52 = bf16[128,4,1152]{2,1,0:T(4,128)(2,1)} copy(bf16[128,4,1152]{0,2,1:T(8,128)(2,1)S(1)} %maximum_maximum_fusion) | data formatting | bytes 2359296 | tf_op jit(solution)/shard_map/concatenate | solution.py:280
  6.8 22.9 %all-to-all-start = ((bf16[128,4,1152]{2,1,0:T(4,128)(2,1)}), bf16[128,4,1152]{2,1,0:T(4,128)(2,1)S(1)}, u32[]{:S(2)}, u32[]{:S(2)}) async-start(bf16[128,4,1152]{2,1,0:T(4,128)(2,1)} %copy.52), calls=%async_computation | async-start | bytes 2359296 | tf_op jit(solution)/shard_map/all_to_all | solution.py:251
  29.7 0.1 pad_maximum_fusion.1.edge_ref
  29.8 55.7 %all-to-all-done = bf16[128,4,1152]{2,1,0:T(4,128)(2,1)S(1)} async-done(((bf16[128,4,1152]{2,1,0:T(4,128)(2,1)}), bf16[128,4,1152]{2,1,0:T(4,128)(2,1)S(1)}, u32[]{:S(2)}, u32[]{:S(2)}) %all-to-all-start) | async-done | bytes 1179680 | tf_op jit(solution)/shard_map/all_to_all | solution.py:251
  85.5 0.0 copy-start.3
  85.5 0.1 fusion.10
  85.6 0.1 copy.53
  85.7 0.2 reshape.62
  85.9 14.9 %all-gather = bf16[4,2,32,4,4,32]{2,4,5,3,1,0:T(4,128)(2,1)S(1)} all-gather(bf16[4,2,32,4,4,8]{2,4,5,3,1,0:T(4,128)(2,1)S(1)} %bitcast.65), channel_id=2, replica_groups=mesh['zq'=4,'zp'=2,'core'=2,'x'=4,'zhi'=2,'y'=4] {'zp','core'}, dimensions={5}, use_global_device_ids=true | all-gather | bytes 327680 | tf_op jit(solution)/shard_map/all_gather | solution.py:290
  100.7 0.0 copy-done.3
  100.7 2.2 %copy.54 = bf16[4,2,32,4,4,32]{5,4,3,2,1,0:T(4,128)(2,1)} copy(bf16[4,2,32,4,4,32]{2,4,5,3,1,0:T(4,128)(2,1)S(1)} %all-gather) | data formatting | bytes 524288 | tf_op jit(solution)/shard_map/all_gather | solution.py:290
  102.9 2.0 %reshape.63.start_ref = bf16[4,2,128,128]{3,2,1,0:T(8,128)(2,1)S(1)} reshape(bf16[4,2,32,4,4,32]{5,4,3,2,1,0:T(4,128)(2,1)} %copy.54) | data formatting | bytes 524288 | tf_op jit(solution)/shard_map/reshape | solution.py:291
  104.9 9.4 %all-gather.1 = bf16[512,2,128]{2,0,1:T(8,128)(2,1)S(1)} all-gather(bf16[128,2,128]{2,0,1:T(8,128)(2,1)S(1)} %copy.70), channel_id=3, replica_groups=mesh['zq'=4,'zp'=2,'core'=2,'x'=4,'zhi'=2,'y'=4] {'y'}, dimensions={0}, use_global_device_ids=true | all-gather | bytes 327680 | tf_op jit(solution)/shard_map/all_gather | solution.py:285
  114.3 0.3 copy.56
  114.6 0.2 reshape.66.mask_ref
  114.7 0.0 copy-start.1
  114.8 0.0 copy-start.2
  114.8 2.4 %reshape.64.block_ref = bf16[4,128,1152]{2,1,0:T(8,128)(2,1)S(1)} reshape(bf16[128,4,1152]{2,1,0:T(4,128)(2,1)} %copy-done.3) | data formatting | bytes 2359296 | tf_op jit(solution)/shard_map/reshape | solution.py:283
  117.2 0.0 copy-done.1
  117.2 0.0 copy-done.2
  117.2 4.4 %shard_map.127 = (f32[4,256,256]{2,1,0:T(8,128)S(1)}, bf16[2,128,128]{2,1,0:T(8,128)(2,1)S(1)}, f32[2,128,128]{2,1,0:T(8,128)S(1)}, f32[2,128,128]{2,1,0:T(8,128)S(1)}) custom-call(f32[2]{0:T(128)S(1)} %pad_maximum_fusion.1.edge_ref, bf16[4,2,128,128]{3,2,1,0:T(8,128)(2,1)S(1)} %reshape.63.start_ref, bf16[4,128,1152]{2,1,0:T(8,128)(2,1)S(1)} %reshape.64.block_ref, ...), custom_call_target="tpu_custom_call" | custom-call | tf_op jit(solution)/shard_map/pallas_call | solution.py:225
  121.6 8.7 %all-gather.2 = bf16[8,128,128]{2,1,0:T(8,128)(2,1)S(1)} all-gather(bf16[2,128,128]{2,1,0:T(8,128)(2,1)S(1)} %get-tuple-element.10), channel_id=4, replica_groups=mesh['zq'=4,'zp'=2,'core'=2,'x'=4,'zhi'=2,'y'=4] {'zp','core'}, dimensions={0}, use_global_device_ids=true | all-gather | bytes 327680 | tf_op jit(solution)/shard_map/all_gather | solution.py:304
  130.3 1.8 %collective-permute-start = (f32[2,128,128]{2,1,0:T(8,128)S(1)}, f32[2,128,128]{2,1,0:T(8,128)S(1)}, u32[]{:S(2)}, u32[]{:S(2)}) collective-permute-start(f32[2,128,128]{2,1,0:T(8,128)S(1)} %get-tuple-element.13.guess_ref), channel_id=1, source_target_pairs={{0,1},{1,2},{2,3},{3,11},{11,10},{10,9},{9,8},{8,16},{16,17},{17,1... | collective-permute-start | bytes 393224 | tf_op jit(solution)/shard_map/ppermute | solution.py:309
  132.2 1.3 collective-permute-start.1
  133.5 3.5 %shard_map.129 = bf16[2,128,128]{2,1,0:T(8,128)(2,1)S(1)} custom-call(f32[2,128,128]{2,1,0:T(8,128)S(1)} %get-tuple-element.13.guess_ref, f32[4,256,256]{2,1,0:T(8,128)S(1)} %get-tuple-element.12.dual_ref, bf16[4,128,1152]{2,1,0:T(8,128)(2,1)S(1)} %reshape.64.block_ref, bf16[4,128,256]{2,1,0:T(8,128)(2,1)S(1)} %reshape.66.mask_ref, ...), custom_call_target="tpu_custom_call" | custom-call | tf_op jit(solution)/shard_map/pallas_call | solution.py:225
  137.0 0.1 copy.59
  137.1 0.6 copy.60
  137.8 3.7 %all-to-all-start.1 = ((bf16[4,2,128,4,8]{2,4,3,1,0:T(8,128)(2,1)}), bf16[4,2,128,4,8]{2,4,3,1,0:T(8,128)(2,1)S(1)}, u32[]{:S(2)}, u32[]{:S(2)}) async-start(bf16[4,2,128,4,8]{2,4,3,1,0:T(8,128)(2,1)} %copy.60), calls=%async_computation.1 | async-start | bytes 131072 | tf_op jit(solution)/shard_map/all_to_all | solution.py:316
  141.5 0.0 collective-permute-done.before_ref
  141.5 0.0 collective-permute-done.1.after_ref
  141.5 1.1 shard_map.128
  142.5 0.1 copy.57
  142.7 0.2 copy.58
  142.9 1.9 %all-to-all-done.1 = bf16[4,2,128,4,8]{2,4,3,1,0:T(8,128)(2,1)S(1)} async-done(((bf16[4,2,128,4,8]{2,4,3,1,0:T(8,128)(2,1)}), bf16[4,2,128,4,8]{2,4,3,1,0:T(8,128)(2,1)S(1)}, u32[]{:S(2)}, u32[]{:S(2)}) %all-to-all-start.1) | async-done | bytes 65568 | tf_op jit(solution)/shard_map/all_to_all | solution.py:316
  144.7 0.2 copy.62
  144.9 0.0 copy-start.7
  145.0 0.1 subtract_bitcast_fusion
  145.1 0.2 copy.63
  145.3 0.1 all_to_all.16
  145.4 0.7 copy.64
  146.2 12.8 %all-to-all-start.2 = ((f32[128,1,64]{2,1,0:T(1,128)}), f32[128,1,64]{2,1,0:T(1,128)S(1)}, u32[]{:S(2)}, u32[]{:S(2)}) async-start(f32[128,1,64]{2,1,0:T(1,128)} %copy.64), calls=%async_computation.2 | async-start | bytes 131072 | tf_op jit(solution)/shard_map/all_to_all | solution.py:251
  159.0 0.0 copy-done.7
  159.0 14.9 %all-to-all-done.2 = f32[128,1,64]{2,1,0:T(1,128)S(1)} async-done(((f32[128,1,64]{2,1,0:T(1,128)}), f32[128,1,64]{2,1,0:T(1,128)S(1)}, u32[]{:S(2)}, u32[]{:S(2)}) %all-to-all-start.2) | async-done | bytes 32800 | tf_op jit(solution)/shard_map/all_to_all | solution.py:251
  174.0 0.6 gather_fusion
  174.6 0.7 copy.65
  (14 shorter events, 0.2 us)
Async XLA Ops:
  0.0 3.5 %copy-start = (bf16[2,2,4,128,128]{4,3,2,1,0:T(8,128)(2,1)S(1)}, bf16[2,2,4,128,128]{4,3,2,1,0:T(8,128)(2,1)}, u32[]{:S(2)}) copy-start(bf16[2,2,4,128,128]{4,3,2,1,0:T(8,128)(2,1)} %param.14) | copy-start | bytes 1572868
  1.9 1.6 copy-start.4
  1.9 1.6 copy-start.5
  3.5 0.7 copy-start.6
  3.8 0.8 slice-start
  6.8 78.7 %all-to-all-start = ((bf16[128,4,1152]{2,1,0:T(4,128)(2,1)}), bf16[128,4,1152]{2,1,0:T(4,128)(2,1)S(1)}, u32[]{:S(2)}, u32[]{:S(2)}) async-start(bf16[128,4,1152]{2,1,0:T(4,128)(2,1)} %copy.52), calls=%async_computation | async-start | bytes 2359296 | tf_op jit(solution)/shard_map/all_to_all | solution.py:251
  85.5 15.3 %copy-start.3 = (bf16[128,4,1152]{2,1,0:T(4,128)(2,1)}, bf16[128,4,1152]{2,1,0:T(4,128)(2,1)S(1)}, u32[]{:S(2)}) copy-start(bf16[128,4,1152]{2,1,0:T(4,128)(2,1)S(1)} %all-to-all-done) | copy-start | bytes 3538948
  114.7 2.5 %copy-start.1 = (bf16[256,256]{1,0:T(8,128)(2,1)S(1)}, bf16[256,256]{1,0:T(8,128)(2,1)}, u32[]{:S(2)}) copy-start(bf16[256,256]{1,0:T(8,128)(2,1)} %constant.68.clone.fz_ref.fy_ref) | copy-start | bytes 393220
  114.8 2.5 %copy-start.2 = (bf16[256,256]{1,0:T(8,128)(2,1)S(1)}, bf16[256,256]{1,0:T(8,128)(2,1)}, u32[]{:S(2)}) copy-start(bf16[256,256]{1,0:T(8,128)(2,1)} %constant.69.clone.gy_ref.gz_ref) | copy-start | bytes 393220
  130.3 11.1 %collective-permute-start = (f32[2,128,128]{2,1,0:T(8,128)S(1)}, f32[2,128,128]{2,1,0:T(8,128)S(1)}, u32[]{:S(2)}, u32[]{:S(2)}) collective-permute-start(f32[2,128,128]{2,1,0:T(8,128)S(1)} %get-tuple-element.13.guess_ref), channel_id=1, source_target_pairs={{0,1},{1,2},{2,3},{3,11},{11,10},{10,9},{9,8},{8,16},{16,17},{17,1... | collective-permute-start | bytes 393224 | tf_op jit(solution)/shard_map/ppermute | solution.py:309
  132.2 9.3 %collective-permute-start.1 = (f32[2,128,128]{2,1,0:T(8,128)S(1)}, f32[2,128,128]{2,1,0:T(8,128)S(1)}, u32[]{:S(2)}, u32[]{:S(2)}) collective-permute-start(f32[2,128,128]{2,1,0:T(8,128)S(1)} %get-tuple-element.13.guess_ref), channel_id=1, source_target_pairs={{1,0},{2,1},{3,2},{11,3},{10,11},{9,10},{8,9},{16,8},{17,16},{18,1... | collective-permute-start | bytes 393224 | tf_op jit(solution)/shard_map/ppermute | solution.py:310
  137.8 7.0 %all-to-all-start.1 = ((bf16[4,2,128,4,8]{2,4,3,1,0:T(8,128)(2,1)}), bf16[4,2,128,4,8]{2,4,3,1,0:T(8,128)(2,1)S(1)}, u32[]{:S(2)}, u32[]{:S(2)}) async-start(bf16[4,2,128,4,8]{2,4,3,1,0:T(8,128)(2,1)} %copy.60), calls=%async_computation.1 | async-start | bytes 131072 | tf_op jit(solution)/shard_map/all_to_all | solution.py:316
  144.9 14.1 %copy-start.7 = (s32[128]{0:T(128)S(1)}, s32[128]{0:T(128)}, u32[]{:S(2)}) copy-start(s32[128]{0:T(128)} %constant.77) | copy-start | bytes 1540
  146.2 27.8 %all-to-all-start.2 = ((f32[128,1,64]{2,1,0:T(1,128)}), f32[128,1,64]{2,1,0:T(1,128)S(1)}, u32[]{:S(2)}, u32[]{:S(2)}) async-start(f32[128,1,64]{2,1,0:T(1,128)} %copy.64), calls=%async_computation.2 | async-start | bytes 131072 | tf_op jit(solution)/shard_map/all_to_all | solution.py:251

commit v4 on v3

--- a/solution.py
+++ b/solution.py
@@ -167,10 +167,7 @@
     return before, here, after
 
 
-def first_kernel(
-    edge_ref, start_ref, block_ref, mask_ref, fz_ref, fy_ref, gy_ref, gz_ref,
-    dual_ref, out_ref, settled_ref, image_ref, sums_ref,
-):
+def spectrum_kernel(edge_ref, start_ref, block_ref, fz_ref, fy_ref, spectrum_ref, settled_ref, image_ref):
     @pl.when(pl.program_id(0) == 0)
     def _():
         before, here, after = read_start(edge_ref, start_ref)
@@ -179,9 +176,13 @@
             image_ref[p] = here[p]
             settled_ref[p] = here[p] - primal_step * spread[p]
 
-    maps, data = split_blocks(block_ref, mask_ref.shape[2] // mask_ref.shape[1])
-    spectrum = to_kspace(maps, image_ref, fz_ref[...], fy_ref[...])
-    dual = (dual_step * masked(mask_ref, spectrum - data)) * (1.0 / (1.0 + dual_step))
+    maps, data = split_blocks(block_ref, spectrum_ref.shape[2] // block_ref.shape[1])
+    spectrum_ref[0] = to_kspace(maps, image_ref, fz_ref[...], fy_ref[...]) - data
+
+
+def first_kernel(spectrum_ref, block_ref, mask_ref, gy_ref, gz_ref, dual_ref, out_ref, sums_ref):
+    maps, _ = split_blocks(block_ref, mask_ref.shape[2] // mask_ref.shape[1])
+    dual = (dual_step * masked(mask_ref, spectrum_ref[0])) * (1.0 / (1.0 + dual_step))
     dual_ref[0] = dual
     accumulate(sums_ref, out_ref, to_image(dual.astype(bf16), maps, gy_ref[...], gz_ref[...]))
 
@@ -282,13 +283,18 @@
     extra = blocks[:, :, 2 * lanes :]
     blocks = blocks.reshape(zq, nz, -1)
 
-    mask = lax.all_gather(extra[:, 2:], COLUMN[3], axis=0)
+    def gather(part, axis):
+        copies = jnp.broadcast_to(part[None], (lax.axis_size(axis), *part.shape))
+        return lax.all_to_all(copies, axis, 0, 0, tiled=True)
+
+    start = extra[:, :2].reshape(zq, slabs, 4, 2, planes, rows)
+    start = gather(start.transpose(2, 3, 1, 4, 0, 5).reshape(4, 2, nz, zq * rows), GROUP)
+    mask = extra[:, 2:].reshape(zq, slabs, -1, nz)
+    start, mask = lax.optimization_barrier((start, mask))
+    mask = gather(mask, COLUMN[3])
+    start = start.reshape(group, 4, 2, nz, zq, rows).transpose(1, 2, 3, 4, 0, 5).reshape(4, 2, nz, ny)
     mask = mask.reshape(coils, quarters // coils, zq, slabs, -1, nz)
     mask = mask.transpose(2, 3, 1, 4, 0, 5).reshape(zq, slabs * lines, coils * nz)
-
-    start = extra[:, :2].reshape(zq, slabs, 4, 2, planes, rows)
-    start = lax.all_gather(start.transpose(2, 3, 1, 4, 0, 5), GROUP, axis=5)
-    start = start.reshape(4, 2, nz, ny)
     edge = jnp.stack([1.0 - is_first.astype(f32), 1.0 - is_last.astype(f32)])
 
     fz, fy = (table(n, False).reshape(2 * n, 2 * n) for n in (nz, ny))
@@ -297,9 +303,13 @@
     grad_like = jax.ShapeDtypeStruct((2, nz, ny), bf16)
     image_like = jax.ShapeDtypeStruct((2, nz, ny), f32)
 
-    dual, grad, settled, current = call(
-        first_kernel, (dual_like, grad_like, image_like, image_like), (0, 0, 1, 1, 0, 0, 0, 0, 1, 0, 0, 0),
-        edge, start, blocks, mask, fz, fy, gy, gz, steps=zq, scratch=[image_like.shape],
+    spectrum, settled, current = call(
+        spectrum_kernel, (dual_like, image_like, image_like), (0, 0, 1, 0, 0, 1, 0, 0),
+        edge, start, blocks, fz, fy, steps=zq,
+    )
+    dual, grad = call(
+        first_kernel, (dual_like, grad_like), (1, 1, 1, 0, 0, 1, 0),
+        spectrum, blocks, mask, gy, gz, steps=zq, scratch=[image_like.shape],
     )
     grad = lax.all_gather(grad, GROUP, axis=0).astype(f32).sum(0)
     updated = settled - primal_step * grad
@@ -323,7 +333,10 @@
     result = rest - primal_step * grad
     result = result.reshape(2, slabs, planes, zq, rows).transpose(3, 1, 0, 2, 4)
     result = spread(result.reshape(count, 2 * planes * rows))
-    return result[place_of].T.reshape(2, planes, rows, nx)
+    result = lax.dot_general(
+        result, pick, (((0,), (0,)), ((), ())), precision=lax.Precision.HIGHEST, preferred_element_type=f32
+    )
+    return result.reshape(2, planes, rows, nx)
 
 
 def solution(mesh):

time: 176 us -> 170 us (0.966)
  blocking collectives: 32.9 us -> 113 us
  waiting for transfers between devices: 72.5 us -> 7.57 us
  starting transfers between devices: 42.6 us -> 21 us
    all_to_all x0 -> x2, blocking collectives: none -> 105 us  [spread(): return lax.all_to_all(blocks, COLUMN, 0, 0, tiled=True)]
    all_to_all x2, waiting for transfers between devices: 70.6 us -> 5.69 us  [gather(): return lax.all_to_all(copies, axis, 0, 0, tiled=True)]
    all_gather x2 -> x0, blocking collectives: 24.2 us -> none  [the longest x1 14.9 us: on_device(): start = lax.all_gather(start.transpose(2, 3, 1, 4, 0, 5), GROUP, axis=5)]
    all_to_all x2, starting transfers between devices: 35.8 us -> 11.8 us  [gather(): return lax.all_to_all(copies, axis, 0, 0, tiled=True)]
    all_gather x1 -> x0, local copies, waits for them, and re-layouts: 2.19 us -> none  [on_device(): start = lax.all_gather(start.transpose(2, 3, 1, 4, 0, 5), GROUP, axis=5)]
    ppermute x1, starting transfers between devices: 1.84 us -> 3.99 us  [on_device(): before = lax.ppermute(guess, COLUMN, forth)]
    broadcast_in_dim x0 -> x4, local copies, waits for them, and re-layouts: none -> 2.13 us  [gather(): copies = jnp.broadcast_to(part[None], (lax.axis_size(axis), *part.shape))]
    reshape x1, local copies, waits for them, and re-layouts: 2.42 us -> 0.29 us  [on_device(): blocks = blocks.reshape(zq, nz, -1)]
  transfers between devices with their start and end apart: 5 -> 5, of which waited for: 3 -> 3; matrix products, arithmetic and copies ran while one was open for 1% -> 1% of each run, Pallas kernels for 3% -> 4%
where the time goes in v4:
time: 170 us
  blocking collectives  113 us (66%)
  starting transfers between devices  21 us (12%)
  local copies, waits for them, and re-layouts  13.2 us (8%)
  Pallas kernels  9.05 us (5%)
  waiting for transfers between devices  7.57 us (4%)
  matrix products  3.64 us (2%)
  other arithmetic  1.94 us (1%)
    all_to_all x2, blocking collectives, spread(): return lax.all_to_all(blocks, COLUMN, 0, 0, tiled=True)  105 us
    all_to_all x2, starting transfers between devices, gather(): return lax.all_to_all(copies, axis, 0, 0, tiled=True)  11.8 us
    pallas_call x4, Pallas kernels, call(): pl.pallas_call(kernel, grid=(steps,), in_specs=specs[:len(operands)], out...  9.05 us
    all_gather x1, blocking collectives, on_device(): grad = lax.all_gather(grad, GROUP, axis=0).astype(f32).sum(0)  7.72 us
    all_to_all x2, waiting for transfers between devices, gather(): return lax.all_to_all(copies, axis, 0, 0, tiled=True)  5.69 us
    ppermute x1, starting transfers between devices, on_device(): before = lax.ppermute(guess, COLUMN, forth)  3.99 us
    all_to_all x1, starting transfers between devices, on_device(): grad = lax.all_to_all(grad, GROUP, 0, 0, tiled=True).astype(f32).sum(0)  3.97 us
  transfers between devices with their start and end apart: 5, of which 3 were waited for; matrix products, arithmetic and copies ran while one was open for 1% of the time, Pallas kernels for 4%

profile of v4, /device:TPU:1, one launch (start us, length us, event | category | flops | bytes accessed | tf_op | source)
XLA Modules:
  0.0 169.7 jit_solution(18108348566261836106)
XLA Ops:
  0.0 0.0 copy-start
  0.0 0.8 subtract_convert_fusion
  0.8 1.1 fusion.3
  1.9 0.0 copy-start.7
  2.0 0.7 convert_element_type.56
  2.7 0.0 copy-start.9
  2.7 0.1 copy.52
  2.8 1.5 fusion.1
  4.4 0.0 copy-done.7
  4.4 0.0 copy-done
  4.4 0.0 copy-done.9
  4.4 0.0 slice-start
  4.4 0.3 fusion.2
  4.8 0.4 slice-done
  5.2 0.1 maximum_maximum_fusion
  5.2 2.1 %copy.53 = bf16[128,4,1152]{2,1,0:T(4,128)(2,1)} copy(bf16[128,4,1152]{0,2,1:T(8,128)(2,1)S(1)} %maximum_maximum_fusion) | data formatting | bytes 2359296 | tf_op jit(solution)/shard_map/concatenate | solution.py:281
  7.3 78.7 %all_to_all.32 = bf16[128,4,1152]{2,1,0:T(4,128)(2,1)S(1)} all-to-all(bf16[128,4,1152]{2,1,0:T(4,128)(2,1)} %copy.53), channel_id=1, replica_groups=mesh['zq'=4,'zp'=2,'core'=2,'x'=4,'zhi'=2,'y'=4] {'zq','x','zhi','y'}, dimensions={0} | all-to-all | bytes 2359296 | tf_op jit(solution)/shard_map/all_to_all | solution.py:252
  86.0 0.1 fusion.10
  86.1 0.1 copy.54
  86.3 0.2 reshape.69
  86.4 1.0 copy.55
  87.4 0.5 broadcast_in_dim.22
  87.9 0.1 copy.56
  88.1 0.8 broadcast_in_dim.23
  88.8 7.8 %all-to-all-start.1 = ((bf16[4,4,2,128,32]{3,4,2,1,0:T(8,128)(2,1)}), bf16[4,4,2,128,32]{3,4,2,1,0:T(8,128)(2,1)S(1)}, u32[]{:S(2)}, u32[]{:S(2)}) async-start(bf16[4,4,2,128,32]{3,4,2,1,0:T(8,128)(2,1)} %broadcast_in_dim.23), calls=%async_computation.1 | async-start | bytes 524288 | tf_op jit(solution)/shard_map/all_to_all | solution.py:288
  96.6 5.0 %all-to-all-done.1 = bf16[4,4,2,128,32]{3,4,2,1,0:T(8,128)(2,1)S(1)} async-done(((bf16[4,4,2,128,32]{3,4,2,1,0:T(8,128)(2,1)}), bf16[4,4,2,128,32]{3,4,2,1,0:T(8,128)(2,1)S(1)}, u32[]{:S(2)}, u32[]{:S(2)}) %all-to-all-start.1) | async-done | bytes 262176 | tf_op jit(solution)/shard_map/all_to_all | solution.py:288
  101.6 0.7 broadcast_in_dim.24
  102.4 4.0 %all-to-all-start.2 = ((bf16[4,4,32,2,128]{4,2,3,1,0:T(8,128)(2,1)}), bf16[4,4,32,2,128]{4,2,3,1,0:T(8,128)(2,1)}, u32[]{:S(2)}, u32[]{:S(2)}) async-start(bf16[4,4,32,2,128]{4,2,3,1,0:T(8,128)(2,1)} %broadcast_in_dim.24), calls=%async_computation.2 | async-start | bytes 524288 | tf_op jit(solution)/shard_map/all_to_all | solution.py:288
  106.4 0.1 pad_maximum_fusion.1.edge_ref
  106.5 0.3 reshape.73.block_ref
  106.9 0.2 copy.62.start_ref
  107.0 0.4 copy-done.1
  107.4 2.7 %shard_map.118 = (f32[4,256,256]{2,1,0:T(8,128)S(1)}, f32[2,128,128]{2,1,0:T(8,128)S(1)}, f32[2,128,128]{2,1,0:T(8,128)S(1)}) custom-call(f32[2]{0:T(128)S(1)} %pad_maximum_fusion.1.edge_ref, bf16[4,2,128,128]{3,2,1,0:T(8,128)(2,1)S(1)} %copy.62.start_ref, bf16[4,128,1152]{2,1,0:T(8,128)(2,1)S(1)} %reshape.73.block_ref, bf16[256,256]{1,0:T(8,128)(2,1)S(1)} %copy-done.1, ...), custom_call_target="tpu_custom_call" | custom-call | tf_op jit(solution)/shard_map/pallas_call | solution.py:226
  110.1 0.6 copy-done.3
  110.7 0.6 copy-done.5
  111.4 0.6 all-to-all-done.2
  112.0 1.9 %copy.61 = bf16[4,32,2,2,2,128]{5,4,3,2,1,0:T(2,128)(2,1)} copy(bf16[4,32,2,2,2,128]{5,1,3,0,2,4:T(8,128)(2,1)} %bitcast.27) | data formatting | bytes 524288 | tf_op jit(solution)/shard_map/transpose | solution.py:297
  113.9 1.1 reshape.75.mask_ref
  115.1 1.8 %shard_map.119 = (f32[4,256,256]{2,1,0:T(8,128)S(1)}, bf16[2,128,128]{2,1,0:T(8,128)(2,1)S(1)}) custom-call(f32[4,256,256]{2,1,0:T(8,128)S(1)} %get-tuple-element.14.spectrum_ref, bf16[4,128,1152]{2,1,0:T(8,128)(2,1)S(1)} %reshape.73.block_ref, bf16[4,128,256]{2,1,0:T(8,128)(2,1)S(1)} %reshape.75.mask_ref, bf16[256,256]{1,0:T(8,128)(2,1)S(1)} %copy-done.2, ...), custom_call_target="tpu_custom_call" | custom-call | tf_op jit(solution)/shard_map/pallas_call | solution.py:226
  116.9 7.7 %all-gather = bf16[8,128,128]{2,1,0:T(8,128)(2,1)S(1)} all-gather(bf16[2,128,128]{2,1,0:T(8,128)(2,1)S(1)} %get-tuple-element.16), channel_id=2, replica_groups=mesh['zq'=4,'zp'=2,'core'=2,'x'=4,'zhi'=2,'y'=4] {'zp','core'}, dimensions={0}, use_global_device_ids=true | all-gather | bytes 327680 | tf_op jit(solution)/shard_map/all_gather | solution.py:314
  124.7 0.0 copy-done.4
  124.7 0.0 copy-done.6
  124.8 1.3 collective-permute-start.1
  126.1 4.0 %collective-permute-start = (f32[2,128,128]{2,1,0:T(8,128)S(1)}, f32[2,128,128]{2,1,0:T(8,128)S(1)}, u32[]{:S(2)}, u32[]{:S(2)}) collective-permute-start(f32[2,128,128]{2,1,0:T(8,128)S(1)} %get-tuple-element.19.guess_ref), channel_id=1, source_target_pairs={{0,1},{1,2},{2,3},{3,11},{11,10},{10,9},{9,8},{8,16},{16,17},{17,1... | collective-permute-start | bytes 393224 | tf_op jit(solution)/shard_map/ppermute | solution.py:319
  130.1 3.5 %shard_map.121 = bf16[2,128,128]{2,1,0:T(8,128)(2,1)S(1)} custom-call(f32[2,128,128]{2,1,0:T(8,128)S(1)} %get-tuple-element.19.guess_ref, f32[4,256,256]{2,1,0:T(8,128)S(1)} %get-tuple-element.18.dual_ref, bf16[4,128,1152]{2,1,0:T(8,128)(2,1)S(1)} %reshape.73.block_ref, bf16[4,128,256]{2,1,0:T(8,128)(2,1)S(1)} %reshape.75.mask_ref, ...), custom_call_target="tpu_custom_call" | custom-call | tf_op jit(solution)/shard_map/pallas_call | solution.py:226
  133.6 0.1 copy.65
  133.7 0.6 copy.66
  134.3 4.0 %all-to-all-start.3 = ((bf16[4,2,128,4,8]{2,4,3,1,0:T(8,128)(2,1)}), bf16[4,2,128,4,8]{2,4,3,1,0:T(8,128)(2,1)S(1)}, u32[]{:S(2)}, u32[]{:S(2)}) async-start(bf16[4,2,128,4,8]{2,4,3,1,0:T(8,128)(2,1)} %copy.66), calls=%async_computation.3 | async-start | bytes 131072 | tf_op jit(solution)/shard_map/all_to_all | solution.py:326
  138.3 0.0 collective-permute-done.1.after_ref
  138.3 0.0 collective-permute-done.before_ref
  138.3 1.1 shard_map.120
  139.4 0.1 copy.63
  139.5 0.2 copy.64
  139.7 1.9 %all-to-all-done.3 = bf16[4,2,128,4,8]{2,4,3,1,0:T(8,128)(2,1)S(1)} async-done(((bf16[4,2,128,4,8]{2,4,3,1,0:T(8,128)(2,1)}), bf16[4,2,128,4,8]{2,4,3,1,0:T(8,128)(2,1)S(1)}, u32[]{:S(2)}, u32[]{:S(2)}) %all-to-all-start.3) | async-done | bytes 65568 | tf_op jit(solution)/shard_map/all_to_all | solution.py:326
  141.6 0.2 copy.68
  141.8 0.0 copy-start.8
  141.8 0.1 subtract_bitcast_fusion
  141.9 0.2 copy.69
  142.2 0.1 all_to_all.24
  142.3 0.1 copy.70
  142.4 26.4 %all_to_all.33 = f32[128,1,64]{2,1,0:T(1,128)S(1)} all-to-all(f32[128,1,64]{2,1,0:T(1,128)S(1)} %copy.70), channel_id=1, replica_groups=mesh['zq'=4,'zp'=2,'core'=2,'x'=4,'zhi'=2,'y'=4] {'zq','x','zhi','y'}, dimensions={0} | all-to-all | bytes 65536 | tf_op jit(solution)/shard_map/all_to_all | solution.py:252
  168.8 0.1 copy.71
  168.9 0.0 copy-done.8
  168.9 0.8 fusion.12
  (21 shorter events, 0.3 us)
Async XLA Ops:
  0.0 4.4 %copy-start = (bf16[2,2,4,128,128]{4,3,2,1,0:T(8,128)(2,1)S(1)}, bf16[2,2,4,128,128]{4,3,2,1,0:T(8,128)(2,1)}, u32[]{:S(2)}) copy-start(bf16[2,2,4,128,128]{4,3,2,1,0:T(8,128)(2,1)} %param.13) | copy-start | bytes 1572868
  1.9 2.4 %copy-start.7 = (bf16[384,128]{0,1:T(8,128)(2,1)}, bf16[384,128]{0,1:T(8,128)(2,1)S(1)}, u32[]{:S(2)}) copy-start(bf16[384,128]{0,1:T(8,128)(2,1)S(1)} %fusion.3) | copy-start | bytes 294916
  2.7 1.7 copy-start.9
  4.4 0.8 slice-start
  88.8 12.8 %all-to-all-start.1 = ((bf16[4,4,2,128,32]{3,4,2,1,0:T(8,128)(2,1)}), bf16[4,4,2,128,32]{3,4,2,1,0:T(8,128)(2,1)S(1)}, u32[]{:S(2)}, u32[]{:S(2)}) async-start(bf16[4,4,2,128,32]{3,4,2,1,0:T(8,128)(2,1)} %broadcast_in_dim.23), calls=%async_computation.1 | async-start | bytes 524288 | tf_op jit(solution)/shard_map/all_to_all | solution.py:288
  102.4 9.7 %all-to-all-start.2 = ((bf16[4,4,32,2,128]{4,2,3,1,0:T(8,128)(2,1)}), bf16[4,4,32,2,128]{4,2,3,1,0:T(8,128)(2,1)}, u32[]{:S(2)}, u32[]{:S(2)}) async-start(bf16[4,4,32,2,128]{4,2,3,1,0:T(8,128)(2,1)} %broadcast_in_dim.24), calls=%async_computation.2 | async-start | bytes 524288 | tf_op jit(solution)/shard_map/all_to_all | solution.py:288
  106.5 0.9 copy-start.1
  107.4 7.7 %copy-start.2 = (bf16[256,256]{1,0:T(8,128)(2,1)S(1)}, bf16[256,256]{1,0:T(8,128)(2,1)}, u32[]{:S(2)}) copy-start(bf16[256,256]{1,0:T(8,128)(2,1)} %constant.65.clone.gy_ref.gz_ref) | copy-start | bytes 393220
  110.1 0.7 copy-start.3
  110.7 0.6 copy-start.5
  115.1 9.6 %copy-start.4 = (f32[2,128,128]{2,1,0:T(8,128)S(1)}, f32[2,128,128]{2,1,0:T(8,128)}, u32[]{:S(2)}) copy-start(f32[2,128,128]{2,1,0:T(8,128)} %copy-done.3) | copy-start | bytes 393220
  115.1 9.6 %copy-start.6 = (f32[2,128,128]{2,1,0:T(8,128)S(1)}, f32[2,128,128]{2,1,0:T(8,128)}, u32[]{:S(2)}) copy-start(f32[2,128,128]{2,1,0:T(8,128)} %copy-done.5) | copy-start | bytes 393220
  124.8 13.5 %collective-permute-start.1 = (f32[2,128,128]{2,1,0:T(8,128)S(1)}, f32[2,128,128]{2,1,0:T(8,128)S(1)}, u32[]{:S(2)}, u32[]{:S(2)}) collective-permute-start(f32[2,128,128]{2,1,0:T(8,128)S(1)} %get-tuple-element.19.guess_ref), channel_id=1, source_target_pairs={{1,0},{2,1},{3,2},{11,3},{10,11},{9,10},{8,9},{16,8},{17,16},{18,1... | collective-permute-start | bytes 393224 | tf_op jit(solution)/shard_map/ppermute | solution.py:320
  126.1 12.2 %collective-permute-start = (f32[2,128,128]{2,1,0:T(8,128)S(1)}, f32[2,128,128]{2,1,0:T(8,128)S(1)}, u32[]{:S(2)}, u32[]{:S(2)}) collective-permute-start(f32[2,128,128]{2,1,0:T(8,128)S(1)} %get-tuple-element.19.guess_ref), channel_id=1, source_target_pairs={{0,1},{1,2},{2,3},{3,11},{11,10},{10,9},{9,8},{8,16},{16,17},{17,1... | collective-permute-start | bytes 393224 | tf_op jit(solution)/shard_map/ppermute | solution.py:319
  134.3 7.2 %all-to-all-start.3 = ((bf16[4,2,128,4,8]{2,4,3,1,0:T(8,128)(2,1)}), bf16[4,2,128,4,8]{2,4,3,1,0:T(8,128)(2,1)S(1)}, u32[]{:S(2)}, u32[]{:S(2)}) async-start(bf16[4,2,128,4,8]{2,4,3,1,0:T(8,128)(2,1)} %copy.66), calls=%async_computation.3 | async-start | bytes 131072 | tf_op jit(solution)/shard_map/all_to_all | solution.py:326
  141.8 27.1 %copy-start.8 = (f32[128,128,1,1]{1,0,3,2:T(8,128)S(1)}, f32[128,128,1,1]{1,0,3,2:T(8,128)}, u32[]{:S(2)}) copy-start(f32[128,128,1,1]{1,0,3,2:T(8,128)} %constant.73) | copy-start | bytes 196612

commit v5 on v3

--- a/solution.py
+++ b/solution.py
@@ -101,25 +101,37 @@
         out_ref[...] = sums_ref[...].astype(out_ref.dtype)
 
 
-def split_blocks(block_ref, coils):
-    n = block_ref.shape[1]
-
-    def lane(i):
-        return block_ref[0, :, i * n : (i + 1) * n].astype(f32)
-
-    maps = [[lane(2 * c + p) for p in range(2)] for c in range(coils)]
-    data = jnp.concatenate(
+def lane_block(ref, i):
+    n = ref.shape[1]
+    return ref[0, :, i * n : (i + 1) * n].astype(f32)
+
+
+def read_maps(maps_ref):
+    coils = maps_ref.shape[2] // maps_ref.shape[1] // 2
+    return [[lane_block(maps_ref, 2 * c + p) for p in range(2)] for c in range(coils)]
+
+
+def read_data(data_ref):
+    coils = data_ref.shape[2] // data_ref.shape[1] // 2
+    return jnp.concatenate(
         [
-            jnp.concatenate([lane(2 * coils + 2 * c + p) for c in range(coils)], 1)
+            jnp.concatenate([lane_block(data_ref, 2 * c + p) for c in range(coils)], 1)
             for p in range(2)
         ],
         0,
     )
-    return maps, data
 
 
 def masked(mask_ref, value):
-    mask = mask_ref[0].astype(f32)
+    coils = value.shape[1] // mask_ref.shape[3]
+    pieces = mask_ref.shape[0] // coils
+    mask = jnp.concatenate(
+        [
+            jnp.concatenate([mask_ref[c * pieces + i, 0].astype(f32) for i in range(pieces)], 0)
+            for c in range(coils)
+        ],
+        1,
+    )
     return jnp.concatenate([mask, mask], 0) * value
 
 
@@ -160,16 +172,13 @@
 
 
 def read_start(edge_ref, start_ref):
-    here = [start_ref[0, p].astype(f32) + start_ref[1, p].astype(f32) for p in range(2)]
-    before = [start_ref[2, p].astype(f32) for p in range(2)]
-    has_after = edge_ref[1]
-    after = [jnp.where(has_after > 0.0, start_ref[3, p].astype(f32), here[p]) for p in range(2)]
-    return before, here, after
+    here, before, after = [[start_ref[i, p].astype(f32) for p in range(2)] for i in range(3)]
+    return before, here, [jnp.where(edge_ref[1] > 0.0, a, h) for a, h in zip(after, here)]
 
 
 def first_kernel(
-    edge_ref, start_ref, block_ref, mask_ref, fz_ref, fy_ref, gy_ref, gz_ref,
-    dual_ref, out_ref, settled_ref, image_ref, sums_ref,
+    edge_ref, start_ref, maps_ref, data_ref, mask_ref, fz_ref, fy_ref, gy_ref, gz_ref,
+    dual_ref, out_ref, change_ref, image_ref, sums_ref,
 ):
     @pl.when(pl.program_id(0) == 0)
     def _():
@@ -177,25 +186,26 @@
         spread = divergence(shrink(here, after, None), shrink(before, here, None), edge_ref[0])
         for p in range(2):
             image_ref[p] = here[p]
-            settled_ref[p] = here[p] - primal_step * spread[p]
-
-    maps, data = split_blocks(block_ref, mask_ref.shape[2] // mask_ref.shape[1])
+            change_ref[p] = spread[p]
+
+    maps = read_maps(maps_ref)
     spectrum = to_kspace(maps, image_ref, fz_ref[...], fy_ref[...])
-    dual = (dual_step * masked(mask_ref, spectrum - data)) * (1.0 / (1.0 + dual_step))
+    dual = (dual_step * masked(mask_ref, spectrum - read_data(data_ref))) * (1.0 / (1.0 + dual_step))
     dual_ref[0] = dual
     accumulate(sums_ref, out_ref, to_image(dual.astype(bf16), maps, gy_ref[...], gz_ref[...]))
 
 
 def second_kernel(
-    guess_ref, dual_ref, block_ref, mask_ref, fz_ref, fy_ref, gy_ref, gz_ref, out_ref, sums_ref
+    guess_ref, dual_ref, maps_ref, data_ref, mask_ref, fz_ref, fy_ref, gy_ref, gz_ref, out_ref, sums_ref
 ):
-    maps, data = split_blocks(block_ref, mask_ref.shape[2] // mask_ref.shape[1])
+    maps = read_maps(maps_ref)
     spectrum = to_kspace(maps, guess_ref, fz_ref[...], fy_ref[...])
-    dual = (dual_ref[0] + dual_step * masked(mask_ref, spectrum - data)) * (1.0 / (1.0 + dual_step))
+    step = dual_step * masked(mask_ref, spectrum - read_data(data_ref))
+    dual = (dual_ref[0] + step) * (1.0 / (1.0 + dual_step))
     accumulate(sums_ref, out_ref, to_image(dual.astype(bf16), maps, gy_ref[...], gz_ref[...]))
 
 
-def last_kernel(edge_ref, start_ref, updated_ref, guess_ref, before_ref, after_ref, out_ref):
+def last_kernel(edge_ref, start_ref, change_ref, guess_ref, before_ref, after_ref, out_ref):
     old_before, old_here, old_after = read_start(edge_ref, start_ref)
     has_after = edge_ref[1]
     here = [guess_ref[p] for p in range(2)]
@@ -205,12 +215,14 @@
     duals_before = shrink(before, here, shrink(old_before, old_here, None))
     spread = divergence(duals, duals_before, edge_ref[0])
     for p in range(2):
-        out_ref[p] = updated_ref[p] - primal_step * spread[p]
-
-
-def step_block(a):
-    rest = (0,) * (a.ndim - 1)
-    return pl.BlockSpec((1, *a.shape[1:]), lambda i: (i, *rest))
+        out_ref[p] = change_ref[p] + spread[p]
+
+
+def step_block(a, dim):
+    return pl.BlockSpec(
+        tuple(1 if i == dim else n for i, n in enumerate(a.shape)),
+        lambda i: tuple(i if k == dim else 0 for k in range(a.ndim)),
+    )
 
 
 def whole_block(a):
@@ -221,7 +233,10 @@
 
 
 def call(kernel, outs, stepped, *operands, steps, scratch=()):
-    specs = [step_block(a) if s else whole_block(a) for a, s in zip((*operands, *outs), stepped)]
+    specs = [
+        whole_block(a) if dim is None else step_block(a, dim)
+        for a, dim in zip((*operands, *outs), stepped)
+    ]
     return pl.pallas_call(
         kernel,
         grid=(steps,),
@@ -260,18 +275,14 @@
     turned = jnp.einsum(
         "ckzyw,jxkw->xycjz", kspace_data, inv_x, preferred_element_type=f32
     ).astype(bf16)
-    high = initial_image.astype(bf16)
-    low = (initial_image - high.astype(f32)).astype(bf16)
     image_rows = jnp.einsum(
         "wx,kx->wk",
         np.concatenate(near).astype(ml_dtypes.bfloat16),
-        jnp.concatenate([high.reshape(-1, nx), low.reshape(-1, nx)]),
+        initial_image.astype(bf16).reshape(-1, nx),
         preferred_element_type=f32,
     ).astype(bf16)
-    half = image_rows.shape[1] // 2
-    image_rows = jnp.concatenate(
-        [image_rows[:nx], image_rows[nx : 2 * nx, :half], image_rows[2 * nx :, :half]], 1
-    ).reshape(nx, 2, 2 * half)
+    image_rows = jnp.concatenate([image_rows[i * nx : (i + 1) * nx] for i in range(3)], 1)
+    image_rows = jnp.pad(image_rows, ((0, 0), (0, -image_rows.shape[1] % nz))).reshape(nx, -1, nz)
     mask_rows = sample_mask.transpose(0, 2, 1).astype(bf16).reshape(quarters, -1, nz)
     mask_rows = jnp.broadcast_to(mask_rows[None], (count // quarters, *mask_rows.shape))
     extra = jnp.concatenate([image_rows, mask_rows.reshape(nx, -1, nz)], 1)
@@ -280,50 +291,60 @@
         jnp.concatenate([map_rows.reshape(nx, planes, lanes), turned.reshape(nx, lines, lanes), extra], 2)
     )
     extra = blocks[:, :, 2 * lanes :]
-    blocks = blocks.reshape(zq, nz, -1)
-
-    mask = lax.all_gather(extra[:, 2:], COLUMN[3], axis=0)
-    mask = mask.reshape(coils, quarters // coils, zq, slabs, -1, nz)
-    mask = mask.transpose(2, 3, 1, 4, 0, 5).reshape(zq, slabs * lines, coils * nz)
-
-    start = extra[:, :2].reshape(zq, slabs, 4, 2, planes, rows)
-    start = lax.all_gather(start.transpose(2, 3, 1, 4, 0, 5), GROUP, axis=5)
-    start = start.reshape(4, 2, nz, ny)
+    pieces = quarters // coils
+
+    mask = extra[:, 2:].reshape(zq, -1, nz)
+    mask = jnp.broadcast_to(mask[None], (quarters, *mask.shape))
+    mask = lax.all_to_all(mask, COLUMN[3], 0, 0, tiled=True)
+
+    start = extra[:, :2].reshape(zq, slabs, -1)[:, :, : 3 * 2 * planes * rows]
+    start = start.reshape(zq, slabs, 3, 2, planes, rows).transpose(2, 3, 1, 4, 0, 5)
+    start = lax.all_gather(start.reshape(3, 2, nz, zq * rows), GROUP, axis=0)
+    start = start.reshape(group, 3, 2, nz, zq, rows).transpose(1, 2, 3, 4, 0, 5).reshape(3, 2, nz, ny)
+
+    maps = blocks[:, :, :lanes].reshape(zq, nz, lanes)
+    data = blocks[:, :, lanes : 2 * lanes].reshape(zq, slabs, pieces, -1, lanes)
+    data = data.transpose(0, 2, 1, 3, 4).reshape(zq, ny, lanes)
     edge = jnp.stack([1.0 - is_first.astype(f32), 1.0 - is_last.astype(f32)])
 
-    fz, fy = (table(n, False).reshape(2 * n, 2 * n) for n in (nz, ny))
-    gy, gz = (table(n, True).reshape(2 * n, 2 * n) for n in (ny, nz))
+    ky_order = np.arange(ny).reshape(slabs, pieces, -1).transpose(1, 0, 2).reshape(-1)
+    fz, gz = (table(nz, inverse).reshape(2 * nz, 2 * nz) for inverse in (False, True))
+    fy = table(ny, False)[:, ky_order].reshape(2 * ny, 2 * ny)
+    gy = table(ny, True)[..., ky_order].reshape(2 * ny, 2 * ny)
     dual_like = jax.ShapeDtypeStruct((zq, 2 * ny, coils * nz), f32)
     grad_like = jax.ShapeDtypeStruct((2, nz, ny), bf16)
     image_like = jax.ShapeDtypeStruct((2, nz, ny), f32)
 
-    dual, grad, settled, current = call(
-        first_kernel, (dual_like, grad_like, image_like, image_like), (0, 0, 1, 1, 0, 0, 0, 0, 1, 0, 0, 0),
-        edge, start, blocks, mask, fz, fy, gy, gz, steps=zq, scratch=[image_like.shape],
-    )
-    grad = lax.all_gather(grad, GROUP, axis=0).astype(f32).sum(0)
-    updated = settled - primal_step * grad
-    guess = 2.0 * updated - current
+    dual, grad, change, current = call(
+        first_kernel, (dual_like, grad_like, image_like, image_like),
+        (None, None, 0, 0, 1, None, None, None, None, 0, None, None, None),
+        edge, start, maps, data, mask, fz, fy, gy, gz, steps=zq, scratch=[image_like.shape],
+    )
+    change = change + lax.all_gather(grad, GROUP, axis=0).astype(f32).sum(0)
+    guess = current - (2.0 * primal_step) * change
 
     forth = [(int(place_of[i]), int(place_of[i + 1])) for i in range(count - 1)]
     before = lax.ppermute(guess, COLUMN, forth)
     after = lax.ppermute(guess, COLUMN, [(b, a) for a, b in forth])
     (grad,) = call(
-        second_kernel, (grad_like,), (0, 1, 1, 1, 0, 0, 0, 0, 0),
-        guess, dual, blocks, mask, fz, fy, gy, gz, steps=zq, scratch=[image_like.shape],
+        second_kernel, (grad_like,), (None, 0, 0, 0, 1, None, None, None, None, None),
+        guess, dual, maps, data, mask, fz, fy, gy, gz, steps=zq, scratch=[image_like.shape],
     )
     grad = grad.reshape(2, nz, zq, group, rows).transpose(3, 0, 1, 2, 4)
     grad = lax.all_to_all(grad, GROUP, 0, 0, tiled=True).astype(f32).sum(0)
 
     (rest,) = call(
-        last_kernel, (image_like,), (0,) * 7, edge, start, updated, guess, before, after, steps=1
+        last_kernel, (image_like,), (None,) * 7, edge, start, change, guess, before, after, steps=1
     )
     rest = rest.reshape(2, nz, zq, group, rows)
     rest = lax.dynamic_index_in_dim(rest, lax.axis_index(GROUP), 3, keepdims=False)
-    result = rest - primal_step * grad
+    result = rest + grad
     result = result.reshape(2, slabs, planes, zq, rows).transpose(3, 1, 0, 2, 4)
     result = spread(result.reshape(count, 2 * planes * rows))
-    return result[place_of].T.reshape(2, planes, rows, nx)
+    result = lax.dot_general(
+        result, pick, (((0,), (0,)), ((), ())), precision=lax.Precision.HIGHEST, preferred_element_type=f32
+    )
+    return initial_image - primal_step * result.reshape(2, planes, rows, nx)
 
 
 def solution(mesh):

time: 176 us -> 162 us (0.920)
  waiting for transfers between devices: 72.5 us -> 57.5 us
  blocking collectives: 32.9 us -> 42.6 us
  starting transfers between devices: 42.6 us -> 36.5 us
  local copies, waits for them, and re-layouts: 13.9 us -> 9.93 us
    all_to_all x0 -> x1, blocking collectives: none -> 26.8 us  [spread(): return lax.all_to_all(blocks, COLUMN, 0, 0, tiled=True)]
    all_gather x3 -> x2, blocking collectives: 32.9 us -> 15.7 us  [the longest x1 9.78 us: on_device(): start = lax.all_gather(start.reshape(3, 2, nz, zq * rows), GROUP, axis=0)]
    all_to_all x2 -> x1, waiting for transfers between devices: 70.6 us -> 55.6 us  [spread(): return lax.all_to_all(blocks, COLUMN, 0, 0, tiled=True)]
    all_to_all x2 -> x1, starting transfers between devices: 35.8 us -> 23 us  [spread(): return lax.all_to_all(blocks, COLUMN, 0, 0, tiled=True)]
    all_to_all x0 -> x1, starting transfers between devices: none -> 4.25 us  [on_device(): mask = lax.all_to_all(mask, COLUMN[3], 0, 0, tiled=True)]
    reshape x4, local copies, waits for them, and re-layouts: 4.7 us -> 0.56 us  [the longest x1 0.2 us: on_device(): data = data.transpose(0, 2, 1, 3, 4).reshape(zq, ny, lanes)]
    ppermute x1, starting transfers between devices: 1.84 us -> 4.28 us  [on_device(): before = lax.ppermute(guess, COLUMN, forth)]
    all_gather x1 -> x0, local copies, waits for them, and re-layouts: 2.19 us -> none  [on_device(): start = lax.all_gather(start.transpose(2, 3, 1, 4, 0, 5), GROUP, axis=5)]
  transfers between devices with their start and end apart: 5 -> 5, of which waited for: 3 -> 2; matrix products, arithmetic and copies ran while one was open for 1% -> 4% of each run, Pallas kernels for 3% -> 3%
where the time goes in v5:
time: 162 us; the launch traced here: 161 us
  waiting for transfers between devices  57.5 us (35%)
  blocking collectives  42.6 us (26%)
  starting transfers between devices  36.5 us (23%)
  local copies, waits for them, and re-layouts  9.93 us (6%)
  Pallas kernels  9.02 us (6%)
  matrix products  3.61 us (2%)
  other arithmetic  1.89 us (1%)
    all_to_all x1, waiting for transfers between devices, spread(): return lax.all_to_all(blocks, COLUMN, 0, 0, tiled=True)  55.6 us
    all_to_all x1, blocking collectives, spread(): return lax.all_to_all(blocks, COLUMN, 0, 0, tiled=True)  26.8 us
    all_to_all x1, starting transfers between devices, spread(): return lax.all_to_all(blocks, COLUMN, 0, 0, tiled=True)  23 us
    all_gather x1, blocking collectives, on_device(): start = lax.all_gather(start.reshape(3, 2, nz, zq * rows), GROUP, axis=0)  9.78 us
    pallas_call x3, Pallas kernels, call(): pl.pallas_call(kernel, grid=(steps,), in_specs=specs[:len(operands)], out...  9.02 us
    all_gather x1, blocking collectives, on_device(): change = change + lax.all_gather(grad, GROUP, axis=0).astype(f32).sum(0)  5.96 us
    ppermute x1, starting transfers between devices, on_device(): before = lax.ppermute(guess, COLUMN, forth)  4.28 us
    all_to_all x1, starting transfers between devices, on_device(): mask = lax.all_to_all(mask, COLUMN[3], 0, 0, tiled=True)  4.25 us
  transfers between devices with their start and end apart: 5, of which 2 were waited for; matrix products, arithmetic and copies ran while one was open for 4% of the time, Pallas kernels for 3%

profile of v5, /device:TPU:1, one launch (start us, length us, event | category | flops | bytes accessed | tf_op | source)
XLA Modules:
  0.0 161.4 jit_solution(5356946652656826444)
XLA Ops:
  0.0 0.0 copy-start
  0.0 0.7 convert_element_type.46
  0.8 0.8 convert_element_type.44
  1.5 1.1 convolution_convert_fusion.1
  2.6 0.0 copy-start.7
  2.6 0.1 copy.55
  2.8 1.5 fusion.1
  4.3 0.0 copy-done
  4.3 0.0 copy-done.7
  4.3 0.3 fusion.2
  4.7 0.1 maximum_maximum_fusion
  4.7 2.0 %copy.56 = bf16[128,4,1152]{2,1,0:T(4,128)(2,1)} copy(bf16[128,4,1152]{0,2,1:T(8,128)(2,1)S(1)} %maximum_maximum_fusion) | data formatting | bytes 2359296 | tf_op jit(solution)/shard_map/concatenate | solution.py:291
  6.8 23.0 %all-to-all-start = ((bf16[128,4,1152]{2,1,0:T(4,128)(2,1)}), bf16[128,4,1152]{2,1,0:T(4,128)(2,1)S(1)}, u32[]{:S(2)}, u32[]{:S(2)}) async-start(bf16[128,4,1152]{2,1,0:T(4,128)(2,1)} %copy.56), calls=%async_computation | async-start | bytes 2359296 | tf_op jit(solution)/shard_map/all_to_all | solution.py:266
  29.7 0.1 pad_maximum_fusion.edge_ref
  29.8 55.6 %all-to-all-done = bf16[128,4,1152]{2,1,0:T(4,128)(2,1)S(1)} async-done(((bf16[128,4,1152]{2,1,0:T(4,128)(2,1)}), bf16[128,4,1152]{2,1,0:T(4,128)(2,1)S(1)}, u32[]{:S(2)}, u32[]{:S(2)}) %all-to-all-start) | async-done | bytes 1179680 | tf_op jit(solution)/shard_map/all_to_all | solution.py:266
  85.4 0.1 fusion.11
  85.5 0.8 broadcast_in_dim.17
  86.3 4.2 %all-to-all-start.1 = ((bf16[4,4,64,128]{3,2,1,0:T(8,128)(2,1)}), bf16[4,4,64,128]{3,2,1,0:T(8,128)(2,1)S(1)}, u32[]{:S(2)}, u32[]{:S(2)}) async-start(bf16[4,4,64,128]{3,2,1,0:T(8,128)(2,1)} %broadcast_in_dim.17), calls=%async_computation.1 | async-start | bytes 524288 | tf_op jit(solution)/shard_map/all_to_all | solution.py:298
  90.6 0.4 fusion.12
  90.9 0.1 copy.79
  91.0 0.5 copy.62
  91.6 0.2 reshape.68.data_ref
  91.8 0.2 copy.57
  92.0 0.1 reshape.66.maps_ref
  92.2 1.5 copy.58
  93.6 0.0 copy-start.1
  93.6 0.0 copy-start.2
  93.6 0.0 copy-start.3
  93.6 0.0 copy-start.4
  93.6 1.7 %all_gather_reshape.3 = bf16[1,3,2,128,32]{4,3,2,1,0:T(8,128)(2,1)S(1)} reshape(bf16[3,2,32,4,4,8]{5,4,3,2,1,0:T(4,128)(2,1)} %copy.58) | data formatting | bytes 98304 | tf_op jit(solution)/shard_map/all_gather;reshape | solution.py:302
  95.3 0.1 copy.59
  95.4 9.8 %all_gather.9 = bf16[4,3,2,128,32]{3,4,2,1,0:T(8,128)(2,1)S(1)} all-gather(bf16[1,3,2,128,32]{3,4,2,1,0:T(8,128)(2,1)S(1)} %copy.59), channel_id=1, replica_groups=mesh['zq'=4,'zp'=2,'core'=2,'x'=4,'zhi'=2,'y'=4] {'zp','core'}, dimensions={0}, use_global_device_ids=true | all-gather | bytes 245760 | tf_op jit(solution)/shard_map/all_gather | solution.py:302
  105.3 0.2 copy.64.start_ref
  105.4 0.0 all-to-all-done.1.mask_ref
  105.5 0.0 copy-done.1
  105.5 0.0 copy-done.2
  105.5 0.0 copy-done.3
  105.5 0.0 copy-done.4
  105.5 4.4 %shard_map.118 = (f32[4,256,256]{2,1,0:T(8,128)S(1)}, bf16[2,128,128]{2,1,0:T(8,128)(2,1)S(1)}, f32[2,128,128]{2,1,0:T(8,128)S(1)}, f32[2,128,128]{2,1,0:T(8,128)S(1)}) custom-call(f32[2]{0:T(128)S(1)} %pad_maximum_fusion.edge_ref, bf16[3,2,128,128]{3,2,1,0:T(8,128)(2,1)S(1)} %copy.64.start_ref, bf16[4,128,512]{2,1,0:T(8,128)(2,1)S(1)} %reshape.66.maps_ref, ...), custom_call_target="tpu_custom_call" | custom-call | tf_op jit(solution)/shard_map/pallas_call | solution.py:240
  109.9 6.0 %all-gather = bf16[8,128,128]{2,1,0:T(8,128)(2,1)S(1)} all-gather(bf16[2,128,128]{2,1,0:T(8,128)(2,1)S(1)} %get-tuple-element.10), channel_id=2, replica_groups=mesh['zq'=4,'zp'=2,'core'=2,'x'=4,'zhi'=2,'y'=4] {'zp','core'}, dimensions={0}, use_global_device_ids=true | all-gather | bytes 327680 | tf_op jit(solution)/shard_map/all_gather | solution.py:323
  116.0 1.3 collective-permute-start.1
  117.2 4.3 %collective-permute-start = (f32[2,128,128]{2,1,0:T(8,128)S(1)}, f32[2,128,128]{2,1,0:T(8,128)S(1)}, u32[]{:S(2)}, u32[]{:S(2)}) collective-permute-start(f32[2,128,128]{2,1,0:T(8,128)S(1)} %get-tuple-element.13.guess_ref), channel_id=1, source_target_pairs={{0,1},{1,2},{2,3},{3,11},{11,10},{10,9},{9,8},{8,16},{16,17},{17,1... | collective-permute-start | bytes 393224 | tf_op jit(solution)/shard_map/ppermute | solution.py:327
  121.5 3.5 %shard_map.120 = bf16[2,128,128]{2,1,0:T(8,128)(2,1)S(1)} custom-call(f32[2,128,128]{2,1,0:T(8,128)S(1)} %get-tuple-element.13.guess_ref, f32[4,256,256]{2,1,0:T(8,128)S(1)} %get-tuple-element.12.dual_ref, bf16[4,128,512]{2,1,0:T(8,128)(2,1)S(1)} %reshape.66.maps_ref, bf16[4,128,512]{2,1,0:T(8,128)(2,1)S(1)} %reshape.68.data_ref, ...), custom_call_target="tpu_custom_call" | custom-call | tf_op jit(solution)/shard_map/pallas_call | solution.py:240
  125.1 0.1 copy.67
  125.2 0.6 copy.68
  125.9 3.7 %all-to-all-start.2 = ((bf16[4,2,128,4,8]{2,4,3,1,0:T(8,128)(2,1)}), bf16[4,2,128,4,8]{2,4,3,1,0:T(8,128)(2,1)S(1)}, u32[]{:S(2)}, u32[]{:S(2)}) async-start(bf16[4,2,128,4,8]{2,4,3,1,0:T(8,128)(2,1)} %copy.68), calls=%async_computation.2 | async-start | bytes 131072 | tf_op jit(solution)/shard_map/all_to_all | solution.py:334
  129.6 0.0 collective-permute-done.1.after_ref
  129.6 0.0 collective-permute-done.before_ref
  129.6 1.1 shard_map.119
  130.6 0.1 copy.65
  130.8 0.2 copy.66
  131.0 1.9 %all-to-all-done.2 = bf16[4,2,128,4,8]{2,4,3,1,0:T(8,128)(2,1)S(1)} async-done(((bf16[4,2,128,4,8]{2,4,3,1,0:T(8,128)(2,1)}), bf16[4,2,128,4,8]{2,4,3,1,0:T(8,128)(2,1)S(1)}, u32[]{:S(2)}, u32[]{:S(2)}) %all-to-all-start.2) | async-done | bytes 65568 | tf_op jit(solution)/shard_map/all_to_all | solution.py:334
  132.8 0.2 copy.70
  133.0 0.0 copy-start.5
  133.0 0.0 copy-start.6
  133.1 0.1 add_bitcast_fusion
  133.2 0.2 copy.71
  133.4 0.1 all_to_all.20
  133.5 0.1 copy.72
  133.6 26.8 %all_to_all.27 = f32[128,1,64]{2,1,0:T(1,128)S(1)} all-to-all(f32[128,1,64]{2,1,0:T(1,128)S(1)} %copy.72), channel_id=1, replica_groups=mesh['zq'=4,'zp'=2,'core'=2,'x'=4,'zhi'=2,'y'=4] {'zq','x','zhi','y'}, dimensions={0} | all-to-all | bytes 65536 | tf_op jit(solution)/shard_map/all_to_all | solution.py:266
  160.5 0.1 copy.73
  160.5 0.0 copy-done.5
  160.6 0.0 copy-done.6
  160.6 0.8 fusion.3
  (12 shorter events, 0.3 us)
Async XLA Ops:
  0.0 4.3 %copy-start = (bf16[2,2,4,128,128]{4,3,2,1,0:T(8,128)(2,1)S(1)}, bf16[2,2,4,128,128]{4,3,2,1,0:T(8,128)(2,1)}, u32[]{:S(2)}) copy-start(bf16[2,2,4,128,128]{4,3,2,1,0:T(8,128)(2,1)} %param.13) | copy-start | bytes 1572868
  2.6 1.7 %copy-start.7 = (bf16[128,128,1,1]{1,0,3,2:T(8,128)(2,1)S(1)}, bf16[128,128,1,1]{1,0,3,2:T(8,128)(2,1)}, u32[]{:S(2)}) copy-start(bf16[128,128,1,1]{1,0,3,2:T(8,128)(2,1)} %constant.80) | copy-start | bytes 98308
  6.8 78.7 %all-to-all-start = ((bf16[128,4,1152]{2,1,0:T(4,128)(2,1)}), bf16[128,4,1152]{2,1,0:T(4,128)(2,1)S(1)}, u32[]{:S(2)}, u32[]{:S(2)}) async-start(bf16[128,4,1152]{2,1,0:T(4,128)(2,1)} %copy.56), calls=%async_computation | async-start | bytes 2359296 | tf_op jit(solution)/shard_map/all_to_all | solution.py:266
  86.3 19.1 %all-to-all-start.1 = ((bf16[4,4,64,128]{3,2,1,0:T(8,128)(2,1)}), bf16[4,4,64,128]{3,2,1,0:T(8,128)(2,1)S(1)}, u32[]{:S(2)}, u32[]{:S(2)}) async-start(bf16[4,4,64,128]{3,2,1,0:T(8,128)(2,1)} %broadcast_in_dim.17), calls=%async_computation.1 | async-start | bytes 524288 | tf_op jit(solution)/shard_map/all_to_all | solution.py:298
  93.6 11.8 %copy-start.1 = (bf16[256,256]{1,0:T(8,128)(2,1)S(1)}, bf16[256,256]{1,0:T(8,128)(2,1)}, u32[]{:S(2)}) copy-start(bf16[256,256]{1,0:T(8,128)(2,1)} %constant.72.clone.gz_ref) | copy-start | bytes 393220
  93.6 11.8 %copy-start.2 = (bf16[256,256]{1,0:T(8,128)(2,1)S(1)}, bf16[256,256]{1,0:T(8,128)(2,1)}, u32[]{:S(2)}) copy-start(bf16[256,256]{1,0:T(8,128)(2,1)} %constant.71.clone.gy_ref) | copy-start | bytes 393220
  93.6 11.9 %copy-start.3 = (bf16[256,256]{1,0:T(8,128)(2,1)S(1)}, bf16[256,256]{1,0:T(8,128)(2,1)}, u32[]{:S(2)}) copy-start(bf16[256,256]{1,0:T(8,128)(2,1)} %constant.70.clone.fy_ref) | copy-start | bytes 393220
  93.6 11.9 %copy-start.4 = (bf16[256,256]{1,0:T(8,128)(2,1)S(1)}, bf16[256,256]{1,0:T(8,128)(2,1)}, u32[]{:S(2)}) copy-start(bf16[256,256]{1,0:T(8,128)(2,1)} %constant.69.clone.fz_ref) | copy-start | bytes 393220
  116.0 13.6 %collective-permute-start.1 = (f32[2,128,128]{2,1,0:T(8,128)S(1)}, f32[2,128,128]{2,1,0:T(8,128)S(1)}, u32[]{:S(2)}, u32[]{:S(2)}) collective-permute-start(f32[2,128,128]{2,1,0:T(8,128)S(1)} %get-tuple-element.13.guess_ref), channel_id=1, source_target_pairs={{1,0},{2,1},{3,2},{11,3},{10,11},{9,10},{8,9},{16,8},{17,16},{18,1... | collective-permute-start | bytes 393224 | tf_op jit(solution)/shard_map/ppermute | solution.py:328
  117.2 12.3 %collective-permute-start = (f32[2,128,128]{2,1,0:T(8,128)S(1)}, f32[2,128,128]{2,1,0:T(8,128)S(1)}, u32[]{:S(2)}, u32[]{:S(2)}) collective-permute-start(f32[2,128,128]{2,1,0:T(8,128)S(1)} %get-tuple-element.13.guess_ref), channel_id=1, source_target_pairs={{0,1},{1,2},{2,3},{3,11},{11,10},{10,9},{9,8},{8,16},{16,17},{17,1... | collective-permute-start | bytes 393224 | tf_op jit(solution)/shard_map/ppermute | solution.py:327
  125.9 7.0 %all-to-all-start.2 = ((bf16[4,2,128,4,8]{2,4,3,1,0:T(8,128)(2,1)}), bf16[4,2,128,4,8]{2,4,3,1,0:T(8,128)(2,1)S(1)}, u32[]{:S(2)}, u32[]{:S(2)}) async-start(bf16[4,2,128,4,8]{2,4,3,1,0:T(8,128)(2,1)} %copy.68), calls=%async_computation.2 | async-start | bytes 131072 | tf_op jit(solution)/shard_map/all_to_all | solution.py:334
  133.0 27.5 %copy-start.5 = (f32[2,4,8,128]{3,2,1,0:T(8,128)S(1)}, f32[2,4,8,128]{3,2,1,0:T(8,128)}, u32[]{:S(2)}) copy-start(f32[2,4,8,128]{3,2,1,0:T(8,128)} %param.15) | copy-start | bytes 98308
  133.0 27.5 %copy-start.6 = (f32[128,128,1,1]{1,0,3,2:T(8,128)S(1)}, f32[128,128,1,1]{1,0,3,2:T(8,128)}, u32[]{:S(2)}) copy-start(f32[128,128,1,1]{1,0,3,2:T(8,128)} %constant.82) | copy-start | bytes 196612

commit v6 on v5

--- a/solution.py
+++ b/solution.py
@@ -102,20 +102,18 @@
 
 
 def lane_block(ref, i):
-    n = ref.shape[1]
-    return ref[0, :, i * n : (i + 1) * n].astype(f32)
-
-
-def read_maps(maps_ref):
-    coils = maps_ref.shape[2] // maps_ref.shape[1] // 2
-    return [[lane_block(maps_ref, 2 * c + p) for p in range(2)] for c in range(coils)]
-
-
-def read_data(data_ref):
-    coils = data_ref.shape[2] // data_ref.shape[1] // 2
+    n = ref.shape[0] * ref.shape[1]
+    return ref[:, :, i * n : (i + 1) * n].astype(f32).reshape(n, n)
+
+
+def read_maps(block_ref, coils):
+    return [[lane_block(block_ref, 2 * c + p) for p in range(2)] for c in range(coils)]
+
+
+def read_data(block_ref, coils):
     return jnp.concatenate(
         [
-            jnp.concatenate([lane_block(data_ref, 2 * c + p) for c in range(coils)], 1)
+            jnp.concatenate([lane_block(block_ref, 2 * (coils + c) + p) for c in range(coils)], 1)
             for p in range(2)
         ],
         0,
@@ -123,16 +121,63 @@
 
 
 def masked(mask_ref, value):
-    coils = value.shape[1] // mask_ref.shape[3]
-    pieces = mask_ref.shape[0] // coils
-    mask = jnp.concatenate(
-        [
-            jnp.concatenate([mask_ref[c * pieces + i, 0].astype(f32) for i in range(pieces)], 0)
-            for c in range(coils)
-        ],
-        1,
-    )
+    n = mask_ref.shape[3]
+    coils = value.shape[1] // n
+    late = pl.program_id(0) >= pl.num_programs(0) // 2
+    left = position((n, n), 1) < n // 2
+    columns = []
+    for c in range(coils):
+        low, high = (mask_ref[2 * c + h, 0].astype(f32) for h in range(2))
+        low = jnp.where(late, pltpu.roll(low, n // 2, 1), low)
+        high = jnp.where(late, high, pltpu.roll(high, n // 2, 1))
+        columns.append(jnp.where(left, low, high))
+    mask = jnp.concatenate(columns, 1)
     return jnp.concatenate([mask, mask], 0) * value
+
+
+def pack_kernel(
+    maps_ref, data_ref, mask_ref, image_ref, near_ref, inv_ref, sort_ref, choose_ref, out_ref
+):
+    coils, _, planes, n, _ = maps_ref.shape
+    lines, rows = data_ref.shape[3], image_ref.shape[2]
+    kinds = near_ref.shape[1] // n
+    lanes = coils * 2 * n
+    pick = near_ref[:, :n]
+    sort = sort_ref[...]
+    group = sort.shape[0]
+    for t in range(planes):
+        planes_t = jnp.concatenate([maps_ref[c, p, t] for c in range(coils) for p in range(2)], 0)
+        out_ref[:, t, :lanes] = dot_t(pick, planes_t).astype(bf16)
+    for c in range(coils):
+        field = jnp.concatenate([data_ref[c, p].reshape(n * lines, n) for p in range(2)], 1)
+        sorted_rows = [
+            dot(sort, field[g * group : (g + 1) * group]).astype(bf16) for g in range(n * lines // group)
+        ]
+        part = group // lines
+        for t in range(lines):
+            line = jnp.concatenate([r[t * part : (t + 1) * part] for r in sorted_rows], 0)
+            turned = dot_t(inv_ref[...], line)
+            for p in range(2):
+                start = lanes + (2 * c + p) * n
+                out_ref[:, t, start : start + n] = turned[p * n : (p + 1) * n].astype(bf16)
+    shape = (n, n)
+    half = n // 2
+    mask = jnp.concatenate([mask_ref[c].astype(f32) for c in range(coils)], 1).astype(bf16)
+    chosen = dot_t(choose_ref[...], mask)
+    for t in range(planes):
+        value = jnp.concatenate([image_ref[p, t] for p in range(2)], 0)
+        high = value.astype(bf16).astype(f32)
+        parts = [high, value - high, high, high]
+        none = jnp.zeros_like(value)
+        spread = jnp.concatenate(
+            [jnp.concatenate([parts[k] if k == i else none for i in range(kinds)], 1) for k in range(kinds)], 0
+        )
+        spread = jnp.concatenate([spread, jnp.zeros_like(spread)], 0).astype(bf16)
+        image = dot_t(near_ref[...], spread)
+        line = chosen[t * n : (t + 1) * n]
+        odd = lax.rem(position(shape, 0), 2) == 1
+        line = jnp.where(odd, line, pltpu.roll(line, half, 1))
+        out_ref[:, t, 2 * lanes :] = jnp.where(position(shape, 1) < half, image, line).astype(bf16)
 
 
 def shifted(a, axis, step):
@@ -171,46 +216,51 @@
     return sums
 
 
-def read_start(edge_ref, start_ref):
-    here, before, after = [[start_ref[i, p].astype(f32) for p in range(2)] for i in range(3)]
-    return before, here, [jnp.where(edge_ref[1] > 0.0, a, h) for a, h in zip(after, here)]
-
-
 def first_kernel(
-    edge_ref, start_ref, maps_ref, data_ref, mask_ref, fz_ref, fy_ref, gy_ref, gz_ref,
+    edge_ref, start_ref, place_ref, block_ref, mask_ref, fz_ref, fy_ref, gy_ref, gz_ref,
     dual_ref, out_ref, change_ref, image_ref, sums_ref,
 ):
+    coils = dual_ref.shape[2] // start_ref.shape[2]
+
     @pl.when(pl.program_id(0) == 0)
     def _():
-        before, here, after = read_start(edge_ref, start_ref)
+        pieces = [start_ref[r, h] for r in range(start_ref.shape[0]) for h in range(start_ref.shape[1])]
+        planes = dot(jnp.concatenate(pieces, 1), place_ref[...])
+        n = planes.shape[0]
+        here, before, after = [
+            [planes[:, (2 * k + p) * n : (2 * k + p + 1) * n] for p in range(2)] for k in range(3)
+        ]
+        after = [jnp.where(edge_ref[1] > 0.0, a, h) for a, h in zip(after, here)]
         spread = divergence(shrink(here, after, None), shrink(before, here, None), edge_ref[0])
         for p in range(2):
-            image_ref[p] = here[p]
+            image_ref[0, p] = here[p]
+            image_ref[1, p] = before[p]
+            image_ref[2, p] = after[p]
             change_ref[p] = spread[p]
 
-    maps = read_maps(maps_ref)
-    spectrum = to_kspace(maps, image_ref, fz_ref[...], fy_ref[...])
-    dual = (dual_step * masked(mask_ref, spectrum - read_data(data_ref))) * (1.0 / (1.0 + dual_step))
+    maps = read_maps(block_ref, coils)
+    spectrum = to_kspace(maps, image_ref.at[0], fz_ref[...], fy_ref[...])
+    dual = (dual_step * masked(mask_ref, spectrum - read_data(block_ref, coils))) * (1.0 / (1.0 + dual_step))
     dual_ref[0] = dual
     accumulate(sums_ref, out_ref, to_image(dual.astype(bf16), maps, gy_ref[...], gz_ref[...]))
 
 
 def second_kernel(
-    guess_ref, dual_ref, maps_ref, data_ref, mask_ref, fz_ref, fy_ref, gy_ref, gz_ref, out_ref, sums_ref
+    guess_ref, dual_ref, block_ref, mask_ref, fz_ref, fy_ref, gy_ref, gz_ref, out_ref, sums_ref
 ):
-    maps = read_maps(maps_ref)
+    coils = dual_ref.shape[2] // guess_ref.shape[1]
+    maps = read_maps(block_ref, coils)
     spectrum = to_kspace(maps, guess_ref, fz_ref[...], fy_ref[...])
-    step = dual_step * masked(mask_ref, spectrum - read_data(data_ref))
+    step = dual_step * masked(mask_ref, spectrum - read_data(block_ref, coils))
     dual = (dual_ref[0] + step) * (1.0 / (1.0 + dual_step))
     accumulate(sums_ref, out_ref, to_image(dual.astype(bf16), maps, gy_ref[...], gz_ref[...]))
 
 
-def last_kernel(edge_ref, start_ref, change_ref, guess_ref, before_ref, after_ref, out_ref):
-    old_before, old_here, old_after = read_start(edge_ref, start_ref)
-    has_after = edge_ref[1]
+def last_kernel(edge_ref, image_ref, change_ref, guess_ref, before_ref, after_ref, out_ref):
+    old_here, old_before, old_after = [[image_ref[k, p] for p in range(2)] for k in range(3)]
     here = [guess_ref[p] for p in range(2)]
     before = [before_ref[p] for p in range(2)]
-    after = [jnp.where(has_after > 0.0, after_ref[p], here[p]) for p in range(2)]
+    after = [jnp.where(edge_ref[1] > 0.0, after_ref[p], here[p]) for p in range(2)]
     duals = shrink(here, after, shrink(old_here, old_after, None))
     duals_before = shrink(before, here, shrink(old_before, old_here, None))
     spread = divergence(duals, duals_before, edge_ref[0])
@@ -218,10 +268,10 @@
         out_ref[p] = change_ref[p] + spread[p]
 
 
-def step_block(a, dim):
+def step_block(a, dim, count, steps):
     return pl.BlockSpec(
-        tuple(1 if i == dim else n for i, n in enumerate(a.shape)),
-        lambda i: tuple(i if k == dim else 0 for k in range(a.ndim)),
+        tuple(n // count if i == dim else n for i, n in enumerate(a.shape)),
+        lambda i: tuple(lax.rem(i, count) if k == dim else 0 for k in range(a.ndim)),
     )
 
 
@@ -234,8 +284,8 @@
 
 def call(kernel, outs, stepped, *operands, steps, scratch=()):
     specs = [
-        whole_block(a) if dim is None else step_block(a, dim)
-        for a, dim in zip((*operands, *outs), stepped)
+        whole_block(a) if cut is None else step_block(a, *cut, steps)
+        for a, cut in zip((*operands, *outs), stepped)
     ]
     return pl.pallas_call(
         kernel,
@@ -266,75 +316,71 @@
         return lax.all_to_all(blocks, COLUMN, 0, 0, tiled=True)
 
     pick = np.eye(nx, dtype=np.float32)[column_of]
-    near = [pick, np.roll(pick, -1, 1), np.roll(pick, 1, 1)]
-    map_rows = jnp.einsum(
-        "wx,iryx->wriy", pick.astype(ml_dtypes.bfloat16), coil_maps.reshape(coils * 2, planes, ny, nx),
-        preferred_element_type=f32,
-    ).astype(bf16)
-    inv_x = table(nx, True)[:, column_of]
-    turned = jnp.einsum(
-        "ckzyw,jxkw->xycjz", kspace_data, inv_x, preferred_element_type=f32
-    ).astype(bf16)
-    image_rows = jnp.einsum(
-        "wx,kx->wk",
-        np.concatenate(near).astype(ml_dtypes.bfloat16),
-        initial_image.astype(bf16).reshape(-1, nx),
-        preferred_element_type=f32,
-    ).astype(bf16)
-    image_rows = jnp.concatenate([image_rows[i * nx : (i + 1) * nx] for i in range(3)], 1)
-    image_rows = jnp.pad(image_rows, ((0, 0), (0, -image_rows.shape[1] % nz))).reshape(nx, -1, nz)
-    mask_rows = sample_mask.transpose(0, 2, 1).astype(bf16).reshape(quarters, -1, nz)
-    mask_rows = jnp.broadcast_to(mask_rows[None], (count // quarters, *mask_rows.shape))
-    extra = jnp.concatenate([image_rows, mask_rows.reshape(nx, -1, nz)], 1)
+    near = np.concatenate([pick, pick, np.roll(pick, -1, 1), np.roll(pick, 1, 1)], 1)
+    inv_x = table(nx, True)[:, column_of].reshape(2 * nx, 2 * nx)
+    sort = np.eye(nx, dtype=np.float32).reshape(nx // lines, lines, nx).transpose(1, 0, 2).reshape(nx, nx)
+    quarter = np.arange(count) % quarters
+    choose = np.zeros((lines, count, coils, lines), np.float32)
+    for t in range(lines):
+        choose[t, np.arange(count), quarter // 2, t] = 1.0
     lanes = coils * 2 * ny
-    blocks = spread(
-        jnp.concatenate([map_rows.reshape(nx, planes, lanes), turned.reshape(nx, lines, lanes), extra], 2)
-    )
-    extra = blocks[:, :, 2 * lanes :]
-    pieces = quarters // coils
-
-    mask = extra[:, 2:].reshape(zq, -1, nz)
+    half = nz // 2
+    packed = jax.ShapeDtypeStruct((nx, planes, 2 * lanes + nz), bf16)
+    (blocks,) = call(
+        pack_kernel, (packed,), (None,) * 9, coil_maps, kspace_data, sample_mask, initial_image,
+        near.astype(bf16), inv_x, sort.astype(bf16), choose.reshape(lines * count, -1).astype(bf16), steps=1,
+    )
+    blocks = spread(blocks)
+    extra = blocks[:, :, 2 * lanes :].reshape(zq, nz, nz)
+
+    def pairs(part):
+        return jnp.concatenate([part[: zq // 2], part[zq // 2 :]], 2)
+
+    mask = pairs(extra[:, :, half:])
     mask = jnp.broadcast_to(mask[None], (quarters, *mask.shape))
     mask = lax.all_to_all(mask, COLUMN[3], 0, 0, tiled=True)
-
-    start = extra[:, :2].reshape(zq, slabs, -1)[:, :, : 3 * 2 * planes * rows]
-    start = start.reshape(zq, slabs, 3, 2, planes, rows).transpose(2, 3, 1, 4, 0, 5)
-    start = lax.all_gather(start.reshape(3, 2, nz, zq * rows), GROUP, axis=0)
-    start = start.reshape(group, 3, 2, nz, zq, rows).transpose(1, 2, 3, 4, 0, 5).reshape(3, 2, nz, ny)
-
-    maps = blocks[:, :, :lanes].reshape(zq, nz, lanes)
-    data = blocks[:, :, lanes : 2 * lanes].reshape(zq, slabs, pieces, -1, lanes)
-    data = data.transpose(0, 2, 1, 3, 4).reshape(zq, ny, lanes)
+    start = lax.all_gather(pairs(extra[:, :, :half]), GROUP, axis=0)
+
+    place = np.zeros((group, zq // 2, 2, 4, 2, rows, 3, 2, zq, group, rows), np.float32)
+    for r in range(group):
+        for a in range(zq):
+            for kind, plane in enumerate((0, 0, 1, 2)):
+                for p in range(2):
+                    for j in range(rows):
+                        place[r, a % (zq // 2), a // (zq // 2), kind, p, j, plane, p, a, r, j] = 1.0
+    place = place.reshape(group * zq // 2 * nz, 3 * 2 * ny).astype(bf16)
     edge = jnp.stack([1.0 - is_first.astype(f32), 1.0 - is_last.astype(f32)])
 
-    ky_order = np.arange(ny).reshape(slabs, pieces, -1).transpose(1, 0, 2).reshape(-1)
     fz, gz = (table(nz, inverse).reshape(2 * nz, 2 * nz) for inverse in (False, True))
-    fy = table(ny, False)[:, ky_order].reshape(2 * ny, 2 * ny)
-    gy = table(ny, True)[..., ky_order].reshape(2 * ny, 2 * ny)
+    fy, gy = (table(ny, inverse).reshape(2 * ny, 2 * ny) for inverse in (False, True))
     dual_like = jax.ShapeDtypeStruct((zq, 2 * ny, coils * nz), f32)
     grad_like = jax.ShapeDtypeStruct((2, nz, ny), bf16)
     image_like = jax.ShapeDtypeStruct((2, nz, ny), f32)
 
-    dual, grad, change, current = call(
-        first_kernel, (dual_like, grad_like, image_like, image_like),
-        (None, None, 0, 0, 1, None, None, None, None, 0, None, None, None),
-        edge, start, maps, data, mask, fz, fy, gy, gz, steps=zq, scratch=[image_like.shape],
+    images_like = jax.ShapeDtypeStruct((3, 2, nz, ny), f32)
+    whole, step, step_mask = None, (0, zq), (1, zq // 2)
+
+    dual, grad, change, images = call(
+        first_kernel, (dual_like, grad_like, image_like, images_like),
+        (whole, whole, whole, step, step_mask, whole, whole, whole, whole, step, whole, whole, whole),
+        edge, start, place, blocks, mask, fz, fy, gy, gz, steps=zq, scratch=[image_like.shape],
     )
     change = change + lax.all_gather(grad, GROUP, axis=0).astype(f32).sum(0)
-    guess = current - (2.0 * primal_step) * change
+    guess = images[0] - (2.0 * primal_step) * change
 
     forth = [(int(place_of[i]), int(place_of[i + 1])) for i in range(count - 1)]
     before = lax.ppermute(guess, COLUMN, forth)
     after = lax.ppermute(guess, COLUMN, [(b, a) for a, b in forth])
     (grad,) = call(
-        second_kernel, (grad_like,), (None, 0, 0, 0, 1, None, None, None, None, None),
-        guess, dual, maps, data, mask, fz, fy, gy, gz, steps=zq, scratch=[image_like.shape],
+        second_kernel, (grad_like,),
+        (whole, step, step, step_mask, whole, whole, whole, whole, whole),
+        guess, dual, blocks, mask, fz, fy, gy, gz, steps=zq, scratch=[image_like.shape],
     )
     grad = grad.reshape(2, nz, zq, group, rows).transpose(3, 0, 1, 2, 4)
     grad = lax.all_to_all(grad, GROUP, 0, 0, tiled=True).astype(f32).sum(0)
 
     (rest,) = call(
-        last_kernel, (image_like,), (None,) * 7, edge, start, change, guess, before, after, steps=1
+        last_kernel, (image_like,), (whole,) * 7, edge, images, change, guess, before, after, steps=1
     )
     rest = rest.reshape(2, nz, zq, group, rows)
     rest = lax.dynamic_index_in_dim(rest, lax.axis_index(GROUP), 3, keepdims=False)

time: 162 us -> 162 us (level)
  Pallas kernels: 9.02 us -> 13.5 us
  matrix products: 3.61 us -> 0.81 us
    unnamed x17 -> x29, local copies, waits for them, and re-layouts: 0.14 us -> 7.16 us
    pallas_call x3 -> x4, Pallas kernels: 9.02 us -> 13.5 us  [call(): pl.pallas_call(kernel, grid=(steps,), in_specs=specs[:len(operands)], out...]
    dot_general x3 -> x0, matrix products: 2.8 us -> none  [the longest x1 1.46 us: on_device(): jnp.einsum('ckzyw,jxkw->xycjz', kspace_data, inv_x, preferred_element_typ...]
    transpose x3 -> x0, local copies, waits for them, and re-layouts: 2.04 us -> none  [the longest x1 1.46 us: on_device(): start.reshape(zq, slabs, 3, 2, planes, rows).transpose(2, 3, 1, 4, 0, 5)]
    concatenate x1 -> x0, local copies, waits for them, and re-layouts: 2.02 us -> none  [on_device(): jnp.concatenate([map_rows.reshape(nx, planes, lanes), turned.reshape(nx,...]
    another operation x2 -> x0, local copies, waits for them, and re-layouts: 1.8 us -> none  [on_device(): start = lax.all_gather(start.reshape(3, 2, nz, zq * rows), GROUP, axis=0)]
  transfers between devices with their start and end apart: 5 -> 5, of which waited for: 2 -> 2; matrix products, arithmetic and copies ran while one was open for 4% -> 1% of each run, Pallas kernels for 3% -> 3%
where the time goes in v6:
time: 162 us
  waiting for transfers between devices  57.6 us (36%)
  blocking collectives  42.7 us (26%)
  starting transfers between devices  36.4 us (22%)
  Pallas kernels  13.5 us (8%)
  local copies, waits for them, and re-layouts  9.78 us (6%)
    all_to_all x1, waiting for transfers between devices, spread(): return lax.all_to_all(blocks, COLUMN, 0, 0, tiled=True)  55.7 us
    all_to_all x1, blocking collectives, spread(): return lax.all_to_all(blocks, COLUMN, 0, 0, tiled=True)  26.1 us
    all_to_all x1, starting transfers between devices, spread(): return lax.all_to_all(blocks, COLUMN, 0, 0, tiled=True)  23 us
    pallas_call x4, Pallas kernels, call(): pl.pallas_call(kernel, grid=(steps,), in_specs=specs[:len(operands)], out...  13.5 us
    all_gather x1, blocking collectives, on_device(): start = lax.all_gather(pairs(extra[:, :, :half]), GROUP, axis=0)  10.1 us
    unnamed x29, local copies, waits for them, and re-layouts  7.16 us
    all_gather x1, blocking collectives, on_device(): change = change + lax.all_gather(grad, GROUP, axis=0).astype(f32).sum(0)  6.58 us
    all_to_all x1, starting transfers between devices, on_device(): mask = lax.all_to_all(mask, COLUMN[3], 0, 0, tiled=True)  4.18 us
  transfers between devices with their start and end apart: 5, of which 2 were waited for; matrix products, arithmetic and copies ran while one was open for 1% of the time, Pallas kernels for 3%

profile of v6, /device:TPU:1, one launch (start us, length us, event | category | flops | bytes accessed | tf_op | source)
XLA Modules:
  0.0 161.6 jit_solution(3137154022324257150)
XLA Ops:
  0.0 0.8 copy.25.mask_ref
  0.8 0.0 copy-start.5
  0.8 1.0 copy-done.5
  1.9 0.0 copy-start.6
  1.9 1.0 copy-done.6
  2.9 0.0 copy-start.7
  2.9 0.8 copy-done.7
  3.7 0.0 copy-start.9
  3.7 0.9 copy-done.9
  4.6 0.0 copy-start.10
  4.6 0.9 copy-done.10
  5.5 0.0 copy-start.11
  5.5 0.9 copy-done.11
  6.4 0.0 copy-start.12
  6.4 0.8 copy-done.12
  7.1 3.7 %shard_map.136 = bf16[128,4,1152]{2,1,0:T(4,128)(2,1)} custom-call(bf16[2,2,4,128,128]{4,3,2,1,0:T(8,128)(2,1)S(1)} %copy-done.5, bf16[2,2,128,4,128]{4,3,2,1,0:T(4,128)(2,1)S(1)} %copy-done.6, s32[2,128,4]{2,1,0:T(8,128)S(1)} %copy.25.mask_ref, f32[2,4,8,128]{3,2,1,0:T(8,128)S(1)} %copy-done.7, bf16[128,512]{1,0:T(8,128)(2,1)S(1)} %copy-done.11, ...), custom_call_target="tpu_custom_call" | custom-call | tf_op jit(solution)/shard_map/pallas_call | solution.py:290
  10.8 23.0 %all-to-all-start = ((bf16[128,4,1152]{2,1,0:T(4,128)(2,1)}), bf16[128,4,1152]{2,1,0:T(4,128)(2,1)S(1)}, u32[]{:S(2)}, u32[]{:S(2)}) async-start(bf16[128,4,1152]{2,1,0:T(4,128)(2,1)} %shard_map.136), calls=%async_computation | async-start | bytes 2359296 | tf_op jit(solution)/shard_map/all_to_all | solution.py:316
  33.8 0.1 pad_maximum_fusion.2.edge_ref
  33.9 0.0 copy-start
  33.9 0.0 copy-start.1
  33.9 0.0 copy-start.2
  33.9 55.7 %all-to-all-done.block_ref = bf16[128,4,1152]{2,1,0:T(4,128)(2,1)S(1)} async-done(((bf16[128,4,1152]{2,1,0:T(4,128)(2,1)}), bf16[128,4,1152]{2,1,0:T(4,128)(2,1)S(1)}, u32[]{:S(2)}, u32[]{:S(2)}) %all-to-all-start) | async-done | bytes 1179680 | tf_op jit(solution)/shard_map/all_to_all | solution.py:316
  89.7 0.1 fusion.1
  89.8 0.1 pad_maximum_fusion.1
  89.9 0.7 broadcast_in_dim.2
  90.6 4.2 %all-to-all-start.1 = ((bf16[4,2,128,128]{3,2,1,0:T(8,128)(2,1)}), bf16[4,2,128,128]{3,2,1,0:T(8,128)(2,1)S(1)}, u32[]{:S(2)}, u32[]{:S(2)}) async-start(bf16[4,2,128,128]{3,2,1,0:T(8,128)(2,1)} %broadcast_in_dim.2), calls=%async_computation.1 | async-start | bytes 524288 | tf_op jit(solution)/shard_map/all_to_all | solution.py:341
  94.8 0.1 pad_maximum_fusion
  94.9 10.1 %all-gather = bf16[8,128,128]{2,1,0:T(8,128)(2,1)S(1)} all-gather(bf16[2,128,128]{2,1,0:T(8,128)(2,1)S(1)} %pad_maximum_fusion), channel_id=2, replica_groups=mesh['zq'=4,'zp'=2,'core'=2,'x'=4,'zhi'=2,'y'=4] {'zp','core'}, dimensions={0}, use_global_device_ids=true | all-gather | bytes 327680 | tf_op jit(solution)/shard_map/all_gather | solution.py:342
  105.0 0.0 all-to-all-done.1.mask_ref
  105.0 0.0 copy-done
  105.0 0.0 copy-done.1
  105.0 0.0 copy-done.2
  105.0 5.0 %shard_map.137 = (f32[4,256,256]{2,1,0:T(8,128)S(1)}, bf16[2,128,128]{2,1,0:T(8,128)(2,1)S(1)}, f32[2,128,128]{2,1,0:T(8,128)S(1)}, f32[3,2,128,128]{3,2,1,0:T(8,128)S(1)}) custom-call(f32[2]{0:T(128)S(1)} %pad_maximum_fusion.2.edge_ref, bf16[4,2,128,128]{3,2,1,0:T(8,128)(2,1)S(1)} %bitcast.27, bf16[1024,768]{1,0:T(8,128)(2,1)S(1)} %copy-done.2, ...), custom_call_target="tpu_custom_call" | custom-call | tf_op jit(solution)/shard_map/pallas_call | solution.py:290
  110.0 0.0 copy-start.3
  110.0 6.6 %all-gather.1 = bf16[8,128,128]{2,1,0:T(8,128)(2,1)S(1)} all-gather(bf16[2,128,128]{2,1,0:T(8,128)(2,1)S(1)} %get-tuple-element.11), channel_id=3, replica_groups=mesh['zq'=4,'zp'=2,'core'=2,'x'=4,'zhi'=2,'y'=4] {'zp','core'}, dimensions={0}, use_global_device_ids=true | all-gather | bytes 327680 | tf_op jit(solution)/shard_map/all_gather | solution.py:368
  116.6 0.0 copy-done.3
  116.7 1.3 collective-permute-start.1
  118.0 4.0 %collective-permute-start = (f32[2,128,128]{2,1,0:T(8,128)S(1)}, f32[2,128,128]{2,1,0:T(8,128)S(1)}, u32[]{:S(2)}, u32[]{:S(2)}) collective-permute-start(f32[2,128,128]{2,1,0:T(8,128)S(1)} %get-tuple-element.13.guess_ref), channel_id=1, source_target_pairs={{0,1},{1,2},{2,3},{3,11},{11,10},{10,9},{9,8},{8,16},{16,17},{17,1... | collective-permute-start | bytes 393224 | tf_op jit(solution)/shard_map/ppermute | solution.py:372
  122.0 0.0 copy-start.4
  122.0 3.8 %shard_map.139 = bf16[2,128,128]{2,1,0:T(8,128)(2,1)S(1)} custom-call(f32[2,128,128]{2,1,0:T(8,128)S(1)} %get-tuple-element.13.guess_ref, f32[4,256,256]{2,1,0:T(8,128)S(1)} %get-tuple-element.12.dual_ref, bf16[128,4,1152]{2,1,0:T(4,128)(2,1)S(1)} %all-to-all-done.block_ref, bf16[4,2,128,128]{3,2,1,0:T(8,128)(2,1)S(1)} %all-to-all-done.1.mask_ref, ...), custom_call_target="tpu_custom_call" | custom-call | tf_op jit(solution)/shard_map/pallas_call | solution.py:290
  125.8 0.1 copy.28
  125.9 0.6 copy.29
  126.6 4.0 %all-to-all-start.2 = ((bf16[4,2,128,4,8]{2,4,3,1,0:T(8,128)(2,1)}), bf16[4,2,128,4,8]{2,4,3,1,0:T(8,128)(2,1)S(1)}, u32[]{:S(2)}, u32[]{:S(2)}) async-start(bf16[4,2,128,4,8]{2,4,3,1,0:T(8,128)(2,1)} %copy.29), calls=%async_computation.2 | async-start | bytes 131072 | tf_op jit(solution)/shard_map/all_to_all | solution.py:380
  130.6 0.0 collective-permute-done.1.after_ref
  130.6 0.0 collective-permute-done.before_ref
  130.6 0.0 copy-done.4
  130.6 1.0 shard_map.138
  131.6 0.1 copy.26
  131.7 0.2 copy.27
  131.9 1.9 %all-to-all-done.2 = bf16[4,2,128,4,8]{2,4,3,1,0:T(8,128)(2,1)S(1)} async-done(((bf16[4,2,128,4,8]{2,4,3,1,0:T(8,128)(2,1)}), bf16[4,2,128,4,8]{2,4,3,1,0:T(8,128)(2,1)S(1)}, u32[]{:S(2)}, u32[]{:S(2)}) %all-to-all-start.2) | async-done | bytes 65568 | tf_op jit(solution)/shard_map/all_to_all | solution.py:380
  133.8 0.2 copy.31
  134.0 0.0 copy-start.8
  134.0 0.0 copy-start.13
  134.1 0.1 add_bitcast_fusion
  134.2 0.2 copy.32
  134.4 0.1 all_to_all.20
  134.5 0.1 copy.33
  134.6 26.1 %all_to_all.27 = f32[128,1,64]{2,1,0:T(1,128)S(1)} all-to-all(f32[128,1,64]{2,1,0:T(1,128)S(1)} %copy.33), channel_id=1, replica_groups=mesh['zq'=4,'zp'=2,'core'=2,'x'=4,'zhi'=2,'y'=4] {'zq','x','zhi','y'}, dimensions={0} | all-to-all | bytes 65536 | tf_op jit(solution)/shard_map/all_to_all | solution.py:316
  160.7 0.1 copy.34
  160.8 0.0 copy-done.8
  160.8 0.0 copy-done.13
  160.8 0.8 fusion
  (5 shorter events, 0.1 us)
Async XLA Ops:
  0.8 1.0 copy-start.5
  1.9 1.0 copy-start.6
  2.9 0.8 copy-start.7
  3.7 0.9 copy-start.9
  4.6 0.9 copy-start.10
  5.5 0.9 copy-start.11
  6.4 0.8 copy-start.12
  10.8 78.8 %all-to-all-start = ((bf16[128,4,1152]{2,1,0:T(4,128)(2,1)}), bf16[128,4,1152]{2,1,0:T(4,128)(2,1)S(1)}, u32[]{:S(2)}, u32[]{:S(2)}) async-start(bf16[128,4,1152]{2,1,0:T(4,128)(2,1)} %shard_map.136), calls=%async_computation | async-start | bytes 2359296 | tf_op jit(solution)/shard_map/all_to_all | solution.py:316
  33.9 71.1 %copy-start = (bf16[256,256]{1,0:T(8,128)(2,1)S(1)}, bf16[256,256]{1,0:T(8,128)(2,1)}, u32[]{:S(2)}) copy-start(bf16[256,256]{1,0:T(8,128)(2,1)} %constant.70.clone.gy_ref.gz_ref) | copy-start | bytes 393220
  33.9 71.1 %copy-start.1 = (bf16[256,256]{1,0:T(8,128)(2,1)S(1)}, bf16[256,256]{1,0:T(8,128)(2,1)}, u32[]{:S(2)}) copy-start(bf16[256,256]{1,0:T(8,128)(2,1)} %constant.69.clone.fz_ref.fy_ref) | copy-start | bytes 393220
  33.9 71.1 %copy-start.2 = (bf16[1024,768]{1,0:T(8,128)(2,1)S(1)}, bf16[1024,768]{1,0:T(8,128)(2,1)}, u32[]{:S(2)}) copy-start(bf16[1024,768]{1,0:T(8,128)(2,1)} %constant.68.clone.place_ref) | copy-start | bytes 4718596
  90.6 14.4 %all-to-all-start.1 = ((bf16[4,2,128,128]{3,2,1,0:T(8,128)(2,1)}), bf16[4,2,128,128]{3,2,1,0:T(8,128)(2,1)S(1)}, u32[]{:S(2)}, u32[]{:S(2)}) async-start(bf16[4,2,128,128]{3,2,1,0:T(8,128)(2,1)} %broadcast_in_dim.2), calls=%async_computation.1 | async-start | bytes 524288 | tf_op jit(solution)/shard_map/all_to_all | solution.py:341
  110.0 6.7 %copy-start.3 = (f32[3,2,128,128]{3,2,1,0:T(8,128)}, f32[3,2,128,128]{3,2,1,0:T(8,128)S(1)}, u32[]{:S(2)}) copy-start(f32[3,2,128,128]{3,2,1,0:T(8,128)S(1)} %get-tuple-element.9.image_ref) | copy-start | bytes 1179652
  116.7 13.9 %collective-permute-start.1 = (f32[2,128,128]{2,1,0:T(8,128)S(1)}, f32[2,128,128]{2,1,0:T(8,128)S(1)}, u32[]{:S(2)}, u32[]{:S(2)}) collective-permute-start(f32[2,128,128]{2,1,0:T(8,128)S(1)} %get-tuple-element.13.guess_ref), channel_id=1, source_target_pairs={{1,0},{2,1},{3,2},{11,3},{10,11},{9,10},{8,9},{16,8},{17,16},{18,1... | collective-permute-start | bytes 393224 | tf_op jit(solution)/shard_map/ppermute | solution.py:373
  118.0 12.6 %collective-permute-start = (f32[2,128,128]{2,1,0:T(8,128)S(1)}, f32[2,128,128]{2,1,0:T(8,128)S(1)}, u32[]{:S(2)}, u32[]{:S(2)}) collective-permute-start(f32[2,128,128]{2,1,0:T(8,128)S(1)} %get-tuple-element.13.guess_ref), channel_id=1, source_target_pairs={{0,1},{1,2},{2,3},{3,11},{11,10},{10,9},{9,8},{8,16},{16,17},{17,1... | collective-permute-start | bytes 393224 | tf_op jit(solution)/shard_map/ppermute | solution.py:372
  122.0 8.6 %copy-start.4 = (f32[3,2,128,128]{3,2,1,0:T(8,128)S(1)}, f32[3,2,128,128]{3,2,1,0:T(8,128)}, u32[]{:S(2)}) copy-start(f32[3,2,128,128]{3,2,1,0:T(8,128)} %copy-done.3) | copy-start | bytes 1179652
  126.6 7.2 %all-to-all-start.2 = ((bf16[4,2,128,4,8]{2,4,3,1,0:T(8,128)(2,1)}), bf16[4,2,128,4,8]{2,4,3,1,0:T(8,128)(2,1)S(1)}, u32[]{:S(2)}, u32[]{:S(2)}) async-start(bf16[4,2,128,4,8]{2,4,3,1,0:T(8,128)(2,1)} %copy.29), calls=%async_computation.2 | async-start | bytes 131072 | tf_op jit(solution)/shard_map/all_to_all | solution.py:380
  134.0 26.7 %copy-start.8 = (f32[2,4,8,128]{3,2,1,0:T(8,128)S(1)}, f32[2,4,8,128]{3,2,1,0:T(8,128)}, u32[]{:S(2)}) copy-start(f32[2,4,8,128]{3,2,1,0:T(8,128)} %image_ref.1) | copy-start | bytes 98308
  134.0 26.7 %copy-start.13 = (f32[128,128,1,1]{1,0,3,2:T(8,128)S(1)}, f32[128,128,1,1]{1,0,3,2:T(8,128)}, u32[]{:S(2)}) copy-start(f32[128,128,1,1]{1,0,3,2:T(8,128)} %constant.76) | copy-start | bytes 196612

commit v7 on v6

--- a/solution.py
+++ b/solution.py
@@ -86,85 +86,65 @@
     return real_sum, imag_sum
 
 
-def accumulate(sums_ref, out_ref, parts):
-    step = pl.program_id(0)
-
-    @pl.when(step == 0)
-    def _():
-        sums_ref[...] = jnp.zeros_like(sums_ref)
-
-    sums_ref[0] += parts[0]
-    sums_ref[1] += parts[1]
-
-    @pl.when(step == pl.num_programs(0) - 1)
-    def _():
-        out_ref[...] = sums_ref[...].astype(out_ref.dtype)
-
-
-def lane_block(ref, i):
-    n = ref.shape[0] * ref.shape[1]
-    return ref[:, :, i * n : (i + 1) * n].astype(f32).reshape(n, n)
-
-
-def read_maps(block_ref, coils):
-    return [[lane_block(block_ref, 2 * c + p) for p in range(2)] for c in range(coils)]
-
-
-def read_data(block_ref, coils):
+def lane_block(block_ref, a, i):
+    n = block_ref.shape[0]
+    slabs = n // block_ref.shape[1]
+    return block_ref[a * slabs : (a + 1) * slabs, :, i * n : (i + 1) * n].astype(f32).reshape(n, n)
+
+
+def read_maps(block_ref, a, coils):
+    return [[lane_block(block_ref, a, 2 * c + p) for p in range(2)] for c in range(coils)]
+
+
+def read_data(block_ref, a, coils):
     return jnp.concatenate(
         [
-            jnp.concatenate([lane_block(block_ref, 2 * (coils + c) + p) for c in range(coils)], 1)
+            jnp.concatenate([lane_block(block_ref, a, 2 * (coils + c) + p) for c in range(coils)], 1)
             for p in range(2)
         ],
         0,
     )
 
 
-def masked(mask_ref, value):
+def masked(mask_ref, a, coils, value):
     n = mask_ref.shape[3]
-    coils = value.shape[1] // n
-    late = pl.program_id(0) >= pl.num_programs(0) // 2
+    late, pair = divmod(a, mask_ref.shape[1])
     left = position((n, n), 1) < n // 2
     columns = []
     for c in range(coils):
-        low, high = (mask_ref[2 * c + h, 0].astype(f32) for h in range(2))
-        low = jnp.where(late, pltpu.roll(low, n // 2, 1), low)
-        high = jnp.where(late, high, pltpu.roll(high, n // 2, 1))
-        columns.append(jnp.where(left, low, high))
+        halves = [mask_ref[2 * c + h, pair].astype(f32) for h in range(2)]
+        halves[1 - late] = pltpu.roll(halves[1 - late], n // 2, 1)
+        columns.append(jnp.where(left, halves[0], halves[1]))
     mask = jnp.concatenate(columns, 1)
     return jnp.concatenate([mask, mask], 0) * value
 
 
-def pack_kernel(
-    maps_ref, data_ref, mask_ref, image_ref, near_ref, inv_ref, sort_ref, choose_ref, out_ref
-):
+def pack_kernel(maps_ref, data_ref, mask_ref, image_ref, near_ref, inv_ref, sort_ref, choose_ref, out_ref):
     coils, _, planes, n, _ = maps_ref.shape
     lines, rows = data_ref.shape[3], image_ref.shape[2]
     kinds = near_ref.shape[1] // n
-    lanes = coils * 2 * n
     pick = near_ref[:, :n]
-    sort = sort_ref[...]
-    group = sort.shape[0]
+    sort, mix = sort_ref[0], sort_ref[1]
+    part = n // lines
+    half = n // 2
+    shape = (n, n)
+
+    field = [jnp.concatenate([data_ref[c, p].reshape(n * lines, n) for p in range(2)], 1) for c in range(coils)]
+    field = jnp.concatenate(field, 1)
+    field = [dot(sort, field[g * n : (g + 1) * n]).astype(bf16) for g in range(lines)]
+    mask = jnp.concatenate([mask_ref[c] for c in range(coils)], 0).astype(f32).astype(bf16)
+    odd = lax.rem(position(shape, 0), 2) == 1
+
+    packed = []
     for t in range(planes):
         planes_t = jnp.concatenate([maps_ref[c, p, t] for c in range(coils) for p in range(2)], 0)
-        out_ref[:, t, :lanes] = dot_t(pick, planes_t).astype(bf16)
-    for c in range(coils):
-        field = jnp.concatenate([data_ref[c, p].reshape(n * lines, n) for p in range(2)], 1)
-        sorted_rows = [
-            dot(sort, field[g * group : (g + 1) * group]).astype(bf16) for g in range(n * lines // group)
+        pieces = [dot_t(pick, planes_t)]
+        line = jnp.concatenate([f[t * part : (t + 1) * part] for f in field], 0)
+        line = jnp.concatenate([line[:, c * 2 * n : (c + 1) * 2 * n] for c in range(coils)], 0)
+        turned = dot_t(inv_ref[...], line)
+        pieces += [
+            turned[p * n : (p + 1) * n, c * n : (c + 1) * n] for c in range(coils) for p in range(2)
         ]
-        part = group // lines
-        for t in range(lines):
-            line = jnp.concatenate([r[t * part : (t + 1) * part] for r in sorted_rows], 0)
-            turned = dot_t(inv_ref[...], line)
-            for p in range(2):
-                start = lanes + (2 * c + p) * n
-                out_ref[:, t, start : start + n] = turned[p * n : (p + 1) * n].astype(bf16)
-    shape = (n, n)
-    half = n // 2
-    mask = jnp.concatenate([mask_ref[c].astype(f32) for c in range(coils)], 1).astype(bf16)
-    chosen = dot_t(choose_ref[...], mask)
-    for t in range(planes):
         value = jnp.concatenate([image_ref[p, t] for p in range(2)], 0)
         high = value.astype(bf16).astype(f32)
         parts = [high, value - high, high, high]
@@ -172,12 +152,15 @@
         spread = jnp.concatenate(
             [jnp.concatenate([parts[k] if k == i else none for i in range(kinds)], 1) for k in range(kinds)], 0
         )
-        spread = jnp.concatenate([spread, jnp.zeros_like(spread)], 0).astype(bf16)
-        image = dot_t(near_ref[...], spread)
-        line = chosen[t * n : (t + 1) * n]
-        odd = lax.rem(position(shape, 0), 2) == 1
-        line = jnp.where(odd, line, pltpu.roll(line, half, 1))
-        out_ref[:, t, 2 * lanes :] = jnp.where(position(shape, 1) < half, image, line).astype(bf16)
+        image = dot_t(near_ref[...], jnp.concatenate([spread, jnp.zeros_like(spread)], 0).astype(bf16))
+        chosen = dot(choose_ref[t * n : (t + 1) * n], mask)
+        chosen = jnp.where(odd, chosen, pltpu.roll(chosen, half, 1))
+        pieces.append(jnp.where(position(shape, 1) < half, image, chosen))
+        packed.append(jnp.concatenate(pieces, 1).astype(bf16))
+    for g in range(lines):
+        together = jnp.concatenate([v[g * part : (g + 1) * part] for v in packed], 0)
+        mixed = dot(mix, together).astype(bf16)
+        out_ref[g * part : (g + 1) * part] = mixed.reshape(part, planes, mixed.shape[1])
 
 
 def shifted(a, axis, step):
@@ -218,42 +201,47 @@
 
 def first_kernel(
     edge_ref, start_ref, place_ref, block_ref, mask_ref, fz_ref, fy_ref, gy_ref, gz_ref,
-    dual_ref, out_ref, change_ref, image_ref, sums_ref,
+    dual_ref, out_ref, change_ref, image_ref,
 ):
+    pairs = dual_ref.shape[0]
     coils = dual_ref.shape[2] // start_ref.shape[2]
-
-    @pl.when(pl.program_id(0) == 0)
-    def _():
-        pieces = [start_ref[r, h] for r in range(start_ref.shape[0]) for h in range(start_ref.shape[1])]
-        planes = dot(jnp.concatenate(pieces, 1), place_ref[...])
-        n = planes.shape[0]
-        here, before, after = [
-            [planes[:, (2 * k + p) * n : (2 * k + p + 1) * n] for p in range(2)] for k in range(3)
-        ]
-        after = [jnp.where(edge_ref[1] > 0.0, a, h) for a, h in zip(after, here)]
-        spread = divergence(shrink(here, after, None), shrink(before, here, None), edge_ref[0])
-        for p in range(2):
-            image_ref[0, p] = here[p]
-            image_ref[1, p] = before[p]
-            image_ref[2, p] = after[p]
-            change_ref[p] = spread[p]
-
-    maps = read_maps(block_ref, coils)
-    spectrum = to_kspace(maps, image_ref.at[0], fz_ref[...], fy_ref[...])
-    dual = (dual_step * masked(mask_ref, spectrum - read_data(block_ref, coils))) * (1.0 / (1.0 + dual_step))
-    dual_ref[0] = dual
-    accumulate(sums_ref, out_ref, to_image(dual.astype(bf16), maps, gy_ref[...], gz_ref[...]))
-
-
-def second_kernel(
-    guess_ref, dual_ref, block_ref, mask_ref, fz_ref, fy_ref, gy_ref, gz_ref, out_ref, sums_ref
-):
+    pieces = [start_ref[r, h] for r in range(start_ref.shape[0]) for h in range(start_ref.shape[1])]
+    planes = dot(jnp.concatenate(pieces, 1), place_ref[...])
+    n = planes.shape[0]
+    here, before, after = [
+        [planes[:, (2 * k + p) * n : (2 * k + p + 1) * n] for p in range(2)] for k in range(3)
+    ]
+    after = [jnp.where(edge_ref[1] > 0.0, a, h) for a, h in zip(after, here)]
+    sums = [0.0, 0.0]
+    for a in range(pairs):
+        maps = read_maps(block_ref, a, coils)
+        spectrum = to_kspace(maps, here, fz_ref[...], fy_ref[...])
+        dual = dual_step * masked(mask_ref, a, coils, spectrum - read_data(block_ref, a, coils))
+        dual = dual * (1.0 / (1.0 + dual_step))
+        dual_ref[a] = dual
+        sums = [s + t for s, t in zip(sums, to_image(dual.astype(bf16), maps, gy_ref[...], gz_ref[...]))]
+    spread = divergence(shrink(here, after, None), shrink(before, here, None), edge_ref[0])
+    for p in range(2):
+        out_ref[p] = sums[p].astype(bf16)
+        image_ref[0, p] = here[p]
+        image_ref[1, p] = before[p]
+        image_ref[2, p] = after[p]
+        change_ref[p] = spread[p]
+
+
+def second_kernel(guess_ref, dual_ref, block_ref, mask_ref, fz_ref, fy_ref, gy_ref, gz_ref, out_ref):
+    pairs = dual_ref.shape[0]
     coils = dual_ref.shape[2] // guess_ref.shape[1]
-    maps = read_maps(block_ref, coils)
-    spectrum = to_kspace(maps, guess_ref, fz_ref[...], fy_ref[...])
-    step = dual_step * masked(mask_ref, spectrum - read_data(block_ref, coils))
-    dual = (dual_ref[0] + step) * (1.0 / (1.0 + dual_step))
-    accumulate(sums_ref, out_ref, to_image(dual.astype(bf16), maps, gy_ref[...], gz_ref[...]))
+    guess = [guess_ref[p] for p in range(2)]
+    sums = [0.0, 0.0]
+    for a in range(pairs):
+        maps = read_maps(block_ref, a, coils)
+        spectrum = to_kspace(maps, guess, fz_ref[...], fy_ref[...])
+        step = dual_step * masked(mask_ref, a, coils, spectrum - read_data(block_ref, a, coils))
+        dual = (dual_ref[a] + step) * (1.0 / (1.0 + dual_step))
+        sums = [s + t for s, t in zip(sums, to_image(dual.astype(bf16), maps, gy_ref[...], gz_ref[...]))]
+    for p in range(2):
+        out_ref[p] = sums[p].astype(bf16)
 
 
 def last_kernel(edge_ref, image_ref, change_ref, guess_ref, before_ref, after_ref, out_ref):
@@ -268,33 +256,16 @@
         out_ref[p] = change_ref[p] + spread[p]
 
 
-def step_block(a, dim, count, steps):
-    return pl.BlockSpec(
-        tuple(n // count if i == dim else n for i, n in enumerate(a.shape)),
-        lambda i: tuple(lax.rem(i, count) if k == dim else 0 for k in range(a.ndim)),
-    )
-
-
-def whole_block(a):
-    if a.ndim == 1:
-        return pl.BlockSpec(memory_space=pltpu.SMEM)
-    zeros = (0,) * a.ndim
-    return pl.BlockSpec(a.shape, lambda i: zeros)
-
-
-def call(kernel, outs, stepped, *operands, steps, scratch=()):
-    specs = [
-        whole_block(a) if cut is None else step_block(a, *cut, steps)
-        for a, cut in zip((*operands, *outs), stepped)
-    ]
+def call(kernel, outs, *operands, vmem=40):
+    def place(a):
+        return pl.BlockSpec(memory_space=pltpu.SMEM if a.ndim == 1 else pltpu.VMEM)
+
     return pl.pallas_call(
         kernel,
-        grid=(steps,),
-        in_specs=specs[: len(operands)],
-        out_specs=specs[len(operands) :],
+        in_specs=[place(a) for a in operands],
+        out_specs=[place(a) for a in outs],
         out_shape=outs,
-        scratch_shapes=[pltpu.VMEM(shape, f32) for shape in scratch],
-        compiler_params=pltpu.CompilerParams(vmem_limit_bytes=40 * 1024 * 1024),
+        compiler_params=pltpu.CompilerParams(vmem_limit_bytes=vmem * 1024 * 1024),
     )(*operands)
 
 
@@ -327,8 +298,9 @@
     half = nz // 2
     packed = jax.ShapeDtypeStruct((nx, planes, 2 * lanes + nz), bf16)
     (blocks,) = call(
-        pack_kernel, (packed,), (None,) * 9, coil_maps, kspace_data, sample_mask, initial_image,
-        near.astype(bf16), inv_x, sort.astype(bf16), choose.reshape(lines * count, -1).astype(bf16), steps=1,
+        pack_kernel, (packed,), coil_maps, kspace_data, sample_mask.transpose(0, 2, 1), initial_image,
+        near.astype(bf16), inv_x, np.stack([sort, sort.T]).astype(bf16),
+        choose.reshape(lines * count, -1).astype(bf16), vmem=60,
     )
     blocks = spread(blocks)
     extra = blocks[:, :, 2 * lanes :].reshape(zq, nz, nz)
@@ -358,12 +330,9 @@
     image_like = jax.ShapeDtypeStruct((2, nz, ny), f32)
 
     images_like = jax.ShapeDtypeStruct((3, 2, nz, ny), f32)
-    whole, step, step_mask = None, (0, zq), (1, zq // 2)
-
     dual, grad, change, images = call(
         first_kernel, (dual_like, grad_like, image_like, images_like),
-        (whole, whole, whole, step, step_mask, whole, whole, whole, whole, step, whole, whole, whole),
-        edge, start, place, blocks, mask, fz, fy, gy, gz, steps=zq, scratch=[image_like.shape],
+        edge, start, place, blocks, mask, fz, fy, gy, gz,
     )
     change = change + lax.all_gather(grad, GROUP, axis=0).astype(f32).sum(0)
     guess = images[0] - (2.0 * primal_step) * change
@@ -371,17 +340,11 @@
     forth = [(int(place_of[i]), int(place_of[i + 1])) for i in range(count - 1)]
     before = lax.ppermute(guess, COLUMN, forth)
     after = lax.ppermute(guess, COLUMN, [(b, a) for a, b in forth])
-    (grad,) = call(
-        second_kernel, (grad_like,),
-        (whole, step, step, step_mask, whole, whole, whole, whole, whole),
-        guess, dual, blocks, mask, fz, fy, gy, gz, steps=zq, scratch=[image_like.shape],
-    )
+    (grad,) = call(second_kernel, (grad_like,), guess, dual, blocks, mask, fz, fy, gy, gz)
     grad = grad.reshape(2, nz, zq, group, rows).transpose(3, 0, 1, 2, 4)
     grad = lax.all_to_all(grad, GROUP, 0, 0, tiled=True).astype(f32).sum(0)
 
-    (rest,) = call(
-        last_kernel, (image_like,), (whole,) * 7, edge, images, change, guess, before, after, steps=1
-    )
+    (rest,) = call(last_kernel, (image_like,), edge, images, change, guess, before, after)
     rest = rest.reshape(2, nz, zq, group, rows)
     rest = lax.dynamic_index_in_dim(rest, lax.axis_index(GROUP), 3, keepdims=False)
     result = rest + grad

time: 162 us -> 152 us (0.938)
  local copies, waits for them, and re-layouts: 9.78 us -> 2.69 us
  Pallas kernels: 13.5 us -> 10.6 us
    unnamed x29 -> x14, local copies, waits for them, and re-layouts: 7.16 us -> 0.04 us
    pallas_call x4, Pallas kernels: 13.5 us -> 10.6 us  [call(): pl.pallas_call(kernel, in_specs=[place(a) for a in operands], out_specs=[...]
  transfers between devices with their start and end apart: 5 -> 5, of which waited for: 2 -> 2; matrix products, arithmetic and copies ran while one was open for 1% -> 1% of each run, Pallas kernels for 3% -> 2%
where the time goes in v7:
time: 152 us
  waiting for transfers between devices  57.6 us (38%)
  blocking collectives  42.8 us (28%)
  starting transfers between devices  36.4 us (24%)
  Pallas kernels  10.6 us (7%)
  local copies, waits for them, and re-layouts  2.69 us (2%)
    all_to_all x1, waiting for transfers between devices, spread(): return lax.all_to_all(blocks, COLUMN, 0, 0, tiled=True)  55.7 us
    all_to_all x1, blocking collectives, spread(): return lax.all_to_all(blocks, COLUMN, 0, 0, tiled=True)  26.1 us
    all_to_all x1, starting transfers between devices, spread(): return lax.all_to_all(blocks, COLUMN, 0, 0, tiled=True)  23 us
    pallas_call x4, Pallas kernels, call(): pl.pallas_call(kernel, in_specs=[place(a) for a in operands], out_specs=[...  10.6 us
    all_gather x1, blocking collectives, on_device(): start = lax.all_gather(pairs(extra[:, :, :half]), GROUP, axis=0)  10.1 us
    all_gather x1, blocking collectives, on_device(): change = change + lax.all_gather(grad, GROUP, axis=0).astype(f32).sum(0)  6.57 us
    all_to_all x1, starting transfers between devices, on_device(): mask = lax.all_to_all(mask, COLUMN[3], 0, 0, tiled=True)  4.19 us
    ppermute x1, starting transfers between devices, on_device(): before = lax.ppermute(guess, COLUMN, forth)  3.99 us
  transfers between devices with their start and end apart: 5, of which 2 were waited for; matrix products, arithmetic and copies ran while one was open for 1% of the time, Pallas kernels for 2%

profile of v7, /device:TPU:1, one launch (start us, length us, event | category | flops | bytes accessed | tf_op | source)
XLA Modules:
  0.0 151.6 jit_solution(7154118332719036184)
XLA Ops:
  0.0 3.7 %shard_map.136 = bf16[128,4,1152]{2,1,0:T(4,128)(2,1)} custom-call(bf16[2,2,4,128,128]{4,3,2,1,0:T(8,128)(2,1)} %maps_ref.1, bf16[2,2,128,4,128]{4,3,2,1,0:T(4,128)(2,1)} %data_ref.1, s32[2,4,128]{2,1,0:T(4,128)} %bitcast.37, f32[2,4,8,128]{3,2,1,0:T(8,128)} %image_ref.1, bf16[128,512]{1,0:T(8,128)(2,1)} %constant.64.clone.near_ref, ...), custom_call_target="tpu_custom_call" | custom-call | tf_op jit(solution)/shard_map/pallas_call | solution.py:263
  3.7 23.0 %all-to-all-start = ((bf16[128,4,1152]{2,1,0:T(4,128)(2,1)}), bf16[128,4,1152]{2,1,0:T(4,128)(2,1)S(1)}, u32[]{:S(2)}, u32[]{:S(2)}) async-start(bf16[128,4,1152]{2,1,0:T(4,128)(2,1)} %shard_map.136), calls=%async_computation | async-start | bytes 2359296 | tf_op jit(solution)/shard_map/all_to_all | solution.py:287
  26.7 0.1 pad_maximum_fusion.2.edge_ref
  26.8 0.0 copy-start
  26.8 0.0 copy-start.1
  26.8 0.0 copy-start.2
  26.8 55.7 %all-to-all-done.block_ref = bf16[128,4,1152]{2,1,0:T(4,128)(2,1)S(1)} async-done(((bf16[128,4,1152]{2,1,0:T(4,128)(2,1)}), bf16[128,4,1152]{2,1,0:T(4,128)(2,1)S(1)}, u32[]{:S(2)}, u32[]{:S(2)}) %all-to-all-start) | async-done | bytes 1179680 | tf_op jit(solution)/shard_map/all_to_all | solution.py:287
  82.6 0.1 fusion.1
  82.7 0.1 pad_maximum_fusion.1
  82.8 0.7 broadcast_in_dim.2
  83.5 4.2 %all-to-all-start.1 = ((bf16[4,2,128,128]{3,2,1,0:T(8,128)(2,1)}), bf16[4,2,128,128]{3,2,1,0:T(8,128)(2,1)S(1)}, u32[]{:S(2)}, u32[]{:S(2)}) async-start(bf16[4,2,128,128]{3,2,1,0:T(8,128)(2,1)} %broadcast_in_dim.2), calls=%async_computation.1 | async-start | bytes 524288 | tf_op jit(solution)/shard_map/all_to_all | solution.py:313
  87.7 0.1 pad_maximum_fusion
  87.8 10.1 %all-gather = bf16[8,128,128]{2,1,0:T(8,128)(2,1)S(1)} all-gather(bf16[2,128,128]{2,1,0:T(8,128)(2,1)S(1)} %pad_maximum_fusion), channel_id=2, replica_groups=mesh['zq'=4,'zp'=2,'core'=2,'x'=4,'zhi'=2,'y'=4] {'zp','core'}, dimensions={0}, use_global_device_ids=true | all-gather | bytes 327680 | tf_op jit(solution)/shard_map/all_gather | solution.py:314
  97.9 0.0 all-to-all-done.1.mask_ref
  97.9 0.0 copy-done
  97.9 0.0 copy-done.1
  97.9 0.0 copy-done.2
  97.9 3.3 %shard_map.137 = (f32[4,256,256]{2,1,0:T(8,128)S(1)}, bf16[2,128,128]{2,1,0:T(8,128)(2,1)S(1)}, f32[2,128,128]{2,1,0:T(8,128)S(1)}, f32[3,2,128,128]{3,2,1,0:T(8,128)S(1)}) custom-call(f32[2]{0:T(128)S(1)} %pad_maximum_fusion.2.edge_ref, bf16[4,2,128,128]{3,2,1,0:T(8,128)(2,1)S(1)} %bitcast.28, bf16[1024,768]{1,0:T(8,128)(2,1)S(1)} %copy-done.2, ...), custom_call_target="tpu_custom_call" | custom-call | tf_op jit(solution)/shard_map/pallas_call | solution.py:263
  101.3 0.0 copy-start.3
  101.3 6.6 %all-gather.1 = bf16[8,128,128]{2,1,0:T(8,128)(2,1)S(1)} all-gather(bf16[2,128,128]{2,1,0:T(8,128)(2,1)S(1)} %get-tuple-element.11), channel_id=3, replica_groups=mesh['zq'=4,'zp'=2,'core'=2,'x'=4,'zhi'=2,'y'=4] {'zp','core'}, dimensions={0}, use_global_device_ids=true | all-gather | bytes 327680 | tf_op jit(solution)/shard_map/all_gather | solution.py:337
  107.9 0.0 copy-done.3
  108.0 1.3 collective-permute-start.1
  109.3 4.0 %collective-permute-start = (f32[2,128,128]{2,1,0:T(8,128)S(1)}, f32[2,128,128]{2,1,0:T(8,128)S(1)}, u32[]{:S(2)}, u32[]{:S(2)}) collective-permute-start(f32[2,128,128]{2,1,0:T(8,128)S(1)} %get-tuple-element.13.guess_ref), channel_id=1, source_target_pairs={{0,1},{1,2},{2,3},{3,11},{11,10},{10,9},{9,8},{8,16},{16,17},{17,1... | collective-permute-start | bytes 393224 | tf_op jit(solution)/shard_map/ppermute | solution.py:341
  113.3 0.0 copy-start.4
  113.3 2.5 %shard_map.139 = bf16[2,128,128]{2,1,0:T(8,128)(2,1)S(1)} custom-call(f32[2,128,128]{2,1,0:T(8,128)S(1)} %get-tuple-element.13.guess_ref, f32[4,256,256]{2,1,0:T(8,128)S(1)} %get-tuple-element.12.dual_ref, bf16[128,4,1152]{2,1,0:T(4,128)(2,1)S(1)} %all-to-all-done.block_ref, bf16[4,2,128,128]{3,2,1,0:T(8,128)(2,1)S(1)} %all-to-all-done.1.mask_ref, ...), custom_call_target="tpu_custom_call" | custom-call | tf_op jit(solution)/shard_map/pallas_call | solution.py:263
  115.8 0.1 copy.24
  115.9 0.6 copy.25
  116.6 4.0 %all-to-all-start.2 = ((bf16[4,2,128,4,8]{2,4,3,1,0:T(8,128)(2,1)}), bf16[4,2,128,4,8]{2,4,3,1,0:T(8,128)(2,1)S(1)}, u32[]{:S(2)}, u32[]{:S(2)}) async-start(bf16[4,2,128,4,8]{2,4,3,1,0:T(8,128)(2,1)} %copy.25), calls=%async_computation.2 | async-start | bytes 131072 | tf_op jit(solution)/shard_map/all_to_all | solution.py:345
  120.5 0.0 collective-permute-done.1.after_ref
  120.5 0.0 collective-permute-done.before_ref
  120.5 0.0 copy-done.4
  120.5 1.0 shard_map.138
  121.6 0.1 copy.22
  121.7 0.2 copy.23
  121.9 1.9 %all-to-all-done.2 = bf16[4,2,128,4,8]{2,4,3,1,0:T(8,128)(2,1)S(1)} async-done(((bf16[4,2,128,4,8]{2,4,3,1,0:T(8,128)(2,1)}), bf16[4,2,128,4,8]{2,4,3,1,0:T(8,128)(2,1)S(1)}, u32[]{:S(2)}, u32[]{:S(2)}) %all-to-all-start.2) | async-done | bytes 65568 | tf_op jit(solution)/shard_map/all_to_all | solution.py:345
  123.8 0.2 copy.27
  124.0 0.0 copy-start.5
  124.0 0.0 copy-start.6
  124.0 0.1 add_bitcast_fusion
  124.2 0.2 copy.28
  124.4 0.1 all_to_all.20
  124.5 0.1 copy.29
  124.6 26.1 %all_to_all.27 = f32[128,1,64]{2,1,0:T(1,128)S(1)} all-to-all(f32[128,1,64]{2,1,0:T(1,128)S(1)} %copy.29), channel_id=1, replica_groups=mesh['zq'=4,'zp'=2,'core'=2,'x'=4,'zhi'=2,'y'=4] {'zq','x','zhi','y'}, dimensions={0} | all-to-all | bytes 65536 | tf_op jit(solution)/shard_map/all_to_all | solution.py:287
  150.7 0.1 copy.30
  150.8 0.0 copy-done.5
  150.8 0.0 copy-done.6
  150.8 0.8 fusion
  (5 shorter events, 0.1 us)
Async XLA Ops:
  3.7 78.8 %all-to-all-start = ((bf16[128,4,1152]{2,1,0:T(4,128)(2,1)}), bf16[128,4,1152]{2,1,0:T(4,128)(2,1)S(1)}, u32[]{:S(2)}, u32[]{:S(2)}) async-start(bf16[128,4,1152]{2,1,0:T(4,128)(2,1)} %shard_map.136), calls=%async_computation | async-start | bytes 2359296 | tf_op jit(solution)/shard_map/all_to_all | solution.py:287
  26.8 71.1 %copy-start = (bf16[256,256]{1,0:T(8,128)(2,1)S(1)}, bf16[256,256]{1,0:T(8,128)(2,1)}, u32[]{:S(2)}) copy-start(bf16[256,256]{1,0:T(8,128)(2,1)} %constant.70.clone.gy_ref.gz_ref) | copy-start | bytes 393220
  26.8 71.1 %copy-start.1 = (bf16[256,256]{1,0:T(8,128)(2,1)S(1)}, bf16[256,256]{1,0:T(8,128)(2,1)}, u32[]{:S(2)}) copy-start(bf16[256,256]{1,0:T(8,128)(2,1)} %constant.69.clone.fz_ref.fy_ref) | copy-start | bytes 393220
  26.8 71.1 %copy-start.2 = (bf16[1024,768]{1,0:T(8,128)(2,1)S(1)}, bf16[1024,768]{1,0:T(8,128)(2,1)}, u32[]{:S(2)}) copy-start(bf16[1024,768]{1,0:T(8,128)(2,1)} %constant.68.clone.place_ref) | copy-start | bytes 4718596
  83.5 14.4 %all-to-all-start.1 = ((bf16[4,2,128,128]{3,2,1,0:T(8,128)(2,1)}), bf16[4,2,128,128]{3,2,1,0:T(8,128)(2,1)S(1)}, u32[]{:S(2)}, u32[]{:S(2)}) async-start(bf16[4,2,128,128]{3,2,1,0:T(8,128)(2,1)} %broadcast_in_dim.2), calls=%async_computation.1 | async-start | bytes 524288 | tf_op jit(solution)/shard_map/all_to_all | solution.py:313
  101.3 6.7 %copy-start.3 = (f32[3,2,128,128]{3,2,1,0:T(8,128)}, f32[3,2,128,128]{3,2,1,0:T(8,128)S(1)}, u32[]{:S(2)}) copy-start(f32[3,2,128,128]{3,2,1,0:T(8,128)S(1)} %get-tuple-element.9.image_ref) | copy-start | bytes 1179652
  108.0 12.6 %collective-permute-start.1 = (f32[2,128,128]{2,1,0:T(8,128)S(1)}, f32[2,128,128]{2,1,0:T(8,128)S(1)}, u32[]{:S(2)}, u32[]{:S(2)}) collective-permute-start(f32[2,128,128]{2,1,0:T(8,128)S(1)} %get-tuple-element.13.guess_ref), channel_id=1, source_target_pairs={{1,0},{2,1},{3,2},{11,3},{10,11},{9,10},{8,9},{16,8},{17,16},{18,1... | collective-permute-start | bytes 393224 | tf_op jit(solution)/shard_map/ppermute | solution.py:342
  109.3 11.3 %collective-permute-start = (f32[2,128,128]{2,1,0:T(8,128)S(1)}, f32[2,128,128]{2,1,0:T(8,128)S(1)}, u32[]{:S(2)}, u32[]{:S(2)}) collective-permute-start(f32[2,128,128]{2,1,0:T(8,128)S(1)} %get-tuple-element.13.guess_ref), channel_id=1, source_target_pairs={{0,1},{1,2},{2,3},{3,11},{11,10},{10,9},{9,8},{8,16},{16,17},{17,1... | collective-permute-start | bytes 393224 | tf_op jit(solution)/shard_map/ppermute | solution.py:341
  113.3 7.3 %copy-start.4 = (f32[3,2,128,128]{3,2,1,0:T(8,128)S(1)}, f32[3,2,128,128]{3,2,1,0:T(8,128)}, u32[]{:S(2)}) copy-start(f32[3,2,128,128]{3,2,1,0:T(8,128)} %copy-done.3) | copy-start | bytes 1179652
  116.6 7.2 %all-to-all-start.2 = ((bf16[4,2,128,4,8]{2,4,3,1,0:T(8,128)(2,1)}), bf16[4,2,128,4,8]{2,4,3,1,0:T(8,128)(2,1)S(1)}, u32[]{:S(2)}, u32[]{:S(2)}) async-start(bf16[4,2,128,4,8]{2,4,3,1,0:T(8,128)(2,1)} %copy.25), calls=%async_computation.2 | async-start | bytes 131072 | tf_op jit(solution)/shard_map/all_to_all | solution.py:345
  124.0 26.8 %copy-start.5 = (f32[2,4,8,128]{3,2,1,0:T(8,128)S(1)}, f32[2,4,8,128]{3,2,1,0:T(8,128)}, u32[]{:S(2)}) copy-start(f32[2,4,8,128]{3,2,1,0:T(8,128)} %image_ref.1) | copy-start | bytes 98308
  124.0 26.8 %copy-start.6 = (f32[128,128,1,1]{1,0,3,2:T(8,128)S(1)}, f32[128,128,1,1]{1,0,3,2:T(8,128)}, u32[]{:S(2)}) copy-start(f32[128,128,1,1]{1,0,3,2:T(8,128)} %constant.76) | copy-start | bytes 196612

commit v8 on v7

--- a/solution.py
+++ b/solution.py
@@ -189,13 +189,12 @@
     return [[m * factor for m in part] for part in moved]
 
 
-def divergence(duals, duals_before, has_before):
+def divergence(duals):
     sums = []
-    for p in range(2):
-        d_z, d_y, d_x = duals[p]
+    for d_z, d_y, d_x in duals:
         back_z = jnp.where(position(d_z.shape, 0) > 0, shifted(d_z, 0, -1), 0.0)
         back_y = jnp.where(position(d_y.shape, 1) > 0, shifted(d_y, 1, -1), 0.0)
-        sums.append((back_z - d_z) + (back_y - d_y) + (has_before * duals_before[p][2] - d_x))
+        sums.append((back_z - d_z) + (back_y - d_y) - d_x)
     return sums
 
 
@@ -220,19 +219,27 @@
         dual = dual * (1.0 / (1.0 + dual_step))
         dual_ref[a] = dual
         sums = [s + t for s, t in zip(sums, to_image(dual.astype(bf16), maps, gy_ref[...], gz_ref[...]))]
-    spread = divergence(shrink(here, after, None), shrink(before, here, None), edge_ref[0])
+    spread = divergence(shrink(here, after, None))
+    duals_before = shrink(before, here, None)
     for p in range(2):
         out_ref[p] = sums[p].astype(bf16)
         image_ref[0, p] = here[p]
         image_ref[1, p] = before[p]
-        image_ref[2, p] = after[p]
-        change_ref[p] = spread[p]
-
-
-def second_kernel(guess_ref, dual_ref, block_ref, mask_ref, fz_ref, fy_ref, gy_ref, gz_ref, out_ref):
+        change_ref[p] = spread[p] + edge_ref[0] * duals_before[p][2]
+
+
+def second_kernel(
+    parts_ref, spread_ref, image_ref, dual_ref, block_ref, mask_ref, fz_ref, fy_ref, gy_ref, gz_ref,
+    out_ref, change_ref, guess_ref,
+):
     pairs = dual_ref.shape[0]
-    coils = dual_ref.shape[2] // guess_ref.shape[1]
-    guess = [guess_ref[p] for p in range(2)]
+    coils = dual_ref.shape[2] // parts_ref.shape[2]
+    guess = []
+    for p in range(2):
+        change = spread_ref[p] + sum(parts_ref[r, p].astype(f32) for r in range(parts_ref.shape[0]))
+        guess.append(image_ref[0, p] - (2.0 * primal_step) * change)
+        change_ref[p] = change
+        guess_ref[p] = guess[p]
     sums = [0.0, 0.0]
     for a in range(pairs):
         maps = read_maps(block_ref, a, coils)
@@ -244,16 +251,16 @@
         out_ref[p] = sums[p].astype(bf16)
 
 
-def last_kernel(edge_ref, image_ref, change_ref, guess_ref, before_ref, after_ref, out_ref):
-    old_here, old_before, old_after = [[image_ref[k, p] for p in range(2)] for k in range(3)]
+def last_kernel(edge_ref, image_ref, change_ref, guess_ref, before_ref, out_ref):
+    old_here, old_before = [[image_ref[k, p] for p in range(2)] for k in range(2)]
     here = [guess_ref[p] for p in range(2)]
     before = [before_ref[p] for p in range(2)]
-    after = [jnp.where(edge_ref[1] > 0.0, after_ref[p], here[p]) for p in range(2)]
-    duals = shrink(here, after, shrink(old_here, old_after, None))
-    duals_before = shrink(before, here, shrink(old_before, old_here, None))
-    spread = divergence(duals, duals_before, edge_ref[0])
-    for p in range(2):
-        out_ref[p] = change_ref[p] + spread[p]
+    duals = shrink(before, here, shrink(old_before, old_here, None))
+    spread = divergence(duals)
+    last = divergence(shrink(here, here, shrink(old_here, old_here, None)))
+    for p in range(2):
+        out_ref[0, p] = change_ref[p] + edge_ref[0] * duals[p][2] + (1.0 - edge_ref[1]) * last[p]
+        out_ref[1, p] = spread[p]
 
 
 def call(kernel, outs, *operands, vmem=40):
@@ -329,29 +336,31 @@
     grad_like = jax.ShapeDtypeStruct((2, nz, ny), bf16)
     image_like = jax.ShapeDtypeStruct((2, nz, ny), f32)
 
-    images_like = jax.ShapeDtypeStruct((3, 2, nz, ny), f32)
-    dual, grad, change, images = call(
+    images_like = jax.ShapeDtypeStruct((2, 2, nz, ny), f32)
+    dual, grad, spread_sum, images = call(
         first_kernel, (dual_like, grad_like, image_like, images_like),
         edge, start, place, blocks, mask, fz, fy, gy, gz,
     )
-    change = change + lax.all_gather(grad, GROUP, axis=0).astype(f32).sum(0)
-    guess = images[0] - (2.0 * primal_step) * change
-
+    parts = lax.all_gather(grad, GROUP, axis=0)
+    grad, change, guess = call(
+        second_kernel, (grad_like, image_like, image_like),
+        parts, spread_sum, images, dual, blocks, mask, fz, fy, gy, gz,
+    )
     forth = [(int(place_of[i]), int(place_of[i + 1])) for i in range(count - 1)]
     before = lax.ppermute(guess, COLUMN, forth)
-    after = lax.ppermute(guess, COLUMN, [(b, a) for a, b in forth])
-    (grad,) = call(second_kernel, (grad_like,), guess, dual, blocks, mask, fz, fy, gy, gz)
     grad = grad.reshape(2, nz, zq, group, rows).transpose(3, 0, 1, 2, 4)
     grad = lax.all_to_all(grad, GROUP, 0, 0, tiled=True).astype(f32).sum(0)
 
-    (rest,) = call(last_kernel, (image_like,), edge, images, change, guess, before, after)
-    rest = rest.reshape(2, nz, zq, group, rows)
-    rest = lax.dynamic_index_in_dim(rest, lax.axis_index(GROUP), 3, keepdims=False)
-    result = rest + grad
-    result = result.reshape(2, slabs, planes, zq, rows).transpose(3, 1, 0, 2, 4)
-    result = spread(result.reshape(count, 2 * planes * rows))
+    (rest,) = call(last_kernel, (images_like,), edge, images, change, guess, before)
+    rest = rest.reshape(2, 2, nz, zq, group, rows)
+    rest = lax.dynamic_index_in_dim(rest, lax.axis_index(GROUP), 4, keepdims=False)
+    result = jnp.concatenate([rest[:1] + grad[None], rest[1:]], 0)
+    result = result.reshape(2, 2, slabs, planes, zq, rows).transpose(4, 2, 0, 1, 3, 5)
+    result = spread(result.reshape(count, 2, 2 * planes * rows))
+    targets = np.stack([pick, np.concatenate([pick[:, 1:], np.zeros_like(pick[:, :1])], 1)], 1)
     result = lax.dot_general(
-        result, pick, (((0,), (0,)), ((), ())), precision=lax.Precision.HIGHEST, preferred_element_type=f32
+        result.reshape(2 * count, -1), targets.reshape(2 * count, nx), (((0,), (0,)), ((), ())),
+        precision=lax.Precision.HIGHEST, preferred_element_type=f32,
     )
     return initial_image - primal_step * result.reshape(2, planes, rows, nx)
 

time: 152 us -> 153 us (level)
  local copies, waits for them, and re-layouts: 2.69 us -> 4.95 us
  starting transfers between devices: 36.4 us -> 34.2 us
  transfers between devices with their start and end apart: 5 -> 4, of which waited for: 2 -> 2; matrix products, arithmetic and copies ran while one was open for 1% -> 1% of each run, Pallas kernels for 2% -> 1%
where the time goes in v8:
time: 153 us; the launch traced here: 152 us
  waiting for transfers between devices  57.1 us (37%)
  blocking collectives  42.6 us (28%)
  starting transfers between devices  34.2 us (22%)
  Pallas kernels  10.9 us (7%)
  local copies, waits for them, and re-layouts  4.95 us (3%)
    all_to_all x1, waiting for transfers between devices, spread(): return lax.all_to_all(blocks, COLUMN, 0, 0, tiled=True)  55.7 us
    all_to_all x1, blocking collectives, spread(): return lax.all_to_all(blocks, COLUMN, 0, 0, tiled=True)  26 us
    all_to_all x1, starting transfers between devices, spread(): return lax.all_to_all(blocks, COLUMN, 0, 0, tiled=True)  23 us
    pallas_call x4, Pallas kernels, call(): pl.pallas_call(kernel, in_specs=[place(a) for a in operands], out_specs=[...  10.9 us
    all_gather x1, blocking collectives, on_device(): start = lax.all_gather(pairs(extra[:, :, :half]), GROUP, axis=0)  10.6 us
    all_gather x1, blocking collectives, on_device(): parts = lax.all_gather(grad, GROUP, axis=0)  6.12 us
    all_to_all x1, starting transfers between devices, on_device(): mask = lax.all_to_all(mask, COLUMN[3], 0, 0, tiled=True)  4.19 us
    all_to_all x1, starting transfers between devices, on_device(): grad = lax.all_to_all(grad, GROUP, 0, 0, tiled=True).astype(f32).sum(0)  3.69 us
  transfers between devices with their start and end apart: 4, of which 2 were waited for; matrix products, arithmetic and copies ran while one was open for 1% of the time, Pallas kernels for 1%

profile of v8, /device:TPU:1, one launch (start us, length us, event | category | flops | bytes accessed | tf_op | source)
XLA Modules:
  0.0 152.1 jit_solution(4815052349153563939)
XLA Ops:
  0.0 3.7 %shard_map.136 = bf16[128,4,1152]{2,1,0:T(4,128)(2,1)} custom-call(bf16[2,2,4,128,128]{4,3,2,1,0:T(8,128)(2,1)} %maps_ref.1, bf16[2,2,128,4,128]{4,3,2,1,0:T(4,128)(2,1)} %data_ref.1, s32[2,4,128]{2,1,0:T(4,128)} %bitcast.36, f32[2,4,8,128]{3,2,1,0:T(8,128)} %image_ref.1, bf16[128,512]{1,0:T(8,128)(2,1)} %constant.62.clone.near_ref, ...), custom_call_target="tpu_custom_call" | custom-call | tf_op jit(solution)/shard_map/pallas_call | solution.py:270
  3.7 23.0 %all-to-all-start = ((bf16[128,4,1152]{2,1,0:T(4,128)(2,1)}), bf16[128,4,1152]{2,1,0:T(4,128)(2,1)S(1)}, u32[]{:S(2)}, u32[]{:S(2)}) async-start(bf16[128,4,1152]{2,1,0:T(4,128)(2,1)} %shard_map.136), calls=%async_computation | async-start | bytes 2359296 | tf_op jit(solution)/shard_map/all_to_all | solution.py:294
  26.7 0.1 pad_maximum_fusion.2.edge_ref
  26.8 0.0 copy-start
  26.8 0.0 copy-start.1
  26.8 0.0 copy-start.2
  26.8 55.7 %all-to-all-done.block_ref = bf16[128,4,1152]{2,1,0:T(4,128)(2,1)S(1)} async-done(((bf16[128,4,1152]{2,1,0:T(4,128)(2,1)}), bf16[128,4,1152]{2,1,0:T(4,128)(2,1)S(1)}, u32[]{:S(2)}, u32[]{:S(2)}) %all-to-all-start) | async-done | bytes 1179680 | tf_op jit(solution)/shard_map/all_to_all | solution.py:294
  82.6 0.1 fusion.1
  82.7 0.1 pad_maximum_fusion.1
  82.8 0.7 broadcast_in_dim.2
  83.5 4.2 %all-to-all-start.1 = ((bf16[4,2,128,128]{3,2,1,0:T(8,128)(2,1)}), bf16[4,2,128,128]{3,2,1,0:T(8,128)(2,1)S(1)}, u32[]{:S(2)}, u32[]{:S(2)}) async-start(bf16[4,2,128,128]{3,2,1,0:T(8,128)(2,1)} %broadcast_in_dim.2), calls=%async_computation.1 | async-start | bytes 524288 | tf_op jit(solution)/shard_map/all_to_all | solution.py:320
  87.7 0.1 pad_maximum_fusion
  87.8 10.6 %all-gather = bf16[8,128,128]{2,1,0:T(8,128)(2,1)} all-gather(bf16[2,128,128]{2,1,0:T(8,128)(2,1)S(1)} %pad_maximum_fusion), channel_id=2, replica_groups=mesh['zq'=4,'zp'=2,'core'=2,'x'=4,'zhi'=2,'y'=4] {'zp','core'}, dimensions={0}, use_global_device_ids=true | all-gather | bytes 327680 | tf_op jit(solution)/shard_map/all_gather | solution.py:321
  98.4 0.0 all-to-all-done.1.mask_ref
  98.4 0.0 copy-done
  98.4 0.0 copy-done.1
  98.4 0.0 copy-done.2
  98.4 0.0 copy-start.3
  98.4 0.9 copy-done.3
  99.3 3.4 %shard_map.137 = (f32[4,256,256]{2,1,0:T(8,128)S(1)}, bf16[2,128,128]{2,1,0:T(8,128)(2,1)S(1)}, f32[2,128,128]{2,1,0:T(8,128)S(1)}, f32[2,2,128,128]{3,2,1,0:T(8,128)S(1)}) custom-call(f32[2]{0:T(128)S(1)} %pad_maximum_fusion.2.edge_ref, bf16[4,2,128,128]{3,2,1,0:T(8,128)(2,1)S(1)} %bitcast.27, bf16[1024,768]{1,0:T(8,128)(2,1)S(1)} %copy-done.2, ...), custom_call_target="tpu_custom_call" | custom-call | tf_op jit(solution)/shard_map/pallas_call | solution.py:270
  102.8 6.1 %all-gather.1 = bf16[8,128,128]{2,1,0:T(8,128)(2,1)S(1)} all-gather(bf16[2,128,128]{2,1,0:T(8,128)(2,1)S(1)} %get-tuple-element.13), channel_id=3, replica_groups=mesh['zq'=4,'zp'=2,'core'=2,'x'=4,'zhi'=2,'y'=4] {'zp','core'}, dimensions={0}, use_global_device_ids=true | all-gather | bytes 327680 | tf_op jit(solution)/shard_map/all_gather | solution.py:344
  108.9 2.6 %shard_map.138 = (bf16[2,128,128]{2,1,0:T(8,128)(2,1)S(1)}, f32[2,128,128]{2,1,0:T(8,128)S(1)}, f32[2,128,128]{2,1,0:T(8,128)S(1)}) custom-call(bf16[4,2,128,128]{3,2,1,0:T(8,128)(2,1)S(1)} %bitcast.26, f32[2,128,128]{2,1,0:T(8,128)S(1)} %get-tuple-element.14.spread_ref, f32[2,2,128,128]{3,2,1,0:T(8,128)S(1)} %get-tuple-element.12.image_ref, ...), custom_call_target="tpu_custom_call" | custom-call | tf_op jit(solution)/shard_map/pallas_call | solution.py:270
  111.5 3.4 %collective-permute-start = (f32[2,128,128]{2,1,0:T(8,128)S(1)}, f32[2,128,128]{2,1,0:T(8,128)S(1)}, u32[]{:S(2)}, u32[]{:S(2)}) collective-permute-start(f32[2,128,128]{2,1,0:T(8,128)S(1)} %get-tuple-element.17.guess_ref), channel_id=1, source_target_pairs={{0,1},{1,2},{2,3},{3,11},{11,10},{10,9},{9,8},{8,16},{16,17},{17,1... | collective-permute-start | bytes 393224 | tf_op jit(solution)/shard_map/ppermute | solution.py:350
  114.9 0.1 copy.30
  115.0 0.6 copy.31
  115.7 3.7 %all-to-all-start.2 = ((bf16[4,2,128,4,8]{2,4,3,1,0:T(8,128)(2,1)}), bf16[4,2,128,4,8]{2,4,3,1,0:T(8,128)(2,1)S(1)}, u32[]{:S(2)}, u32[]{:S(2)}) async-start(bf16[4,2,128,4,8]{2,4,3,1,0:T(8,128)(2,1)} %copy.31), calls=%async_computation.2 | async-start | bytes 131072 | tf_op jit(solution)/shard_map/all_to_all | solution.py:352
  119.4 0.0 collective-permute-done.before_ref
  119.4 1.1 shard_map.139
  120.5 0.1 copy.28
  120.7 0.2 copy.29
  120.9 0.2 copy.34
  121.1 0.2 copy.36
  121.3 1.4 all-to-all-done.2
  122.7 0.2 copy.33
  122.9 0.1 add.33
  123.0 0.2 copy.35
  123.2 0.0 copy-start.4
  123.2 0.0 copy-start.5
  123.2 0.1 copy.37
  123.3 0.2 reshape.48
  123.5 0.1 copy.38
  123.6 0.1 reshape.53
  123.8 26.0 %all_to_all.20 = f32[128,1,128]{2,1,0:T(1,128)S(1)} all-to-all(f32[128,1,128]{2,1,0:T(1,128)S(1)} %reshape.53), channel_id=1, replica_groups=mesh['zq'=4,'zp'=2,'core'=2,'x'=4,'zhi'=2,'y'=4] {'zq','x','zhi','y'}, dimensions={0} | all-to-all | bytes 131072 | tf_op jit(solution)/shard_map/all_to_all | solution.py:294
  149.7 0.5 broadcast.1
  150.2 0.8 reduce
  151.0 0.1 reshape.54
  151.2 0.1 copy.39
  151.3 0.0 copy-done.4
  151.3 0.0 copy-done.5
  151.3 0.8 fusion
  (4 shorter events, 0.1 us)
Async XLA Ops:
  3.7 78.8 %all-to-all-start = ((bf16[128,4,1152]{2,1,0:T(4,128)(2,1)}), bf16[128,4,1152]{2,1,0:T(4,128)(2,1)S(1)}, u32[]{:S(2)}, u32[]{:S(2)}) async-start(bf16[128,4,1152]{2,1,0:T(4,128)(2,1)} %shard_map.136), calls=%async_computation | async-start | bytes 2359296 | tf_op jit(solution)/shard_map/all_to_all | solution.py:294
  26.8 71.6 %copy-start = (bf16[256,256]{1,0:T(8,128)(2,1)S(1)}, bf16[256,256]{1,0:T(8,128)(2,1)}, u32[]{:S(2)}) copy-start(bf16[256,256]{1,0:T(8,128)(2,1)} %constant.67.clone.fz_ref.fy_ref) | copy-start | bytes 393220
  26.8 71.6 %copy-start.1 = (bf16[256,256]{1,0:T(8,128)(2,1)S(1)}, bf16[256,256]{1,0:T(8,128)(2,1)}, u32[]{:S(2)}) copy-start(bf16[256,256]{1,0:T(8,128)(2,1)} %constant.68.clone.gy_ref.gz_ref) | copy-start | bytes 393220
  26.8 71.6 %copy-start.2 = (bf16[1024,768]{1,0:T(8,128)(2,1)S(1)}, bf16[1024,768]{1,0:T(8,128)(2,1)}, u32[]{:S(2)}) copy-start(bf16[1024,768]{1,0:T(8,128)(2,1)} %constant.66.clone.place_ref) | copy-start | bytes 4718596
  83.5 14.8 %all-to-all-start.1 = ((bf16[4,2,128,128]{3,2,1,0:T(8,128)(2,1)}), bf16[4,2,128,128]{3,2,1,0:T(8,128)(2,1)S(1)}, u32[]{:S(2)}, u32[]{:S(2)}) async-start(bf16[4,2,128,128]{3,2,1,0:T(8,128)(2,1)} %broadcast_in_dim.2), calls=%async_computation.1 | async-start | bytes 524288 | tf_op jit(solution)/shard_map/all_to_all | solution.py:320
  98.4 1.0 copy-start.3
  111.5 7.9 %collective-permute-start = (f32[2,128,128]{2,1,0:T(8,128)S(1)}, f32[2,128,128]{2,1,0:T(8,128)S(1)}, u32[]{:S(2)}, u32[]{:S(2)}) collective-permute-start(f32[2,128,128]{2,1,0:T(8,128)S(1)} %get-tuple-element.17.guess_ref), channel_id=1, source_target_pairs={{0,1},{1,2},{2,3},{3,11},{11,10},{10,9},{9,8},{8,16},{16,17},{17,1... | collective-permute-start | bytes 393224 | tf_op jit(solution)/shard_map/ppermute | solution.py:350
  115.7 7.0 %all-to-all-start.2 = ((bf16[4,2,128,4,8]{2,4,3,1,0:T(8,128)(2,1)}), bf16[4,2,128,4,8]{2,4,3,1,0:T(8,128)(2,1)S(1)}, u32[]{:S(2)}, u32[]{:S(2)}) async-start(bf16[4,2,128,4,8]{2,4,3,1,0:T(8,128)(2,1)} %copy.31), calls=%async_computation.2 | async-start | bytes 131072 | tf_op jit(solution)/shard_map/all_to_all | solution.py:352
  123.2 28.1 %copy-start.4 = (f32[2,4,8,128]{3,2,1,0:T(8,128)S(1)}, f32[2,4,8,128]{3,2,1,0:T(8,128)}, u32[]{:S(2)}) copy-start(f32[2,4,8,128]{3,2,1,0:T(8,128)} %image_ref.1) | copy-start | bytes 98308
  123.2 28.1 %copy-start.5 = (f32[256,128,1,1]{1,0,3,2:T(8,128)S(1)}, f32[256,128,1,1]{1,0,3,2:T(8,128)}, u32[]{:S(2)}) copy-start(f32[256,128,1,1]{1,0,3,2:T(8,128)} %constant.74) | copy-start | bytes 393220

commit v9 on v8

--- a/solution.py
+++ b/solution.py
@@ -251,19 +251,50 @@
         out_ref[p] = sums[p].astype(bf16)
 
 
-def last_kernel(edge_ref, image_ref, change_ref, guess_ref, before_ref, out_ref):
+def last_kernel(edge_ref, place_ref, image_ref, change_ref, guess_ref, before_ref, parts_ref, out_ref, plane_ref):
     old_here, old_before = [[image_ref[k, p] for p in range(2)] for k in range(2)]
     here = [guess_ref[p] for p in range(2)]
     before = [before_ref[p] for p in range(2)]
     duals = shrink(before, here, shrink(old_before, old_here, None))
     spread = divergence(duals)
     last = divergence(shrink(here, here, shrink(old_here, old_here, None)))
+    group = parts_ref.shape[0]
+    n = here[0].shape[1]
+    rows = n // group // group
+    back = lax.rem(n - rows * place_ref[0], n)
     for p in range(2):
-        out_ref[0, p] = change_ref[p] + edge_ref[0] * duals[p][2] + (1.0 - edge_ref[1]) * last[p]
-        out_ref[1, p] = spread[p]
-
-
-def call(kernel, outs, *operands, vmem=40):
+        own = change_ref[p] + sum(parts_ref[r, p].astype(f32) for r in range(group))
+        own = own + edge_ref[0] * duals[p][2] + (1.0 - edge_ref[1]) * last[p]
+        plane_ref[p] = pltpu.roll(own, back, 1)
+        plane_ref[2 + p] = pltpu.roll(spread[p], back, 1)
+    slabs = out_ref.shape[0] // group
+    planes = n // slabs
+    lane = position((slabs, n), 1)
+    packed = [jnp.zeros((slabs, n), f32) for _ in range(group)]
+    for k in range(4):
+        for z in range(planes):
+            value = plane_ref[k, pl.ds(z, slabs, stride=planes), :]
+            target = (k * planes + z) * rows
+            chosen = (lane >= target) & (lane < target + rows)
+            for a in range(group):
+                moved = pltpu.roll(value, (target - a * group * rows) % n, 1)
+                packed[a] = jnp.where(chosen, moved, packed[a])
+    for a in range(group):
+        out_ref[a * slabs : (a + 1) * slabs] = packed[a]
+
+
+def result_kernel(packed_ref, target_ref, image_ref, out_ref):
+    n = packed_ref.shape[0]
+    half = n // 2
+    value = packed_ref[...].T
+    high = value.astype(bf16)
+    low = (value - high.astype(f32)).astype(bf16)
+    spread = dot(high, target_ref[...]) + dot(low, target_ref[...])
+    change = spread[:half, :n] + spread[half:, n:]
+    out_ref[...] = image_ref[...] - primal_step * change.reshape(out_ref.shape)
+
+
+def call(kernel, outs, *operands, vmem=24, scratch=()):
     def place(a):
         return pl.BlockSpec(memory_space=pltpu.SMEM if a.ndim == 1 else pltpu.VMEM)
 
@@ -272,6 +303,7 @@
         in_specs=[place(a) for a in operands],
         out_specs=[place(a) for a in outs],
         out_shape=outs,
+        scratch_shapes=[pltpu.VMEM(shape, f32) for shape in scratch],
         compiler_params=pltpu.CompilerParams(vmem_limit_bytes=vmem * 1024 * 1024),
     )(*operands)
 
@@ -348,21 +380,18 @@
     )
     forth = [(int(place_of[i]), int(place_of[i + 1])) for i in range(count - 1)]
     before = lax.ppermute(guess, COLUMN, forth)
-    grad = grad.reshape(2, nz, zq, group, rows).transpose(3, 0, 1, 2, 4)
-    grad = lax.all_to_all(grad, GROUP, 0, 0, tiled=True).astype(f32).sum(0)
-
-    (rest,) = call(last_kernel, (images_like,), edge, images, change, guess, before)
-    rest = rest.reshape(2, 2, nz, zq, group, rows)
-    rest = lax.dynamic_index_in_dim(rest, lax.axis_index(GROUP), 4, keepdims=False)
-    result = jnp.concatenate([rest[:1] + grad[None], rest[1:]], 0)
-    result = result.reshape(2, 2, slabs, planes, zq, rows).transpose(4, 2, 0, 1, 3, 5)
-    result = spread(result.reshape(count, 2, 2 * planes * rows))
-    targets = np.stack([pick, np.concatenate([pick[:, 1:], np.zeros_like(pick[:, :1])], 1)], 1)
-    result = lax.dot_general(
-        result.reshape(2 * count, -1), targets.reshape(2 * count, nx), (((0,), (0,)), ((), ())),
-        precision=lax.Precision.HIGHEST, preferred_element_type=f32,
-    )
-    return initial_image - primal_step * result.reshape(2, planes, rows, nx)
+    parts = lax.all_gather(grad, GROUP, axis=0)
+    place_in_group = lax.axis_index(GROUP).astype(jnp.int32)[None]
+    (packed,) = call(
+        last_kernel, (jax.ShapeDtypeStruct((count, nx), f32),),
+        edge, place_in_group, images, change, guess, before, parts, scratch=[(4, nz, ny)],
+    )
+    packed = spread(packed)
+    targets = np.concatenate([pick, pick[:, 1:], np.zeros_like(pick[:, :1])], 1).astype(bf16)
+    (image,) = call(
+        result_kernel, (jax.ShapeDtypeStruct(initial_image.shape, f32),), packed, targets, initial_image
+    )
+    return image
 
 
 def solution(mesh):

time: 153 us -> 150 us (0.980)
  blocking collectives: 42.6 us -> 48.7 us
  starting transfers between devices: 34.2 us -> 30.7 us
  local copies, waits for them, and re-layouts: 4.95 us -> 1.86 us
    all_gather x1 -> x2, blocking collectives: 6.12 us -> 12.2 us  [on_device(): parts = lax.all_gather(grad, GROUP, axis=0)]
    all_to_all x1 -> x0, starting transfers between devices: 3.69 us -> none  [on_device(): grad = lax.all_to_all(grad, GROUP, 0, 0, tiled=True).astype(f32).sum(0)]
    pallas_call x4 -> x5, Pallas kernels: 10.9 us -> 12.1 us  [call(): pl.pallas_call(kernel, in_specs=[place(a) for a in operands], out_specs=[...]
  transfers between devices with their start and end apart: 4 -> 3, of which waited for: 2 -> 1; matrix products, arithmetic and copies ran while one was open for 1% -> 0% of each run, Pallas kernels for 1% -> 0%
where the time goes in v9:
time: 150 us
  waiting for transfers between devices  55.7 us (37%)
  blocking collectives  48.7 us (32%)
  starting transfers between devices  30.7 us (20%)
  Pallas kernels  12.1 us (8%)
  local copies, waits for them, and re-layouts  1.86 us (1%)
    all_to_all x1, waiting for transfers between devices, spread(): return lax.all_to_all(blocks, COLUMN, 0, 0, tiled=True)  55.7 us
    all_to_all x1, blocking collectives, spread(): return lax.all_to_all(blocks, COLUMN, 0, 0, tiled=True)  26 us
    all_to_all x1, starting transfers between devices, spread(): return lax.all_to_all(blocks, COLUMN, 0, 0, tiled=True)  23 us
    all_gather x2, blocking collectives, on_device(): parts = lax.all_gather(grad, GROUP, axis=0)  12.2 us
    pallas_call x5, Pallas kernels, call(): pl.pallas_call(kernel, in_specs=[place(a) for a in operands], out_specs=[...  12.1 us
    all_gather x1, blocking collectives, on_device(): start = lax.all_gather(pairs(extra[:, :, :half]), GROUP, axis=0)  10.6 us
    all_to_all x1, starting transfers between devices, on_device(): mask = lax.all_to_all(mask, COLUMN[3], 0, 0, tiled=True)  4.19 us
    ppermute x1, starting transfers between devices, on_device(): before = lax.ppermute(guess, COLUMN, forth)  3.52 us
  transfers between devices with their start and end apart: 3, of which 1 were waited for; matrix products, arithmetic and copies ran while one was open for 0% of the time, Pallas kernels for 0%

profile of v9, /device:TPU:1, one launch (start us, length us, event | category | flops | bytes accessed | tf_op | source)
XLA Modules:
  0.0 149.5 jit_solution(10935964298011319698)
XLA Ops:
  0.0 3.7 %shard_map.136 = bf16[128,4,1152]{2,1,0:T(4,128)(2,1)} custom-call(bf16[2,2,4,128,128]{4,3,2,1,0:T(8,128)(2,1)} %maps_ref.1, bf16[2,2,128,4,128]{4,3,2,1,0:T(4,128)(2,1)} %data_ref.1, s32[2,4,128]{2,1,0:T(4,128)} %bitcast.18, f32[2,4,8,128]{3,2,1,0:T(8,128)} %image_ref.3, bf16[128,512]{1,0:T(8,128)(2,1)} %constant.54.clone.near_ref, ...), custom_call_target="tpu_custom_call" | custom-call | tf_op jit(solution)/shard_map/pallas_call | solution.py:301
  3.7 23.0 %all-to-all-start = ((bf16[128,4,1152]{2,1,0:T(4,128)(2,1)}), bf16[128,4,1152]{2,1,0:T(4,128)(2,1)S(1)}, u32[]{:S(2)}, u32[]{:S(2)}) async-start(bf16[128,4,1152]{2,1,0:T(4,128)(2,1)} %shard_map.136), calls=%async_computation | async-start | bytes 2359296 | tf_op jit(solution)/shard_map/all_to_all | solution.py:326
  26.7 0.1 pad_maximum_fusion.2.edge_ref
  26.8 0.0 copy-start
  26.8 0.0 copy-start.1
  26.8 0.0 copy-start.2
  26.8 55.7 %all-to-all-done.block_ref = bf16[128,4,1152]{2,1,0:T(4,128)(2,1)S(1)} async-done(((bf16[128,4,1152]{2,1,0:T(4,128)(2,1)}), bf16[128,4,1152]{2,1,0:T(4,128)(2,1)S(1)}, u32[]{:S(2)}, u32[]{:S(2)}) %all-to-all-start) | async-done | bytes 1179680 | tf_op jit(solution)/shard_map/all_to_all | solution.py:326
  82.6 0.1 fusion
  82.7 0.1 pad_maximum_fusion.1
  82.8 0.7 broadcast_in_dim.10
  83.5 4.2 %all-to-all-start.1 = ((bf16[4,2,128,128]{3,2,1,0:T(8,128)(2,1)}), bf16[4,2,128,128]{3,2,1,0:T(8,128)(2,1)S(1)}, u32[]{:S(2)}, u32[]{:S(2)}) async-start(bf16[4,2,128,128]{3,2,1,0:T(8,128)(2,1)} %broadcast_in_dim.10), calls=%async_computation.1 | async-start | bytes 524288 | tf_op jit(solution)/shard_map/all_to_all | solution.py:352
  87.7 0.1 pad_maximum_fusion
  87.8 10.6 %all-gather = bf16[8,128,128]{2,1,0:T(8,128)(2,1)} all-gather(bf16[2,128,128]{2,1,0:T(8,128)(2,1)S(1)} %pad_maximum_fusion), channel_id=2, replica_groups=mesh['zq'=4,'zp'=2,'core'=2,'x'=4,'zhi'=2,'y'=4] {'zp','core'}, dimensions={0}, use_global_device_ids=true | all-gather | bytes 327680 | tf_op jit(solution)/shard_map/all_gather | solution.py:353
  98.4 0.0 all-to-all-done.1.mask_ref
  98.4 0.0 copy-done
  98.4 0.0 copy-done.1
  98.4 0.0 copy-done.2
  98.4 0.0 copy-start.3
  98.4 0.9 copy-done.3
  99.3 3.4 %shard_map.137 = (f32[4,256,256]{2,1,0:T(8,128)S(1)}, bf16[2,128,128]{2,1,0:T(8,128)(2,1)S(1)}, f32[2,128,128]{2,1,0:T(8,128)S(1)}, f32[2,2,128,128]{3,2,1,0:T(8,128)S(1)}) custom-call(f32[2]{0:T(128)S(1)} %pad_maximum_fusion.2.edge_ref, bf16[4,2,128,128]{3,2,1,0:T(8,128)(2,1)S(1)} %bitcast.13, bf16[1024,768]{1,0:T(8,128)(2,1)S(1)} %copy-done.2, ...), custom_call_target="tpu_custom_call" | custom-call | tf_op jit(solution)/shard_map/pallas_call | solution.py:301
  102.8 6.1 %all-gather.1 = bf16[8,128,128]{2,1,0:T(8,128)(2,1)S(1)} all-gather(bf16[2,128,128]{2,1,0:T(8,128)(2,1)S(1)} %get-tuple-element.13), channel_id=3, replica_groups=mesh['zq'=4,'zp'=2,'core'=2,'x'=4,'zhi'=2,'y'=4] {'zp','core'}, dimensions={0}, use_global_device_ids=true | all-gather | bytes 327680 | tf_op jit(solution)/shard_map/all_gather | solution.py:376
  108.9 2.6 %shard_map.138 = (bf16[2,128,128]{2,1,0:T(8,128)(2,1)S(1)}, f32[2,128,128]{2,1,0:T(8,128)S(1)}, f32[2,128,128]{2,1,0:T(8,128)S(1)}) custom-call(bf16[4,2,128,128]{3,2,1,0:T(8,128)(2,1)S(1)} %bitcast.12, f32[2,128,128]{2,1,0:T(8,128)S(1)} %get-tuple-element.14.spread_ref, f32[2,2,128,128]{3,2,1,0:T(8,128)S(1)} %get-tuple-element.12.image_ref, ...), custom_call_target="tpu_custom_call" | custom-call | tf_op jit(solution)/shard_map/pallas_call | solution.py:301
  111.5 0.0 copy-start.4
  111.5 0.0 copy-start.5
  111.6 3.5 %collective-permute-start = (f32[2,128,128]{2,1,0:T(8,128)S(1)}, f32[2,128,128]{2,1,0:T(8,128)S(1)}, u32[]{:S(2)}, u32[]{:S(2)}) collective-permute-start(f32[2,128,128]{2,1,0:T(8,128)S(1)} %get-tuple-element.17.guess_ref), channel_id=1, source_target_pairs={{0,1},{1,2},{2,3},{3,11},{11,10},{10,9},{9,8},{8,16},{16,17},{17,1... | collective-permute-start | bytes 393224 | tf_op jit(solution)/shard_map/ppermute | solution.py:382
  115.1 6.1 %all-gather.2 = bf16[8,128,128]{2,1,0:T(8,128)(2,1)S(1)} all-gather(bf16[2,128,128]{2,1,0:T(8,128)(2,1)S(1)} %get-tuple-element.18), channel_id=4, replica_groups=mesh['zq'=4,'zp'=2,'core'=2,'x'=4,'zhi'=2,'y'=4] {'zp','core'}, dimensions={0}, use_global_device_ids=true | all-gather | bytes 327680 | tf_op jit(solution)/shard_map/all_gather | solution.py:383
  121.2 0.0 collective-permute-done.before_ref
  121.2 1.5 %shard_map.139 = f32[128,128]{1,0:T(8,128)S(1)} custom-call(f32[2]{0:T(128)S(1)} %pad_maximum_fusion.2.edge_ref, s32[1]{0:T(128)} %bitcast.2.place_ref, f32[2,2,128,128]{3,2,1,0:T(8,128)S(1)} %get-tuple-element.12.image_ref, f32[2,128,128]{2,1,0:T(8,128)S(1)} %get-tuple-element.16.change_ref, f32[2,128,128]{2,1,0:T(8,128)S(1)} %get-tuple-element.17.guess_ref, ...), custom_call_target="tpu_custom_call" | custom-call | tf_op jit(solution)/shard_map/pallas_call | solution.py:301
  122.7 26.0 %all_to_all.21 = f32[128,1,128]{2,1,0:T(1,128)S(1)} all-to-all(f32[128,1,128]{2,1,0:T(1,128)S(1)} %bitcast.15), channel_id=1, replica_groups=mesh['zq'=4,'zp'=2,'core'=2,'x'=4,'zhi'=2,'y'=4] {'zq','x','zhi','y'}, dimensions={0} | all-to-all | bytes 131072 | tf_op jit(solution)/shard_map/all_to_all | solution.py:326
  148.7 0.0 copy-done.4
  148.7 0.0 copy-done.5
  148.7 0.9 shard_map.140
  (1 shorter events, 0.0 us)
Async XLA Ops:
  3.7 78.8 %all-to-all-start = ((bf16[128,4,1152]{2,1,0:T(4,128)(2,1)}), bf16[128,4,1152]{2,1,0:T(4,128)(2,1)S(1)}, u32[]{:S(2)}, u32[]{:S(2)}) async-start(bf16[128,4,1152]{2,1,0:T(4,128)(2,1)} %shard_map.136), calls=%async_computation | async-start | bytes 2359296 | tf_op jit(solution)/shard_map/all_to_all | solution.py:326
  26.8 71.6 %copy-start = (bf16[256,256]{1,0:T(8,128)(2,1)S(1)}, bf16[256,256]{1,0:T(8,128)(2,1)}, u32[]{:S(2)}) copy-start(bf16[256,256]{1,0:T(8,128)(2,1)} %constant.60.clone.gy_ref.gz_ref) | copy-start | bytes 393220
  26.8 71.6 %copy-start.1 = (bf16[256,256]{1,0:T(8,128)(2,1)S(1)}, bf16[256,256]{1,0:T(8,128)(2,1)}, u32[]{:S(2)}) copy-start(bf16[256,256]{1,0:T(8,128)(2,1)} %constant.59.clone.fz_ref.fy_ref) | copy-start | bytes 393220
  26.8 71.6 %copy-start.2 = (bf16[1024,768]{1,0:T(8,128)(2,1)S(1)}, bf16[1024,768]{1,0:T(8,128)(2,1)}, u32[]{:S(2)}) copy-start(bf16[1024,768]{1,0:T(8,128)(2,1)} %constant.58.clone.place_ref) | copy-start | bytes 4718596
  83.5 14.8 %all-to-all-start.1 = ((bf16[4,2,128,128]{3,2,1,0:T(8,128)(2,1)}), bf16[4,2,128,128]{3,2,1,0:T(8,128)(2,1)S(1)}, u32[]{:S(2)}, u32[]{:S(2)}) async-start(bf16[4,2,128,128]{3,2,1,0:T(8,128)(2,1)} %broadcast_in_dim.10), calls=%async_computation.1 | async-start | bytes 524288 | tf_op jit(solution)/shard_map/all_to_all | solution.py:352
  98.4 1.0 copy-start.3
  111.5 37.1 %copy-start.4 = (f32[2,4,8,128]{3,2,1,0:T(8,128)S(1)}, f32[2,4,8,128]{3,2,1,0:T(8,128)}, u32[]{:S(2)}) copy-start(f32[2,4,8,128]{3,2,1,0:T(8,128)} %image_ref.3) | copy-start | bytes 98308
  111.5 37.1 %copy-start.5 = (bf16[128,256]{1,0:T(8,128)(2,1)S(1)}, bf16[128,256]{1,0:T(8,128)(2,1)}, u32[]{:S(2)}) copy-start(bf16[128,256]{1,0:T(8,128)(2,1)} %constant.61.clone.target_ref) | copy-start | bytes 196612
  111.6 9.6 %collective-permute-start = (f32[2,128,128]{2,1,0:T(8,128)S(1)}, f32[2,128,128]{2,1,0:T(8,128)S(1)}, u32[]{:S(2)}, u32[]{:S(2)}) collective-permute-start(f32[2,128,128]{2,1,0:T(8,128)S(1)} %get-tuple-element.17.guess_ref), channel_id=1, source_target_pairs={{0,1},{1,2},{2,3},{3,11},{11,10},{10,9},{9,8},{8,16},{16,17},{17,1... | collective-permute-start | bytes 393224 | tf_op jit(solution)/shard_map/ppermute | solution.py:382

commit v10 on v9

--- a/solution.py
+++ b/solution.py
@@ -106,17 +106,26 @@
     )
 
 
-def masked(mask_ref, a, coils, value):
+def read_mask(mask_ref, coils):
     n = mask_ref.shape[3]
-    late, pair = divmod(a, mask_ref.shape[1])
     left = position((n, n), 1) < n // 2
     columns = []
-    for c in range(coils):
-        halves = [mask_ref[2 * c + h, pair].astype(f32) for h in range(2)]
-        halves[1 - late] = pltpu.roll(halves[1 - late], n // 2, 1)
-        columns.append(jnp.where(left, halves[0], halves[1]))
-    mask = jnp.concatenate(columns, 1)
-    return jnp.concatenate([mask, mask], 0) * value
+    for a in range(2 * mask_ref.shape[1]):
+        late, pair = divmod(a, mask_ref.shape[1])
+        for c in range(coils):
+            halves = [mask_ref[2 * c + h, pair].astype(f32) for h in range(2)]
+            halves[1 - late] = pltpu.roll(halves[1 - late], n // 2, 1)
+            columns.append(jnp.where(left, halves[0], halves[1]))
+    return jnp.concatenate(columns, 1)
+
+
+def read_coils(block_ref, mask_ref):
+    coils = block_ref.shape[2] // block_ref.shape[0] // 4
+    pairs = range(2 * mask_ref.shape[1])
+    maps = [m for a in pairs for m in read_maps(block_ref, a, coils)]
+    data = jnp.concatenate([read_data(block_ref, a, coils) for a in pairs], 1)
+    mask = read_mask(mask_ref, coils)
+    return maps, data, jnp.concatenate([mask, mask], 0)
 
 
 def pack_kernel(maps_ref, data_ref, mask_ref, image_ref, near_ref, inv_ref, sort_ref, choose_ref, out_ref):
@@ -202,23 +211,18 @@
     edge_ref, start_ref, place_ref, block_ref, mask_ref, fz_ref, fy_ref, gy_ref, gz_ref,
     dual_ref, out_ref, change_ref, image_ref,
 ):
-    pairs = dual_ref.shape[0]
-    coils = dual_ref.shape[2] // start_ref.shape[2]
-    pieces = [start_ref[r, h] for r in range(start_ref.shape[0]) for h in range(start_ref.shape[1])]
+    maps, data, mask = read_coils(block_ref, mask_ref)
+    pieces = [start_ref[h, r] for r in range(start_ref.shape[1]) for h in range(start_ref.shape[0])]
     planes = dot(jnp.concatenate(pieces, 1), place_ref[...])
     n = planes.shape[0]
     here, before, after = [
         [planes[:, (2 * k + p) * n : (2 * k + p + 1) * n] for p in range(2)] for k in range(3)
     ]
     after = [jnp.where(edge_ref[1] > 0.0, a, h) for a, h in zip(after, here)]
-    sums = [0.0, 0.0]
-    for a in range(pairs):
-        maps = read_maps(block_ref, a, coils)
-        spectrum = to_kspace(maps, here, fz_ref[...], fy_ref[...])
-        dual = dual_step * masked(mask_ref, a, coils, spectrum - read_data(block_ref, a, coils))
-        dual = dual * (1.0 / (1.0 + dual_step))
-        dual_ref[a] = dual
-        sums = [s + t for s, t in zip(sums, to_image(dual.astype(bf16), maps, gy_ref[...], gz_ref[...]))]
+    spectrum = to_kspace(maps, here, fz_ref[...], fy_ref[...])
+    dual = dual_step * (mask * (spectrum - data)) * (1.0 / (1.0 + dual_step))
+    dual_ref[...] = dual
+    sums = to_image(dual.astype(bf16), maps, gy_ref[...], gz_ref[...])
     spread = divergence(shrink(here, after, None))
     duals_before = shrink(before, here, None)
     for p in range(2):
@@ -232,21 +236,16 @@
     parts_ref, spread_ref, image_ref, dual_ref, block_ref, mask_ref, fz_ref, fy_ref, gy_ref, gz_ref,
     out_ref, change_ref, guess_ref,
 ):
-    pairs = dual_ref.shape[0]
-    coils = dual_ref.shape[2] // parts_ref.shape[2]
     guess = []
     for p in range(2):
         change = spread_ref[p] + sum(parts_ref[r, p].astype(f32) for r in range(parts_ref.shape[0]))
         guess.append(image_ref[0, p] - (2.0 * primal_step) * change)
         change_ref[p] = change
         guess_ref[p] = guess[p]
-    sums = [0.0, 0.0]
-    for a in range(pairs):
-        maps = read_maps(block_ref, a, coils)
-        spectrum = to_kspace(maps, guess, fz_ref[...], fy_ref[...])
-        step = dual_step * masked(mask_ref, a, coils, spectrum - read_data(block_ref, a, coils))
-        dual = (dual_ref[a] + step) * (1.0 / (1.0 + dual_step))
-        sums = [s + t for s, t in zip(sums, to_image(dual.astype(bf16), maps, gy_ref[...], gz_ref[...]))]
+    maps, data, mask = read_coils(block_ref, mask_ref)
+    spectrum = to_kspace(maps, guess, fz_ref[...], fy_ref[...])
+    dual = (dual_ref[...] + dual_step * (mask * (spectrum - data))) * (1.0 / (1.0 + dual_step))
+    sums = to_image(dual.astype(bf16), maps, gy_ref[...], gz_ref[...])
     for p in range(2):
         out_ref[p] = sums[p].astype(bf16)
 
@@ -303,7 +302,7 @@
         in_specs=[place(a) for a in operands],
         out_specs=[place(a) for a in outs],
         out_shape=outs,
-        scratch_shapes=[pltpu.VMEM(shape, f32) for shape in scratch],
+        scratch_shapes=scratch,
         compiler_params=pltpu.CompilerParams(vmem_limit_bytes=vmem * 1024 * 1024),
     )(*operands)
 
@@ -350,7 +349,7 @@
     mask = pairs(extra[:, :, half:])
     mask = jnp.broadcast_to(mask[None], (quarters, *mask.shape))
     mask = lax.all_to_all(mask, COLUMN[3], 0, 0, tiled=True)
-    start = lax.all_gather(pairs(extra[:, :, :half]), GROUP, axis=0)
+    start = lax.all_gather(pairs(extra[:, :, :half]), GROUP, axis=1)
 
     place = np.zeros((group, zq // 2, 2, 4, 2, rows, 3, 2, zq, group, rows), np.float32)
     for r in range(group):
@@ -364,7 +363,7 @@
 
     fz, gz = (table(nz, inverse).reshape(2 * nz, 2 * nz) for inverse in (False, True))
     fy, gy = (table(ny, inverse).reshape(2 * ny, 2 * ny) for inverse in (False, True))
-    dual_like = jax.ShapeDtypeStruct((zq, 2 * ny, coils * nz), f32)
+    dual_like = jax.ShapeDtypeStruct((2 * ny, zq * coils * nz), f32)
     grad_like = jax.ShapeDtypeStruct((2, nz, ny), bf16)
     image_like = jax.ShapeDtypeStruct((2, nz, ny), f32)
 
@@ -384,7 +383,7 @@
     place_in_group = lax.axis_index(GROUP).astype(jnp.int32)[None]
     (packed,) = call(
         last_kernel, (jax.ShapeDtypeStruct((count, nx), f32),),
-        edge, place_in_group, images, change, guess, before, parts, scratch=[(4, nz, ny)],
+        edge, place_in_group, images, change, guess, before, parts, scratch=[pltpu.VMEM((4, nz, ny), f32)],
     )
     packed = spread(packed)
     targets = np.concatenate([pick, pick[:, 1:], np.zeros_like(pick[:, :1])], 1).astype(bf16)

time: 150 us -> 148 us (0.987)
  Pallas kernels: 12.1 us -> 10.3 us
    pallas_call x5, Pallas kernels: 12.1 us -> 10.3 us  [call(): pl.pallas_call(kernel, in_specs=[place(a) for a in operands], out_specs=[...]
where the time goes in v10:
time: 148 us
  waiting for transfers between devices  55.7 us (38%)
  blocking collectives  48.7 us (33%)
  starting transfers between devices  30.7 us (21%)
  Pallas kernels  10.3 us (7%)
  local copies, waits for them, and re-layouts  1.86 us (1%)
    all_to_all x1, waiting for transfers between devices, spread(): return lax.all_to_all(blocks, COLUMN, 0, 0, tiled=True)  55.7 us
    all_to_all x1, blocking collectives, spread(): return lax.all_to_all(blocks, COLUMN, 0, 0, tiled=True)  26 us
    all_to_all x1, starting transfers between devices, spread(): return lax.all_to_all(blocks, COLUMN, 0, 0, tiled=True)  23 us
    all_gather x2, blocking collectives, on_device(): parts = lax.all_gather(grad, GROUP, axis=0)  12.2 us
    all_gather x1, blocking collectives, on_device(): start = lax.all_gather(pairs(extra[:, :, :half]), GROUP, axis=1)  10.6 us
    pallas_call x5, Pallas kernels, call(): pl.pallas_call(kernel, in_specs=[place(a) for a in operands], out_specs=[...  10.3 us
    all_to_all x1, starting transfers between devices, on_device(): mask = lax.all_to_all(mask, COLUMN[3], 0, 0, tiled=True)  4.19 us
    ppermute x1, starting transfers between devices, on_device(): before = lax.ppermute(guess, COLUMN, forth)  3.55 us
  transfers between devices with their start and end apart: 3, of which 1 were waited for; matrix products, arithmetic and copies ran while one was open for 0% of the time, Pallas kernels for 0%

profile of v10, /device:TPU:1, one launch (start us, length us, event | category | flops | bytes accessed | tf_op | source)
XLA Modules:
  0.0 147.7 jit_solution(7134493252836988864)
XLA Ops:
  0.0 3.7 %shard_map.136 = bf16[128,4,1152]{2,1,0:T(4,128)(2,1)} custom-call(bf16[2,2,4,128,128]{4,3,2,1,0:T(8,128)(2,1)} %maps_ref.1, bf16[2,2,128,4,128]{4,3,2,1,0:T(4,128)(2,1)} %data_ref.1, s32[2,4,128]{2,1,0:T(4,128)} %bitcast.18, f32[2,4,8,128]{3,2,1,0:T(8,128)} %image_ref.3, bf16[128,512]{1,0:T(8,128)(2,1)} %constant.54.clone.near_ref, ...), custom_call_target="tpu_custom_call" | custom-call | tf_op jit(solution)/shard_map/pallas_call | solution.py:300
  3.7 23.0 %all-to-all-start = ((bf16[128,4,1152]{2,1,0:T(4,128)(2,1)}), bf16[128,4,1152]{2,1,0:T(4,128)(2,1)S(1)}, u32[]{:S(2)}, u32[]{:S(2)}) async-start(bf16[128,4,1152]{2,1,0:T(4,128)(2,1)} %shard_map.136), calls=%async_computation | async-start | bytes 2359296 | tf_op jit(solution)/shard_map/all_to_all | solution.py:325
  26.7 0.1 pad_maximum_fusion.2.edge_ref
  26.8 0.0 copy-start
  26.8 0.0 copy-start.1
  26.8 0.0 copy-start.2
  26.8 55.7 %all-to-all-done.block_ref = bf16[128,4,1152]{2,1,0:T(4,128)(2,1)S(1)} async-done(((bf16[128,4,1152]{2,1,0:T(4,128)(2,1)}), bf16[128,4,1152]{2,1,0:T(4,128)(2,1)S(1)}, u32[]{:S(2)}, u32[]{:S(2)}) %all-to-all-start) | async-done | bytes 1179680 | tf_op jit(solution)/shard_map/all_to_all | solution.py:325
  82.6 0.1 fusion
  82.7 0.1 pad_maximum_fusion.1
  82.8 0.7 broadcast_in_dim.10
  83.5 4.2 %all-to-all-start.1 = ((bf16[4,2,128,128]{3,2,1,0:T(8,128)(2,1)}), bf16[4,2,128,128]{3,2,1,0:T(8,128)(2,1)S(1)}, u32[]{:S(2)}, u32[]{:S(2)}) async-start(bf16[4,2,128,128]{3,2,1,0:T(8,128)(2,1)} %broadcast_in_dim.10), calls=%async_computation.1 | async-start | bytes 524288 | tf_op jit(solution)/shard_map/all_to_all | solution.py:351
  87.7 0.1 pad_maximum_fusion
  87.8 10.6 %all-gather = bf16[2,512,128]{2,1,0:T(8,128)(2,1)} all-gather(bf16[2,128,128]{2,1,0:T(8,128)(2,1)S(1)} %pad_maximum_fusion), channel_id=2, replica_groups=mesh['zq'=4,'zp'=2,'core'=2,'x'=4,'zhi'=2,'y'=4] {'zp','core'}, dimensions={1}, use_global_device_ids=true | all-gather | bytes 327680 | tf_op jit(solution)/shard_map/all_gather | solution.py:352
  98.4 0.0 all-to-all-done.1.mask_ref
  98.4 0.0 copy-done
  98.4 0.0 copy-done.1
  98.4 0.0 copy-done.2
  98.4 0.0 copy-start.3
  98.4 0.9 copy-done.3
  99.4 2.5 %shard_map.137 = (f32[256,1024]{1,0:T(8,128)S(1)}, bf16[2,128,128]{2,1,0:T(8,128)(2,1)S(1)}, f32[2,128,128]{2,1,0:T(8,128)S(1)}, f32[2,2,128,128]{3,2,1,0:T(8,128)S(1)}) custom-call(f32[2]{0:T(128)S(1)} %pad_maximum_fusion.2.edge_ref, bf16[2,4,128,128]{3,2,1,0:T(8,128)(2,1)S(1)} %bitcast.13, bf16[1024,768]{1,0:T(8,128)(2,1)S(1)} %copy-done.2, ...), custom_call_target="tpu_custom_call" | custom-call | tf_op jit(solution)/shard_map/pallas_call | solution.py:300
  101.9 6.1 %all-gather.1 = bf16[8,128,128]{2,1,0:T(8,128)(2,1)S(1)} all-gather(bf16[2,128,128]{2,1,0:T(8,128)(2,1)S(1)} %get-tuple-element.13), channel_id=3, replica_groups=mesh['zq'=4,'zp'=2,'core'=2,'x'=4,'zhi'=2,'y'=4] {'zp','core'}, dimensions={0}, use_global_device_ids=true | all-gather | bytes 327680 | tf_op jit(solution)/shard_map/all_gather | solution.py:375
  108.0 1.7 %shard_map.138 = (bf16[2,128,128]{2,1,0:T(8,128)(2,1)S(1)}, f32[2,128,128]{2,1,0:T(8,128)S(1)}, f32[2,128,128]{2,1,0:T(8,128)S(1)}) custom-call(bf16[4,2,128,128]{3,2,1,0:T(8,128)(2,1)S(1)} %bitcast.12, f32[2,128,128]{2,1,0:T(8,128)S(1)} %get-tuple-element.14.spread_ref, f32[2,2,128,128]{3,2,1,0:T(8,128)S(1)} %get-tuple-element.12.image_ref, ...), custom_call_target="tpu_custom_call" | custom-call | tf_op jit(solution)/shard_map/pallas_call | solution.py:300
  109.7 0.0 copy-start.4
  109.7 0.0 copy-start.5
  109.7 3.6 %collective-permute-start = (f32[2,128,128]{2,1,0:T(8,128)S(1)}, f32[2,128,128]{2,1,0:T(8,128)S(1)}, u32[]{:S(2)}, u32[]{:S(2)}) collective-permute-start(f32[2,128,128]{2,1,0:T(8,128)S(1)} %get-tuple-element.17.guess_ref), channel_id=1, source_target_pairs={{0,1},{1,2},{2,3},{3,11},{11,10},{10,9},{9,8},{8,16},{16,17},{17,1... | collective-permute-start | bytes 393224 | tf_op jit(solution)/shard_map/ppermute | solution.py:381
  113.3 6.1 %all-gather.2 = bf16[8,128,128]{2,1,0:T(8,128)(2,1)S(1)} all-gather(bf16[2,128,128]{2,1,0:T(8,128)(2,1)S(1)} %get-tuple-element.18), channel_id=4, replica_groups=mesh['zq'=4,'zp'=2,'core'=2,'x'=4,'zhi'=2,'y'=4] {'zp','core'}, dimensions={0}, use_global_device_ids=true | all-gather | bytes 327680 | tf_op jit(solution)/shard_map/all_gather | solution.py:382
  119.4 0.0 collective-permute-done.before_ref
  119.4 1.5 %shard_map.139 = f32[128,128]{1,0:T(8,128)S(1)} custom-call(f32[2]{0:T(128)S(1)} %pad_maximum_fusion.2.edge_ref, s32[1]{0:T(128)} %bitcast.2.place_ref, f32[2,2,128,128]{3,2,1,0:T(8,128)S(1)} %get-tuple-element.12.image_ref, f32[2,128,128]{2,1,0:T(8,128)S(1)} %get-tuple-element.16.change_ref, f32[2,128,128]{2,1,0:T(8,128)S(1)} %get-tuple-element.17.guess_ref, ...), custom_call_target="tpu_custom_call" | custom-call | tf_op jit(solution)/shard_map/pallas_call | solution.py:300
  120.9 26.0 %all_to_all.21 = f32[128,1,128]{2,1,0:T(1,128)S(1)} all-to-all(f32[128,1,128]{2,1,0:T(1,128)S(1)} %bitcast.15), channel_id=1, replica_groups=mesh['zq'=4,'zp'=2,'core'=2,'x'=4,'zhi'=2,'y'=4] {'zq','x','zhi','y'}, dimensions={0} | all-to-all | bytes 131072 | tf_op jit(solution)/shard_map/all_to_all | solution.py:325
  146.9 0.0 copy-done.4
  146.9 0.0 copy-done.5
  146.9 0.8 shard_map.140
  (1 shorter events, 0.0 us)
Async XLA Ops:
  3.7 78.8 %all-to-all-start = ((bf16[128,4,1152]{2,1,0:T(4,128)(2,1)}), bf16[128,4,1152]{2,1,0:T(4,128)(2,1)S(1)}, u32[]{:S(2)}, u32[]{:S(2)}) async-start(bf16[128,4,1152]{2,1,0:T(4,128)(2,1)} %shard_map.136), calls=%async_computation | async-start | bytes 2359296 | tf_op jit(solution)/shard_map/all_to_all | solution.py:325
  26.8 71.6 %copy-start = (bf16[256,256]{1,0:T(8,128)(2,1)S(1)}, bf16[256,256]{1,0:T(8,128)(2,1)}, u32[]{:S(2)}) copy-start(bf16[256,256]{1,0:T(8,128)(2,1)} %constant.60.clone.gy_ref.gz_ref) | copy-start | bytes 393220
  26.8 71.6 %copy-start.1 = (bf16[256,256]{1,0:T(8,128)(2,1)S(1)}, bf16[256,256]{1,0:T(8,128)(2,1)}, u32[]{:S(2)}) copy-start(bf16[256,256]{1,0:T(8,128)(2,1)} %constant.59.clone.fz_ref.fy_ref) | copy-start | bytes 393220
  26.8 71.6 %copy-start.2 = (bf16[1024,768]{1,0:T(8,128)(2,1)S(1)}, bf16[1024,768]{1,0:T(8,128)(2,1)}, u32[]{:S(2)}) copy-start(bf16[1024,768]{1,0:T(8,128)(2,1)} %constant.58.clone.place_ref) | copy-start | bytes 4718596
  83.5 14.9 %all-to-all-start.1 = ((bf16[4,2,128,128]{3,2,1,0:T(8,128)(2,1)}), bf16[4,2,128,128]{3,2,1,0:T(8,128)(2,1)S(1)}, u32[]{:S(2)}, u32[]{:S(2)}) async-start(bf16[4,2,128,128]{3,2,1,0:T(8,128)(2,1)} %broadcast_in_dim.10), calls=%async_computation.1 | async-start | bytes 524288 | tf_op jit(solution)/shard_map/all_to_all | solution.py:351
  98.4 1.0 copy-start.3
  109.7 37.2 %copy-start.4 = (f32[2,4,8,128]{3,2,1,0:T(8,128)S(1)}, f32[2,4,8,128]{3,2,1,0:T(8,128)}, u32[]{:S(2)}) copy-start(f32[2,4,8,128]{3,2,1,0:T(8,128)} %image_ref.3) | copy-start | bytes 98308
  109.7 37.2 %copy-start.5 = (bf16[128,256]{1,0:T(8,128)(2,1)S(1)}, bf16[128,256]{1,0:T(8,128)(2,1)}, u32[]{:S(2)}) copy-start(bf16[128,256]{1,0:T(8,128)(2,1)} %constant.61.clone.target_ref) | copy-start | bytes 196612
  109.7 9.6 %collective-permute-start = (f32[2,128,128]{2,1,0:T(8,128)S(1)}, f32[2,128,128]{2,1,0:T(8,128)S(1)}, u32[]{:S(2)}, u32[]{:S(2)}) collective-permute-start(f32[2,128,128]{2,1,0:T(8,128)S(1)} %get-tuple-element.17.guess_ref), channel_id=1, source_target_pairs={{0,1},{1,2},{2,3},{3,11},{11,10},{10,9},{9,8},{8,16},{16,17},{17,1... | collective-permute-start | bytes 393224 | tf_op jit(solution)/shard_map/ppermute | solution.py:381

commit v11 on v10

--- a/solution.py
+++ b/solution.py
@@ -128,32 +128,53 @@
     return maps, data, jnp.concatenate([mask, mask], 0)
 
 
-def pack_kernel(maps_ref, data_ref, mask_ref, image_ref, near_ref, inv_ref, sort_ref, choose_ref, out_ref):
+def pack_kernel(*refs):
+    sources, out_hbm = refs[:8], refs[8]
+    held, out_ref, arrived, left = refs[9:17], refs[17], refs[18], refs[19]
+    loads = [pltpu.make_async_copy(a, b, arrived.at[i]) for i, (a, b) in enumerate(zip(sources, held))]
+    for load in loads:
+        load.start()
+    near_ref, maps_ref, sort_ref, data_ref, inv_ref, mask_ref, image_ref, choose_ref = held
     coils, _, planes, n, _ = maps_ref.shape
-    lines, rows = data_ref.shape[3], image_ref.shape[2]
+    lines = data_ref.shape[3]
     kinds = near_ref.shape[1] // n
-    pick = near_ref[:, :n]
-    sort, mix = sort_ref[0], sort_ref[1]
+    lanes = coils * 2 * n
     part = n // lines
     half = n // 2
     shape = (n, n)
 
+    def place(rows, start, stop):
+        for g in range(lines):
+            together = jnp.concatenate([v[g * part : (g + 1) * part] for v in rows], 0)
+            mixed = dot(sort_ref[1], together).astype(bf16)
+            out_ref[g * part : (g + 1) * part, :, start:stop] = mixed.reshape(part, planes, stop - start)
+        return pltpu.make_async_copy(
+            out_ref.at[:, :, start:stop], out_hbm.at[:, :, start:stop], left.at[start // lanes]
+        )
+
+    for load in loads[:3]:
+        load.wait()
+    pick = near_ref[:, :n]
+    rows = []
+    for t in range(planes):
+        planes_t = jnp.concatenate([maps_ref[c, p, t] for c in range(coils) for p in range(2)], 0)
+        rows.append(dot_t(pick, planes_t).astype(bf16))
+    first = place(rows, 0, lanes)
+    first.start()
+
+    for load in loads[3:]:
+        load.wait()
     field = [jnp.concatenate([data_ref[c, p].reshape(n * lines, n) for p in range(2)], 1) for c in range(coils)]
     field = jnp.concatenate(field, 1)
-    field = [dot(sort, field[g * n : (g + 1) * n]).astype(bf16) for g in range(lines)]
+    field = [dot(sort_ref[0], field[g * n : (g + 1) * n]).astype(bf16) for g in range(lines)]
     mask = jnp.concatenate([mask_ref[c] for c in range(coils)], 0).astype(f32).astype(bf16)
     odd = lax.rem(position(shape, 0), 2) == 1
-
-    packed = []
+    rows = []
     for t in range(planes):
-        planes_t = jnp.concatenate([maps_ref[c, p, t] for c in range(coils) for p in range(2)], 0)
-        pieces = [dot_t(pick, planes_t)]
         line = jnp.concatenate([f[t * part : (t + 1) * part] for f in field], 0)
         line = jnp.concatenate([line[:, c * 2 * n : (c + 1) * 2 * n] for c in range(coils)], 0)
         turned = dot_t(inv_ref[...], line)
-        pieces += [
-            turned[p * n : (p + 1) * n, c * n : (c + 1) * n] for c in range(coils) for p in range(2)
-        ]
+        pieces = [turned[p * n : (p + 1) * n, c * n : (c + 1) * n] for c in range(coils) for p in range(2)]
         value = jnp.concatenate([image_ref[p, t] for p in range(2)], 0)
         high = value.astype(bf16).astype(f32)
         parts = [high, value - high, high, high]
@@ -165,11 +186,11 @@
         chosen = dot(choose_ref[t * n : (t + 1) * n], mask)
         chosen = jnp.where(odd, chosen, pltpu.roll(chosen, half, 1))
         pieces.append(jnp.where(position(shape, 1) < half, image, chosen))
-        packed.append(jnp.concatenate(pieces, 1).astype(bf16))
-    for g in range(lines):
-        together = jnp.concatenate([v[g * part : (g + 1) * part] for v in packed], 0)
-        mixed = dot(mix, together).astype(bf16)
-        out_ref[g * part : (g + 1) * part] = mixed.reshape(part, planes, mixed.shape[1])
+        rows.append(jnp.concatenate(pieces, 1).astype(bf16))
+    second = place(rows, lanes, 2 * lanes + n)
+    second.start()
+    first.wait()
+    second.wait()
 
 
 def shifted(a, axis, step):
@@ -208,12 +229,11 @@
 
 
 def first_kernel(
-    edge_ref, start_ref, place_ref, block_ref, mask_ref, fz_ref, fy_ref, gy_ref, gz_ref,
+    edge_ref, start_ref, block_ref, mask_ref, fz_ref, fy_ref, gy_ref, gz_ref,
     dual_ref, out_ref, change_ref, image_ref,
 ):
     maps, data, mask = read_coils(block_ref, mask_ref)
-    pieces = [start_ref[h, r] for r in range(start_ref.shape[1]) for h in range(start_ref.shape[0])]
-    planes = dot(jnp.concatenate(pieces, 1), place_ref[...])
+    planes = start_ref[...]
     n = planes.shape[0]
     here, before, after = [
         [planes[:, (2 * k + p) * n : (2 * k + p + 1) * n] for p in range(2)] for k in range(3)
@@ -335,11 +355,19 @@
     lanes = coils * 2 * ny
     half = nz // 2
     packed = jax.ShapeDtypeStruct((nx, planes, 2 * lanes + nz), bf16)
-    (blocks,) = call(
-        pack_kernel, (packed,), coil_maps, kspace_data, sample_mask.transpose(0, 2, 1), initial_image,
-        near.astype(bf16), inv_x, np.stack([sort, sort.T]).astype(bf16),
-        choose.reshape(lines * count, -1).astype(bf16), vmem=60,
-    )
+    sources = (
+        near.astype(bf16), coil_maps, np.stack([sort, sort.T]).astype(bf16), kspace_data, inv_x,
+        sample_mask.transpose(0, 2, 1), initial_image, choose.reshape(lines * count, -1).astype(bf16),
+    )
+    blocks = pl.pallas_call(
+        pack_kernel,
+        in_specs=[pl.BlockSpec(memory_space=pl.ANY)] * len(sources),
+        out_specs=pl.BlockSpec(memory_space=pl.ANY),
+        out_shape=packed,
+        scratch_shapes=[pltpu.VMEM(a.shape, a.dtype) for a in (*sources, packed)]
+        + [pltpu.SemaphoreType.DMA((len(sources),)), pltpu.SemaphoreType.DMA((2,))],
+        compiler_params=pltpu.CompilerParams(vmem_limit_bytes=60 * 1024 * 1024),
+    )(*sources)
     blocks = spread(blocks)
     extra = blocks[:, :, 2 * lanes :].reshape(zq, nz, nz)
 
@@ -348,8 +376,9 @@
 
     mask = pairs(extra[:, :, half:])
     mask = jnp.broadcast_to(mask[None], (quarters, *mask.shape))
+    mask, start = lax.optimization_barrier((mask, pairs(extra[:, :, :half])))
     mask = lax.all_to_all(mask, COLUMN[3], 0, 0, tiled=True)
-    start = lax.all_gather(pairs(extra[:, :, :half]), GROUP, axis=1)
+    start = lax.all_gather(start, GROUP, axis=1)
 
     place = np.zeros((group, zq // 2, 2, 4, 2, rows, 3, 2, zq, group, rows), np.float32)
     for r in range(group):
@@ -359,6 +388,8 @@
                     for j in range(rows):
                         place[r, a % (zq // 2), a // (zq // 2), kind, p, j, plane, p, a, r, j] = 1.0
     place = place.reshape(group * zq // 2 * nz, 3 * 2 * ny).astype(bf16)
+    place = place.reshape(group, zq // 2, nz, -1)
+    start = jnp.einsum("hrzl,rhlk->zk", start, place, preferred_element_type=f32)
     edge = jnp.stack([1.0 - is_first.astype(f32), 1.0 - is_last.astype(f32)])
 
     fz, gz = (table(nz, inverse).reshape(2 * nz, 2 * nz) for inverse in (False, True))
@@ -370,7 +401,7 @@
     images_like = jax.ShapeDtypeStruct((2, 2, nz, ny), f32)
     dual, grad, spread_sum, images = call(
         first_kernel, (dual_like, grad_like, image_like, images_like),
-        edge, start, place, blocks, mask, fz, fy, gy, gz,
+        edge, start, blocks, mask, fz, fy, gy, gz,
     )
     parts = lax.all_gather(grad, GROUP, axis=0)
     grad, change, guess = call(

time: 148 us -> 148 us (level)
  matrix products: 0 us -> 1.79 us
    pallas_call x5 -> x4, Pallas kernels: 10.3 us -> 6.36 us  [call(): pl.pallas_call(kernel, in_specs=[place(a) for a in operands], out_specs=[...]
    pallas_call x0 -> x1, Pallas kernels: none -> 3.69 us  [on_device(): pl.pallas_call(pack_kernel, in_specs=[pl.BlockSpec(memory_space=pl.ANY)]...]
    dot_general x0 -> x1, matrix products: none -> 1.79 us  [on_device(): jnp.einsum('hrzl,rhlk->zk', start, place, preferred_element_type=f32)]
  transfers between devices with their start and end apart: 3 -> 3, of which waited for: 1 -> 1; matrix products, arithmetic and copies ran while one was open for 0% -> 1% of each run, Pallas kernels for 0% -> 0%
where the time goes in v11:
time: 148 us
  waiting for transfers between devices  55.7 us (38%)
  blocking collectives  48.1 us (32%)
  starting transfers between devices  31 us (21%)
  Pallas kernels  10.1 us (7%)
  matrix products  1.79 us (1%)
    all_to_all x1, waiting for transfers between devices, spread(): return lax.all_to_all(blocks, COLUMN, 0, 0, tiled=True)  55.7 us
    all_to_all x1, blocking collectives, spread(): return lax.all_to_all(blocks, COLUMN, 0, 0, tiled=True)  26 us
    all_to_all x1, starting transfers between devices, spread(): return lax.all_to_all(blocks, COLUMN, 0, 0, tiled=True)  23 us
    all_gather x2, blocking collectives, on_device(): parts = lax.all_gather(grad, GROUP, axis=0)  11.9 us
    all_gather x1, blocking collectives, on_device(): start = lax.all_gather(start, GROUP, axis=1)  10.1 us
    pallas_call x4, Pallas kernels, call(): pl.pallas_call(kernel, in_specs=[place(a) for a in operands], out_specs=[...  6.36 us
    all_to_all x1, starting transfers between devices, on_device(): mask = lax.all_to_all(mask, COLUMN[3], 0, 0, tiled=True)  4.35 us
    pallas_call x1, Pallas kernels, on_device(): pl.pallas_call(pack_kernel, in_specs=[pl.BlockSpec(memory_space=pl.ANY)]...  3.69 us
  transfers between devices with their start and end apart: 3, of which 1 were waited for; matrix products, arithmetic and copies ran while one was open for 1% of the time, Pallas kernels for 0%

profile of v11, /device:TPU:1, one launch (start us, length us, event | category | flops | bytes accessed | tf_op | source)
XLA Modules:
  0.0 147.8 jit_solution(3400598887608688989)
XLA Ops:
  0.0 3.7 %shard_map.136 = bf16[128,4,1152]{2,1,0:T(4,128)(2,1)} custom-call(bf16[128,512]{1,0:T(8,128)(2,1)} %constant.54.clone.refs_0_, bf16[2,2,4,128,128]{4,3,2,1,0:T(8,128)(2,1)} %refs_1_.1, bf16[2,128,128]{2,1,0:T(8,128)(2,1)} %constant.55.clone.refs_2_, bf16[2,2,128,4,128]{4,3,2,1,0:T(4,128)(2,1)} %refs_3_.1, bf16[256,256]{1,0:T(8,128)(2,1)} %constant.56.clone.refs_4_, ...), custom_call_target="tpu_custom_call" | custom-call | tf_op jit(solution)/shard_map/pallas_call | solution.py:362
  3.7 23.0 %all-to-all-start = ((bf16[128,4,1152]{2,1,0:T(4,128)(2,1)}), bf16[128,4,1152]{2,1,0:T(4,128)(2,1)S(1)}, u32[]{:S(2)}, u32[]{:S(2)}) async-start(bf16[128,4,1152]{2,1,0:T(4,128)(2,1)} %shard_map.136), calls=%async_computation | async-start | bytes 2359296 | tf_op jit(solution)/shard_map/all_to_all | solution.py:345
  26.7 0.1 pad_maximum_fusion.2.edge_ref
  26.8 55.7 %all-to-all-done.block_ref = bf16[128,4,1152]{2,1,0:T(4,128)(2,1)S(1)} async-done(((bf16[128,4,1152]{2,1,0:T(4,128)(2,1)}), bf16[128,4,1152]{2,1,0:T(4,128)(2,1)S(1)}, u32[]{:S(2)}, u32[]{:S(2)}) %all-to-all-start) | async-done | bytes 1179680 | tf_op jit(solution)/shard_map/all_to_all | solution.py:345
  82.5 0.1 fusion
  82.6 0.1 pad_maximum_fusion
  82.7 0.7 broadcast_in_dim.10
  83.5 0.0 copy-start
  83.5 0.0 copy-start.1
  83.5 4.3 %all-to-all-start.1 = ((bf16[4,2,128,128]{3,2,1,0:T(8,128)(2,1)}), bf16[4,2,128,128]{3,2,1,0:T(8,128)(2,1)S(1)}, u32[]{:S(2)}, u32[]{:S(2)}) async-start(bf16[4,2,128,128]{3,2,1,0:T(8,128)(2,1)} %broadcast_in_dim.10), calls=%async_computation.1 | async-start | bytes 524288 | tf_op jit(solution)/shard_map/all_to_all | solution.py:380
  87.8 10.1 %all-gather = bf16[2,512,128]{2,1,0:T(8,128)(2,1)S(1)} all-gather(bf16[2,128,128]{2,1,0:T(8,128)(2,1)S(1)} %get-tuple-element.14), channel_id=2, replica_groups=mesh['zq'=4,'zp'=2,'core'=2,'x'=4,'zhi'=2,'y'=4] {'zp','core'}, dimensions={1}, use_global_device_ids=true | all-gather | bytes 327680 | tf_op jit(solution)/shard_map/all_gather | solution.py:381
  97.9 1.8 %convolution_bitcast_fusion.start_ref = f32[128,768]{1,0:T(8,128)S(1)} fusion(bf16[2,4,128,128]{3,2,1,0:T(8,128)(2,1)S(1)} %bitcast.23, bf16[4,2,128,768]{3,2,0,1:T(8,128)(2,1)} %constant.58.clone), kind=kOutput, calls=%fused_computation | convolution fusion | flops 201326592 | bytes 2228224 | tf_op jit(solution)/shard_map/hrzl,rhlk->zk/dot_general | solution.py:392
  99.7 0.0 all-to-all-done.1.mask_ref
  99.7 0.0 copy-done
  99.8 0.0 copy-done.1
  99.8 2.3 %shard_map.137 = (f32[256,1024]{1,0:T(8,128)S(1)}, bf16[2,128,128]{2,1,0:T(8,128)(2,1)S(1)}, f32[2,128,128]{2,1,0:T(8,128)S(1)}, f32[2,2,128,128]{3,2,1,0:T(8,128)S(1)}) custom-call(f32[2]{0:T(128)S(1)} %pad_maximum_fusion.2.edge_ref, f32[128,768]{1,0:T(8,128)S(1)} %convolution_bitcast_fusion.start_ref, bf16[128,4,1152]{2,1,0:T(4,128)(2,1)S(1)} %all-to-all-done.block_ref, ...), custom_call_target="tpu_custom_call" | custom-call | tf_op jit(solution)/shard_map/pallas_call | solution.py:320
  102.1 5.9 %all-gather.1 = bf16[8,128,128]{2,1,0:T(8,128)(2,1)S(1)} all-gather(bf16[2,128,128]{2,1,0:T(8,128)(2,1)S(1)} %get-tuple-element.17), channel_id=3, replica_groups=mesh['zq'=4,'zp'=2,'core'=2,'x'=4,'zhi'=2,'y'=4] {'zp','core'}, dimensions={0}, use_global_device_ids=true | all-gather | bytes 327680 | tf_op jit(solution)/shard_map/all_gather | solution.py:406
  107.9 0.0 copy-start.2
  107.9 0.0 copy-start.3
  108.0 1.7 %shard_map.138 = (bf16[2,128,128]{2,1,0:T(8,128)(2,1)S(1)}, f32[2,128,128]{2,1,0:T(8,128)S(1)}, f32[2,128,128]{2,1,0:T(8,128)S(1)}) custom-call(bf16[4,2,128,128]{3,2,1,0:T(8,128)(2,1)S(1)} %bitcast.18, f32[2,128,128]{2,1,0:T(8,128)S(1)} %get-tuple-element.18.spread_ref, f32[2,2,128,128]{3,2,1,0:T(8,128)S(1)} %get-tuple-element.16.image_ref, ...), custom_call_target="tpu_custom_call" | custom-call | tf_op jit(solution)/shard_map/pallas_call | solution.py:320
  109.6 3.7 %collective-permute-start = (f32[2,128,128]{2,1,0:T(8,128)S(1)}, f32[2,128,128]{2,1,0:T(8,128)S(1)}, u32[]{:S(2)}, u32[]{:S(2)}) collective-permute-start(f32[2,128,128]{2,1,0:T(8,128)S(1)} %get-tuple-element.21.guess_ref), channel_id=1, source_target_pairs={{0,1},{1,2},{2,3},{3,11},{11,10},{10,9},{9,8},{8,16},{16,17},{17,1... | collective-permute-start | bytes 393224 | tf_op jit(solution)/shard_map/ppermute | solution.py:412
  113.3 6.1 %all-gather.2 = bf16[8,128,128]{2,1,0:T(8,128)(2,1)S(1)} all-gather(bf16[2,128,128]{2,1,0:T(8,128)(2,1)S(1)} %get-tuple-element.22), channel_id=4, replica_groups=mesh['zq'=4,'zp'=2,'core'=2,'x'=4,'zhi'=2,'y'=4] {'zp','core'}, dimensions={0}, use_global_device_ids=true | all-gather | bytes 327680 | tf_op jit(solution)/shard_map/all_gather | solution.py:413
  119.4 0.0 collective-permute-done.before_ref
  119.4 1.5 %shard_map.139 = f32[128,128]{1,0:T(8,128)S(1)} custom-call(f32[2]{0:T(128)S(1)} %pad_maximum_fusion.2.edge_ref, s32[1]{0:T(128)} %bitcast.2.place_ref, f32[2,2,128,128]{3,2,1,0:T(8,128)S(1)} %get-tuple-element.16.image_ref, f32[2,128,128]{2,1,0:T(8,128)S(1)} %get-tuple-element.20.change_ref, f32[2,128,128]{2,1,0:T(8,128)S(1)} %get-tuple-element.21.guess_ref, ...), custom_call_target="tpu_custom_call" | custom-call | tf_op jit(solution)/shard_map/pallas_call | solution.py:320
  120.9 26.0 %all_to_all.21 = f32[128,1,128]{2,1,0:T(1,128)S(1)} all-to-all(f32[128,1,128]{2,1,0:T(1,128)S(1)} %bitcast.20), channel_id=1, replica_groups=mesh['zq'=4,'zp'=2,'core'=2,'x'=4,'zhi'=2,'y'=4] {'zq','x','zhi','y'}, dimensions={0} | all-to-all | bytes 131072 | tf_op jit(solution)/shard_map/all_to_all | solution.py:345
  146.9 0.0 copy-done.2
  147.0 0.0 copy-done.3
  147.0 0.9 shard_map.140
  (1 shorter events, 0.0 us)
Async XLA Ops:
  3.7 78.7 %all-to-all-start = ((bf16[128,4,1152]{2,1,0:T(4,128)(2,1)}), bf16[128,4,1152]{2,1,0:T(4,128)(2,1)S(1)}, u32[]{:S(2)}, u32[]{:S(2)}) async-start(bf16[128,4,1152]{2,1,0:T(4,128)(2,1)} %shard_map.136), calls=%async_computation | async-start | bytes 2359296 | tf_op jit(solution)/shard_map/all_to_all | solution.py:345
  83.5 16.3 %copy-start = (bf16[256,256]{1,0:T(8,128)(2,1)S(1)}, bf16[256,256]{1,0:T(8,128)(2,1)}, u32[]{:S(2)}) copy-start(bf16[256,256]{1,0:T(8,128)(2,1)} %constant.60.clone.gy_ref.gz_ref) | copy-start | bytes 393220
  83.5 16.3 %copy-start.1 = (bf16[256,256]{1,0:T(8,128)(2,1)S(1)}, bf16[256,256]{1,0:T(8,128)(2,1)}, u32[]{:S(2)}) copy-start(bf16[256,256]{1,0:T(8,128)(2,1)} %constant.59.clone.fz_ref.fy_ref) | copy-start | bytes 393220
  83.5 16.3 %all-to-all-start.1 = ((bf16[4,2,128,128]{3,2,1,0:T(8,128)(2,1)}), bf16[4,2,128,128]{3,2,1,0:T(8,128)(2,1)S(1)}, u32[]{:S(2)}, u32[]{:S(2)}) async-start(bf16[4,2,128,128]{3,2,1,0:T(8,128)(2,1)} %broadcast_in_dim.10), calls=%async_computation.1 | async-start | bytes 524288 | tf_op jit(solution)/shard_map/all_to_all | solution.py:380
  107.9 39.0 %copy-start.2 = (f32[2,4,8,128]{3,2,1,0:T(8,128)S(1)}, f32[2,4,8,128]{3,2,1,0:T(8,128)}, u32[]{:S(2)}) copy-start(f32[2,4,8,128]{3,2,1,0:T(8,128)} %image_ref.1) | copy-start | bytes 98308
  107.9 39.0 %copy-start.3 = (bf16[128,256]{1,0:T(8,128)(2,1)S(1)}, bf16[128,256]{1,0:T(8,128)(2,1)}, u32[]{:S(2)}) copy-start(bf16[128,256]{1,0:T(8,128)(2,1)} %constant.61.clone.target_ref) | copy-start | bytes 196612
  109.6 9.7 %collective-permute-start = (f32[2,128,128]{2,1,0:T(8,128)S(1)}, f32[2,128,128]{2,1,0:T(8,128)S(1)}, u32[]{:S(2)}, u32[]{:S(2)}) collective-permute-start(f32[2,128,128]{2,1,0:T(8,128)S(1)} %get-tuple-element.21.guess_ref), channel_id=1, source_target_pairs={{0,1},{1,2},{2,3},{3,11},{11,10},{10,9},{9,8},{8,16},{16,17},{17,1... | collective-permute-start | bytes 393224 | tf_op jit(solution)/shard_map/ppermute | solution.py:412

commit v12 on v10

--- a/solution.py
+++ b/solution.py
@@ -205,6 +205,17 @@
         back_y = jnp.where(position(d_y.shape, 1) > 0, shifted(d_y, 1, -1), 0.0)
         sums.append((back_z - d_z) + (back_y - d_y) - d_x)
     return sums
+
+
+def share_kernel(extra_ref, mask_ref, start_ref):
+    pairs, n, _ = start_ref.shape
+    left = position((n, n), 1) < n // 2
+    for h in range(pairs):
+        low, high = (extra_ref[h + k * pairs].astype(f32) for k in range(2))
+        start_ref[h] = jnp.where(left, low, pltpu.roll(high, n // 2, 1)).astype(bf16)
+        mask = jnp.where(left, pltpu.roll(low, n // 2, 1), high).astype(bf16)
+        for q in range(mask_ref.shape[0]):
+            mask_ref[q, h] = mask
 
 
 def first_kernel(
@@ -333,7 +344,6 @@
     for t in range(lines):
         choose[t, np.arange(count), quarter // 2, t] = 1.0
     lanes = coils * 2 * ny
-    half = nz // 2
     packed = jax.ShapeDtypeStruct((nx, planes, 2 * lanes + nz), bf16)
     (blocks,) = call(
         pack_kernel, (packed,), coil_maps, kspace_data, sample_mask.transpose(0, 2, 1), initial_image,
@@ -343,13 +353,13 @@
     blocks = spread(blocks)
     extra = blocks[:, :, 2 * lanes :].reshape(zq, nz, nz)
 
-    def pairs(part):
-        return jnp.concatenate([part[: zq // 2], part[zq // 2 :]], 2)
-
-    mask = pairs(extra[:, :, half:])
-    mask = jnp.broadcast_to(mask[None], (quarters, *mask.shape))
+    mask, start = call(
+        share_kernel,
+        (jax.ShapeDtypeStruct((quarters, zq // 2, nz, nz), bf16), jax.ShapeDtypeStruct((zq // 2, nz, nz), bf16)),
+        extra,
+    )
     mask = lax.all_to_all(mask, COLUMN[3], 0, 0, tiled=True)
-    start = lax.all_gather(pairs(extra[:, :, :half]), GROUP, axis=1)
+    start = lax.all_gather(start, GROUP, axis=1)
 
     place = np.zeros((group, zq // 2, 2, 4, 2, rows, 3, 2, zq, group, rows), np.float32)
     for r in range(group):

time: 148 us -> 148 us (level)
    pallas_call x5 -> x6, Pallas kernels: 10.3 us -> 11.1 us  [call(): pl.pallas_call(kernel, in_specs=[place(a) for a in operands], out_specs=[...]
where the time goes in v12:
time: 148 us
  waiting for transfers between devices  55.8 us (38%)
  blocking collectives  48.8 us (33%)
  starting transfers between devices  30.8 us (21%)
  Pallas kernels  11.1 us (8%)
    all_to_all x1, waiting for transfers between devices, spread(): return lax.all_to_all(blocks, COLUMN, 0, 0, tiled=True)  55.8 us
    all_to_all x1, blocking collectives, spread(): return lax.all_to_all(blocks, COLUMN, 0, 0, tiled=True)  26 us
    all_to_all x1, starting transfers between devices, spread(): return lax.all_to_all(blocks, COLUMN, 0, 0, tiled=True)  23.1 us
    all_gather x2, blocking collectives, on_device(): parts = lax.all_gather(grad, GROUP, axis=0)  12.2 us
    pallas_call x6, Pallas kernels, call(): pl.pallas_call(kernel, in_specs=[place(a) for a in operands], out_specs=[...  11.1 us
    all_gather x1, blocking collectives, on_device(): start = lax.all_gather(start, GROUP, axis=1)  10.6 us
    all_to_all x1, starting transfers between devices, on_device(): mask = lax.all_to_all(mask, COLUMN[3], 0, 0, tiled=True)  4.19 us
    ppermute x1, starting transfers between devices, on_device(): before = lax.ppermute(guess, COLUMN, forth)  3.52 us
  transfers between devices with their start and end apart: 3, of which 1 were waited for; matrix products, arithmetic and copies ran while one was open for 0% of the time, Pallas kernels for 0%

profile of v12, /device:TPU:1, one launch (start us, length us, event | category | flops | bytes accessed | tf_op | source)
XLA Modules:
  0.0 147.6 jit_solution(5355020125784425331)
XLA Ops:
  0.0 3.7 %shard_map.136 = bf16[128,4,1152]{2,1,0:T(4,128)(2,1)} custom-call(bf16[2,2,4,128,128]{4,3,2,1,0:T(8,128)(2,1)} %maps_ref.1, bf16[2,2,128,4,128]{4,3,2,1,0:T(4,128)(2,1)} %data_ref.1, s32[2,4,128]{2,1,0:T(4,128)} %bitcast.18, f32[2,4,8,128]{3,2,1,0:T(8,128)} %image_ref.3, bf16[128,512]{1,0:T(8,128)(2,1)} %constant.54.clone.near_ref, ...), custom_call_target="tpu_custom_call" | custom-call | tf_op jit(solution)/shard_map/pallas_call | solution.py:311
  3.7 0.0 copy-start.2
  3.7 23.1 %all-to-all-start = ((bf16[128,4,1152]{2,1,0:T(4,128)(2,1)}), bf16[128,4,1152]{2,1,0:T(4,128)(2,1)S(1)}, u32[]{:S(2)}, u32[]{:S(2)}) async-start(bf16[128,4,1152]{2,1,0:T(4,128)(2,1)} %shard_map.136), calls=%async_computation | async-start | bytes 2359296 | tf_op jit(solution)/shard_map/all_to_all | solution.py:336
  26.8 0.0 copy-start
  26.9 0.0 copy-start.1
  26.9 55.8 %all-to-all-done.block_ref = bf16[128,4,1152]{2,1,0:T(4,128)(2,1)S(1)} async-done(((bf16[128,4,1152]{2,1,0:T(4,128)(2,1)}), bf16[128,4,1152]{2,1,0:T(4,128)(2,1)S(1)}, u32[]{:S(2)}, u32[]{:S(2)}) %all-to-all-start) | async-done | bytes 1179680 | tf_op jit(solution)/shard_map/all_to_all | solution.py:336
  82.7 0.8 shard_map.137
  83.5 4.2 %all-to-all-start.1 = ((bf16[4,2,128,128]{3,2,1,0:T(8,128)(2,1)}), bf16[4,2,128,128]{3,2,1,0:T(8,128)(2,1)S(1)}, u32[]{:S(2)}, u32[]{:S(2)}) async-start(bf16[4,2,128,128]{3,2,1,0:T(8,128)(2,1)} %get-tuple-element.15), calls=%async_computation.1 | async-start | bytes 524288 | tf_op jit(solution)/shard_map/all_to_all | solution.py:361
  87.7 0.1 pad_maximum_fusion.edge_ref
  87.8 10.6 %all-gather = bf16[2,512,128]{2,1,0:T(8,128)(2,1)} all-gather(bf16[2,128,128]{2,1,0:T(8,128)(2,1)S(1)} %get-tuple-element.14), channel_id=2, replica_groups=mesh['zq'=4,'zp'=2,'core'=2,'x'=4,'zhi'=2,'y'=4] {'zp','core'}, dimensions={1}, use_global_device_ids=true | all-gather | bytes 327680 | tf_op jit(solution)/shard_map/all_gather | solution.py:362
  98.3 0.0 all-to-all-done.1.mask_ref
  98.3 0.0 copy-done.2
  98.3 0.0 copy-done
  98.3 0.0 copy-done.1
  98.4 0.0 copy-start.3
  98.4 0.9 copy-done.3
  99.3 2.5 %shard_map.138 = (f32[256,1024]{1,0:T(8,128)S(1)}, bf16[2,128,128]{2,1,0:T(8,128)(2,1)S(1)}, f32[2,128,128]{2,1,0:T(8,128)S(1)}, f32[2,2,128,128]{3,2,1,0:T(8,128)S(1)}) custom-call(f32[2]{0:T(128)S(1)} %pad_maximum_fusion.edge_ref, bf16[2,4,128,128]{3,2,1,0:T(8,128)(2,1)S(1)} %bitcast.13, bf16[1024,768]{1,0:T(8,128)(2,1)S(1)} %copy-done.2, ...), custom_call_target="tpu_custom_call" | custom-call | tf_op jit(solution)/shard_map/pallas_call | solution.py:311
  101.8 6.1 %all-gather.1 = bf16[8,128,128]{2,1,0:T(8,128)(2,1)S(1)} all-gather(bf16[2,128,128]{2,1,0:T(8,128)(2,1)S(1)} %get-tuple-element.17), channel_id=3, replica_groups=mesh['zq'=4,'zp'=2,'core'=2,'x'=4,'zhi'=2,'y'=4] {'zp','core'}, dimensions={0}, use_global_device_ids=true | all-gather | bytes 327680 | tf_op jit(solution)/shard_map/all_gather | solution.py:385
  108.0 1.7 %shard_map.139 = (bf16[2,128,128]{2,1,0:T(8,128)(2,1)S(1)}, f32[2,128,128]{2,1,0:T(8,128)S(1)}, f32[2,128,128]{2,1,0:T(8,128)S(1)}) custom-call(bf16[4,2,128,128]{3,2,1,0:T(8,128)(2,1)S(1)} %bitcast.12, f32[2,128,128]{2,1,0:T(8,128)S(1)} %get-tuple-element.18.spread_ref, f32[2,2,128,128]{3,2,1,0:T(8,128)S(1)} %get-tuple-element.16.image_ref, ...), custom_call_target="tpu_custom_call" | custom-call | tf_op jit(solution)/shard_map/pallas_call | solution.py:311
  109.6 0.0 copy-start.4
  109.6 0.0 copy-start.5
  109.7 3.5 %collective-permute-start = (f32[2,128,128]{2,1,0:T(8,128)S(1)}, f32[2,128,128]{2,1,0:T(8,128)S(1)}, u32[]{:S(2)}, u32[]{:S(2)}) collective-permute-start(f32[2,128,128]{2,1,0:T(8,128)S(1)} %get-tuple-element.21.guess_ref), channel_id=1, source_target_pairs={{0,1},{1,2},{2,3},{3,11},{11,10},{10,9},{9,8},{8,16},{16,17},{17,1... | collective-permute-start | bytes 393224 | tf_op jit(solution)/shard_map/ppermute | solution.py:391
  113.2 6.1 %all-gather.2 = bf16[8,128,128]{2,1,0:T(8,128)(2,1)S(1)} all-gather(bf16[2,128,128]{2,1,0:T(8,128)(2,1)S(1)} %get-tuple-element.22), channel_id=4, replica_groups=mesh['zq'=4,'zp'=2,'core'=2,'x'=4,'zhi'=2,'y'=4] {'zp','core'}, dimensions={0}, use_global_device_ids=true | all-gather | bytes 327680 | tf_op jit(solution)/shard_map/all_gather | solution.py:392
  119.2 0.0 collective-permute-done.before_ref
  119.3 1.5 %shard_map.140 = f32[128,128]{1,0:T(8,128)S(1)} custom-call(f32[2]{0:T(128)S(1)} %pad_maximum_fusion.edge_ref, s32[1]{0:T(128)} %bitcast.2.place_ref, f32[2,2,128,128]{3,2,1,0:T(8,128)S(1)} %get-tuple-element.16.image_ref, f32[2,128,128]{2,1,0:T(8,128)S(1)} %get-tuple-element.20.change_ref, f32[2,128,128]{2,1,0:T(8,128)S(1)} %get-tuple-element.21.guess_ref, ...), custom_call_target="tpu_custom_call" | custom-call | tf_op jit(solution)/shard_map/pallas_call | solution.py:311
  120.8 26.0 %all_to_all.21 = f32[128,1,128]{2,1,0:T(1,128)S(1)} all-to-all(f32[128,1,128]{2,1,0:T(1,128)S(1)} %bitcast.16), channel_id=1, replica_groups=mesh['zq'=4,'zp'=2,'core'=2,'x'=4,'zhi'=2,'y'=4] {'zq','x','zhi','y'}, dimensions={0} | all-to-all | bytes 131072 | tf_op jit(solution)/shard_map/all_to_all | solution.py:336
  146.7 0.0 copy-done.4
  146.7 0.0 copy-done.5
  146.8 0.9 shard_map.141
  (1 shorter events, 0.0 us)
Async XLA Ops:
  3.7 94.6 %copy-start.2 = (bf16[1024,768]{1,0:T(8,128)(2,1)S(1)}, bf16[1024,768]{1,0:T(8,128)(2,1)}, u32[]{:S(2)}) copy-start(bf16[1024,768]{1,0:T(8,128)(2,1)} %constant.58.clone.place_ref) | copy-start | bytes 4718596
  3.7 78.9 %all-to-all-start = ((bf16[128,4,1152]{2,1,0:T(4,128)(2,1)}), bf16[128,4,1152]{2,1,0:T(4,128)(2,1)S(1)}, u32[]{:S(2)}, u32[]{:S(2)}) async-start(bf16[128,4,1152]{2,1,0:T(4,128)(2,1)} %shard_map.136), calls=%async_computation | async-start | bytes 2359296 | tf_op jit(solution)/shard_map/all_to_all | solution.py:336
  26.8 71.5 %copy-start = (bf16[256,256]{1,0:T(8,128)(2,1)S(1)}, bf16[256,256]{1,0:T(8,128)(2,1)}, u32[]{:S(2)}) copy-start(bf16[256,256]{1,0:T(8,128)(2,1)} %constant.60.clone.gy_ref.gz_ref) | copy-start | bytes 393220
  26.9 71.5 %copy-start.1 = (bf16[256,256]{1,0:T(8,128)(2,1)S(1)}, bf16[256,256]{1,0:T(8,128)(2,1)}, u32[]{:S(2)}) copy-start(bf16[256,256]{1,0:T(8,128)(2,1)} %constant.59.clone.fz_ref.fy_ref) | copy-start | bytes 393220
  83.5 14.8 %all-to-all-start.1 = ((bf16[4,2,128,128]{3,2,1,0:T(8,128)(2,1)}), bf16[4,2,128,128]{3,2,1,0:T(8,128)(2,1)S(1)}, u32[]{:S(2)}, u32[]{:S(2)}) async-start(bf16[4,2,128,128]{3,2,1,0:T(8,128)(2,1)} %get-tuple-element.15), calls=%async_computation.1 | async-start | bytes 524288 | tf_op jit(solution)/shard_map/all_to_all | solution.py:361
  98.4 1.0 copy-start.3
  109.6 37.1 %copy-start.4 = (f32[2,4,8,128]{3,2,1,0:T(8,128)S(1)}, f32[2,4,8,128]{3,2,1,0:T(8,128)}, u32[]{:S(2)}) copy-start(f32[2,4,8,128]{3,2,1,0:T(8,128)} %image_ref.3) | copy-start | bytes 98308
  109.6 37.1 %copy-start.5 = (bf16[128,256]{1,0:T(8,128)(2,1)S(1)}, bf16[128,256]{1,0:T(8,128)(2,1)}, u32[]{:S(2)}) copy-start(bf16[128,256]{1,0:T(8,128)(2,1)} %constant.61.clone.target_ref) | copy-start | bytes 196612
  109.7 9.6 %collective-permute-start = (f32[2,128,128]{2,1,0:T(8,128)S(1)}, f32[2,128,128]{2,1,0:T(8,128)S(1)}, u32[]{:S(2)}, u32[]{:S(2)}) collective-permute-start(f32[2,128,128]{2,1,0:T(8,128)S(1)} %get-tuple-element.21.guess_ref), channel_id=1, source_target_pairs={{0,1},{1,2},{2,3},{3,11},{11,10},{10,9},{9,8},{8,16},{16,17},{17,1... | collective-permute-start | bytes 393224 | tf_op jit(solution)/shard_map/ppermute | solution.py:391

commit v13 on v12

--- a/solution.py
+++ b/solution.py
@@ -207,11 +207,11 @@
     return sums
 
 
-def share_kernel(extra_ref, mask_ref, start_ref):
+def share_kernel(block_ref, mask_ref, start_ref):
     pairs, n, _ = start_ref.shape
     left = position((n, n), 1) < n // 2
     for h in range(pairs):
-        low, high = (extra_ref[h + k * pairs].astype(f32) for k in range(2))
+        low, high = (lane_block(block_ref, h + k * pairs, block_ref.shape[2] // n - 1) for k in range(2))
         start_ref[h] = jnp.where(left, low, pltpu.roll(high, n // 2, 1)).astype(bf16)
         mask = jnp.where(left, pltpu.roll(low, n // 2, 1), high).astype(bf16)
         for q in range(mask_ref.shape[0]):
@@ -351,12 +351,11 @@
         choose.reshape(lines * count, -1).astype(bf16), vmem=60,
     )
     blocks = spread(blocks)
-    extra = blocks[:, :, 2 * lanes :].reshape(zq, nz, nz)
 
     mask, start = call(
         share_kernel,
         (jax.ShapeDtypeStruct((quarters, zq // 2, nz, nz), bf16), jax.ShapeDtypeStruct((zq // 2, nz, nz), bf16)),
-        extra,
+        blocks,
     )
     mask = lax.all_to_all(mask, COLUMN[3], 0, 0, tiled=True)
     start = lax.all_gather(start, GROUP, axis=1)

time: 148 us -> 148 us (level)
  no operation moved by 1% of the time
where the time goes in v13:
time: 148 us; the launch traced here: 147 us
  waiting for transfers between devices  55.8 us (38%)
  blocking collectives  48.8 us (33%)
  starting transfers between devices  30.7 us (21%)
  Pallas kernels  11.1 us (8%)
    all_to_all x1, waiting for transfers between devices, spread(): return lax.all_to_all(blocks, COLUMN, 0, 0, tiled=True)  55.8 us
    all_to_all x1, blocking collectives, spread(): return lax.all_to_all(blocks, COLUMN, 0, 0, tiled=True)  26 us
    all_to_all x1, starting transfers between devices, spread(): return lax.all_to_all(blocks, COLUMN, 0, 0, tiled=True)  23 us
    all_gather x2, blocking collectives, on_device(): parts = lax.all_gather(grad, GROUP, axis=0)  12.2 us
    pallas_call x6, Pallas kernels, call(): pl.pallas_call(kernel, in_specs=[place(a) for a in operands], out_specs=[...  11.1 us
    all_gather x1, blocking collectives, on_device(): start = lax.all_gather(start, GROUP, axis=1)  10.6 us
    all_to_all x1, starting transfers between devices, on_device(): mask = lax.all_to_all(mask, COLUMN[3], 0, 0, tiled=True)  4.19 us
    ppermute x1, starting transfers between devices, on_device(): before = lax.ppermute(guess, COLUMN, forth)  3.52 us
  transfers between devices with their start and end apart: 3, of which 1 were waited for; matrix products, arithmetic and copies ran while one was open for 0% of the time, Pallas kernels for 0%

profile of v13, /device:TPU:1, one launch (start us, length us, event | category | flops | bytes accessed | tf_op | source)
XLA Modules:
  0.0 147.4 jit_solution(13585758862427952571)
XLA Ops:
  0.0 3.7 %shard_map.136 = bf16[128,4,1152]{2,1,0:T(4,128)(2,1)} custom-call(bf16[2,2,4,128,128]{4,3,2,1,0:T(8,128)(2,1)} %maps_ref.1, bf16[2,2,128,4,128]{4,3,2,1,0:T(4,128)(2,1)} %data_ref.1, s32[2,4,128]{2,1,0:T(4,128)} %bitcast.16, f32[2,4,8,128]{3,2,1,0:T(8,128)} %image_ref.3, bf16[128,512]{1,0:T(8,128)(2,1)} %constant.54.clone.near_ref, ...), custom_call_target="tpu_custom_call" | custom-call | tf_op jit(solution)/shard_map/pallas_call | solution.py:311
  3.7 23.0 %all-to-all-start = ((bf16[128,4,1152]{2,1,0:T(4,128)(2,1)}), bf16[128,4,1152]{2,1,0:T(4,128)(2,1)S(1)}, u32[]{:S(2)}, u32[]{:S(2)}) async-start(bf16[128,4,1152]{2,1,0:T(4,128)(2,1)} %shard_map.136), calls=%async_computation | async-start | bytes 2359296 | tf_op jit(solution)/shard_map/all_to_all | solution.py:336
  26.7 0.0 copy-start
  26.7 0.0 copy-start.1
  26.7 0.0 copy-start.2
  26.8 55.8 %all-to-all-done.block_ref = bf16[128,4,1152]{2,1,0:T(4,128)(2,1)S(1)} async-done(((bf16[128,4,1152]{2,1,0:T(4,128)(2,1)}), bf16[128,4,1152]{2,1,0:T(4,128)(2,1)S(1)}, u32[]{:S(2)}, u32[]{:S(2)}) %all-to-all-start) | async-done | bytes 1179680 | tf_op jit(solution)/shard_map/all_to_all | solution.py:336
  82.5 0.8 shard_map.137
  83.3 4.2 %all-to-all-start.1 = ((bf16[4,2,128,128]{3,2,1,0:T(8,128)(2,1)}), bf16[4,2,128,128]{3,2,1,0:T(8,128)(2,1)S(1)}, u32[]{:S(2)}, u32[]{:S(2)}) async-start(bf16[4,2,128,128]{3,2,1,0:T(8,128)(2,1)} %get-tuple-element.15), calls=%async_computation.1 | async-start | bytes 524288 | tf_op jit(solution)/shard_map/all_to_all | solution.py:360
  87.5 0.1 pad_maximum_fusion.edge_ref
  87.6 10.6 %all-gather = bf16[2,512,128]{2,1,0:T(8,128)(2,1)} all-gather(bf16[2,128,128]{2,1,0:T(8,128)(2,1)S(1)} %get-tuple-element.14), channel_id=2, replica_groups=mesh['zq'=4,'zp'=2,'core'=2,'x'=4,'zhi'=2,'y'=4] {'zp','core'}, dimensions={1}, use_global_device_ids=true | all-gather | bytes 327680 | tf_op jit(solution)/shard_map/all_gather | solution.py:361
  98.2 0.0 all-to-all-done.1.mask_ref
  98.2 0.0 copy-done
  98.2 0.0 copy-done.1
  98.2 0.0 copy-done.2
  98.2 0.0 copy-start.3
  98.2 0.9 copy-done.3
  99.1 2.5 %shard_map.138 = (f32[256,1024]{1,0:T(8,128)S(1)}, bf16[2,128,128]{2,1,0:T(8,128)(2,1)S(1)}, f32[2,128,128]{2,1,0:T(8,128)S(1)}, f32[2,2,128,128]{3,2,1,0:T(8,128)S(1)}) custom-call(f32[2]{0:T(128)S(1)} %pad_maximum_fusion.edge_ref, bf16[2,4,128,128]{3,2,1,0:T(8,128)(2,1)S(1)} %bitcast.12, bf16[1024,768]{1,0:T(8,128)(2,1)S(1)} %copy-done.2, ...), custom_call_target="tpu_custom_call" | custom-call | tf_op jit(solution)/shard_map/pallas_call | solution.py:311
  101.6 6.1 %all-gather.1 = bf16[8,128,128]{2,1,0:T(8,128)(2,1)S(1)} all-gather(bf16[2,128,128]{2,1,0:T(8,128)(2,1)S(1)} %get-tuple-element.17), channel_id=3, replica_groups=mesh['zq'=4,'zp'=2,'core'=2,'x'=4,'zhi'=2,'y'=4] {'zp','core'}, dimensions={0}, use_global_device_ids=true | all-gather | bytes 327680 | tf_op jit(solution)/shard_map/all_gather | solution.py:384
  107.8 1.7 %shard_map.139 = (bf16[2,128,128]{2,1,0:T(8,128)(2,1)S(1)}, f32[2,128,128]{2,1,0:T(8,128)S(1)}, f32[2,128,128]{2,1,0:T(8,128)S(1)}) custom-call(bf16[4,2,128,128]{3,2,1,0:T(8,128)(2,1)S(1)} %bitcast.11, f32[2,128,128]{2,1,0:T(8,128)S(1)} %get-tuple-element.18.spread_ref, f32[2,2,128,128]{3,2,1,0:T(8,128)S(1)} %get-tuple-element.16.image_ref, ...), custom_call_target="tpu_custom_call" | custom-call | tf_op jit(solution)/shard_map/pallas_call | solution.py:311
  109.4 0.0 copy-start.4
  109.5 0.0 copy-start.5
  109.5 3.5 %collective-permute-start = (f32[2,128,128]{2,1,0:T(8,128)S(1)}, f32[2,128,128]{2,1,0:T(8,128)S(1)}, u32[]{:S(2)}, u32[]{:S(2)}) collective-permute-start(f32[2,128,128]{2,1,0:T(8,128)S(1)} %get-tuple-element.21.guess_ref), channel_id=1, source_target_pairs={{0,1},{1,2},{2,3},{3,11},{11,10},{10,9},{9,8},{8,16},{16,17},{17,1... | collective-permute-start | bytes 393224 | tf_op jit(solution)/shard_map/ppermute | solution.py:390
  113.0 6.1 %all-gather.2 = bf16[8,128,128]{2,1,0:T(8,128)(2,1)S(1)} all-gather(bf16[2,128,128]{2,1,0:T(8,128)(2,1)S(1)} %get-tuple-element.22), channel_id=4, replica_groups=mesh['zq'=4,'zp'=2,'core'=2,'x'=4,'zhi'=2,'y'=4] {'zp','core'}, dimensions={0}, use_global_device_ids=true | all-gather | bytes 327680 | tf_op jit(solution)/shard_map/all_gather | solution.py:391
  119.1 0.0 collective-permute-done.before_ref
  119.1 1.5 %shard_map.140 = f32[128,128]{1,0:T(8,128)S(1)} custom-call(f32[2]{0:T(128)S(1)} %pad_maximum_fusion.edge_ref, s32[1]{0:T(128)} %bitcast.2.place_ref, f32[2,2,128,128]{3,2,1,0:T(8,128)S(1)} %get-tuple-element.16.image_ref, f32[2,128,128]{2,1,0:T(8,128)S(1)} %get-tuple-element.20.change_ref, f32[2,128,128]{2,1,0:T(8,128)S(1)} %get-tuple-element.21.guess_ref, ...), custom_call_target="tpu_custom_call" | custom-call | tf_op jit(solution)/shard_map/pallas_call | solution.py:311
  120.6 26.0 %all_to_all.21 = f32[128,1,128]{2,1,0:T(1,128)S(1)} all-to-all(f32[128,1,128]{2,1,0:T(1,128)S(1)} %bitcast.14), channel_id=1, replica_groups=mesh['zq'=4,'zp'=2,'core'=2,'x'=4,'zhi'=2,'y'=4] {'zq','x','zhi','y'}, dimensions={0} | all-to-all | bytes 131072 | tf_op jit(solution)/shard_map/all_to_all | solution.py:336
  146.6 0.0 copy-done.4
  146.6 0.0 copy-done.5
  146.6 0.8 shard_map.141
Async XLA Ops:
  3.7 78.8 %all-to-all-start = ((bf16[128,4,1152]{2,1,0:T(4,128)(2,1)}), bf16[128,4,1152]{2,1,0:T(4,128)(2,1)S(1)}, u32[]{:S(2)}, u32[]{:S(2)}) async-start(bf16[128,4,1152]{2,1,0:T(4,128)(2,1)} %shard_map.136), calls=%async_computation | async-start | bytes 2359296 | tf_op jit(solution)/shard_map/all_to_all | solution.py:336
  26.7 71.4 %copy-start = (bf16[256,256]{1,0:T(8,128)(2,1)S(1)}, bf16[256,256]{1,0:T(8,128)(2,1)}, u32[]{:S(2)}) copy-start(bf16[256,256]{1,0:T(8,128)(2,1)} %constant.60.clone.gy_ref.gz_ref) | copy-start | bytes 393220
  26.7 71.4 %copy-start.1 = (bf16[256,256]{1,0:T(8,128)(2,1)S(1)}, bf16[256,256]{1,0:T(8,128)(2,1)}, u32[]{:S(2)}) copy-start(bf16[256,256]{1,0:T(8,128)(2,1)} %constant.59.clone.fz_ref.fy_ref) | copy-start | bytes 393220
  26.7 71.4 %copy-start.2 = (bf16[1024,768]{1,0:T(8,128)(2,1)S(1)}, bf16[1024,768]{1,0:T(8,128)(2,1)}, u32[]{:S(2)}) copy-start(bf16[1024,768]{1,0:T(8,128)(2,1)} %constant.58.clone.place_ref) | copy-start | bytes 4718596
  83.3 14.8 %all-to-all-start.1 = ((bf16[4,2,128,128]{3,2,1,0:T(8,128)(2,1)}), bf16[4,2,128,128]{3,2,1,0:T(8,128)(2,1)S(1)}, u32[]{:S(2)}, u32[]{:S(2)}) async-start(bf16[4,2,128,128]{3,2,1,0:T(8,128)(2,1)} %get-tuple-element.15), calls=%async_computation.1 | async-start | bytes 524288 | tf_op jit(solution)/shard_map/all_to_all | solution.py:360
  98.2 1.0 copy-start.3
  109.4 37.1 %copy-start.4 = (f32[2,4,8,128]{3,2,1,0:T(8,128)S(1)}, f32[2,4,8,128]{3,2,1,0:T(8,128)}, u32[]{:S(2)}) copy-start(f32[2,4,8,128]{3,2,1,0:T(8,128)} %image_ref.3) | copy-start | bytes 98308
  109.5 37.1 %copy-start.5 = (bf16[128,256]{1,0:T(8,128)(2,1)S(1)}, bf16[128,256]{1,0:T(8,128)(2,1)}, u32[]{:S(2)}) copy-start(bf16[128,256]{1,0:T(8,128)(2,1)} %constant.61.clone.target_ref) | copy-start | bytes 196612
  109.5 9.6 %collective-permute-start = (f32[2,128,128]{2,1,0:T(8,128)S(1)}, f32[2,128,128]{2,1,0:T(8,128)S(1)}, u32[]{:S(2)}, u32[]{:S(2)}) collective-permute-start(f32[2,128,128]{2,1,0:T(8,128)S(1)} %get-tuple-element.21.guess_ref), channel_id=1, source_target_pairs={{0,1},{1,2},{2,3},{3,11},{11,10},{10,9},{9,8},{8,16},{16,17},{17,1... | collective-permute-start | bytes 393224 | tf_op jit(solution)/shard_map/ppermute | solution.py:390
